TPU v7x, 768 devices: a whole 4x8x12 slice. The times are simulated.
768 devices in a mesh: expert: 8 (over y_hi, x), edata: 96 (over y_lo, z, core).
Axes of the slice: x: 4, y: 8 (y_hi: 2, y_lo: 4; y = y_hi * 4 + y_lo), z: 12, core: 2. Of those that a mesh axis runs over, the one named last changes fastest.
Arguments:
- grad_out: bfloat16 [196608, 2560], P(('expert', 'edata')), may hold values from -6 to 6
- route_weight: float32 [196608], P(('expert', 'edata')), may hold values from 0.05 to 1
- counts: int32 [6144], P(('expert', 'edata')), may hold values from 1 to 32, as said below
- preact: bfloat16 [196608, 1536], P(('expert', 'edata')), may hold values from -24 to 24
- down_weight: bfloat16 [8, 768, 2560], P('expert'), may hold values from -0.21875 to 0.21875
Outputs:
- grad_preact: bfloat16 [196608, 1536], P(('expert', 'edata'))
- weight_grad: float32 [8, 768, 2560], P('expert', 'edata')
- route_grad: float32 [196608], P(('expert', 'edata'))
Inputs may be any that keep to these rules, and one draw needn't show every extreme that they name: `counts`: every count is at most 32; in every draw one expert device receives 32 live rows from every sending device.
All inputs are finite; a program needn't handle non-finite values.
Results may differ from a plain program's by a relative error of at most 0.0085.
Values may be sent and summed in bfloat16 or wider, within the bound.
No kernel may reach another device: no remote copies, remote signals or barrier semaphores. Data moves between devices by JAX's collectives and lax.ppermute only.
A program may use at most 32 MiB of HBM per device.

v0:
```python
import jax
import jax.numpy as jnp
from jax import lax
from jax.sharding import PartitionSpec as P


def body(grad_out, route_weight, counts, preact, down_weight):
    row_total, feature_count = grad_out.shape
    expert_count = lax.axis_size("expert")
    capacity = row_total // expert_count
    hidden_count = down_weight.shape[1]
    slot_index = lax.broadcasted_iota(jnp.int32, (expert_count, capacity), 1)
    live_rows = (slot_index < counts[:, None]).astype(jnp.float32)
    route_matrix = route_weight.reshape(expert_count, capacity)
    slot_weight = route_matrix * live_rows
    scaled_rows = (
        grad_out.reshape(expert_count, capacity, feature_count) * slot_weight[:, :, None]
    ).astype(jnp.bfloat16)
    arrived_rows = lax.all_to_all(
        scaled_rows, "expert", split_axis=0, concat_axis=0, tiled=True
    ).reshape(row_total, feature_count)
    gate_value = preact[:, :hidden_count].astype(jnp.float32)
    up_value = preact[:, hidden_count:].astype(jnp.float32)
    sigmoid_gate = jax.nn.sigmoid(gate_value)
    silu_gate = gate_value * sigmoid_gate
    hidden_act = (silu_gate * up_value).astype(jnp.bfloat16)
    weight_mat = down_weight[0]
    replica_count = lax.axis_size("edata")
    grad_hidden = lax.dot_general(
        arrived_rows, weight_mat, (((1,), (1,)), ((), ())), preferred_element_type=jnp.float32
    )
    grad_gate = grad_hidden * up_value * sigmoid_gate * (1.0 + gate_value * (1.0 - sigmoid_gate))
    grad_up = grad_hidden * silu_gate
    grad_rows = jnp.concatenate([grad_gate, grad_up], axis=1).astype(jnp.bfloat16)
    row_score = jnp.sum(grad_hidden * hidden_act.astype(jnp.float32), axis=1)
    returned_score = lax.all_to_all(
        row_score.reshape(expert_count, capacity), "expert", split_axis=0, concat_axis=0, tiled=True
    )
    route_grad = live_rows * returned_score / route_matrix
    grad_rows, route_grad = (grad_rows, route_grad.reshape(row_total))
    partial_sum = lax.dot_general(
        hidden_act, arrived_rows, (((0,), (0,)), ((), ())), preferred_element_type=jnp.float32
    )
    summed_grad = lax.psum_scatter(partial_sum, "edata", scatter_dimension=0, tiled=True)
    weight_grad = (summed_grad / replica_count)[None]
    return (grad_rows, weight_grad, route_grad)


def solution(mesh):
    in_specs = (
        P(("expert", "edata"), None),
        P(("expert", "edata")),
        P(("expert", "edata")),
        P(("expert", "edata"), None),
        P("expert", None, None),
    )
    out_specs = (P(("expert", "edata"), None), P("expert", "edata", None), P(("expert", "edata")))
    return jax.shard_map(body, mesh=mesh, in_specs=in_specs, out_specs=out_specs, check_vma=False)
```

profile of v0, /device:TPU:1, one launch (start us, length us, event | category | flops | bytes accessed | tf_op | source)
XLA Modules:
  0.0 494.5 jit_solution(11993748442334636520)
XLA Ops:
  7.2 0.0 reduce-scatter.2.cloned.1.call-start
  7.2 0.8 reshape.48
  8.0 0.7 broadcast_select_fusion
  8.7 1.6 fusion.2
  10.3 0.0 copy-start
  10.3 32.8 %all_to_all.17 = bf16[8,32,2560]{2,1,0:T(8,128)(2,1)S(1)} all-to-all(bf16[8,32,2560]{2,1,0:T(8,128)(2,1)S(1)} %fusion.2), channel_id=1, replica_groups=mesh['expert'=8,'edata'=96] {'expert'}, dimensions={0} | all-to-all | bytes 2621440 | tf_op jit(solution)/shard_map/all_to_all | solution.py:19
  43.2 0.0 copy-done
  43.2 4.4 fusion.11
  47.5 0.0 copy-start.2
  47.5 0.0 reduce-scatter.2.cloned.1.call-update
  47.5 0.6 copy-done.2
  48.2 0.1 iota_compare_fusion
  48.2 0.1 lt.18
  48.3 3.6 multiply_reduce_fusion
  52.0 0.0 copy-start.1
  52.0 0.7 all_to_all.12
  52.6 4.2 all-to-all-start.1
  56.9 0.9 pad_maximum_fusion
  57.8 7.9 %all-to-all-done.1 = f32[8,1,32]{2,1,0:T(1,128)S(1)} async-done(((f32[8,1,32]{2,1,0:T(1,128)}), f32[8,1,32]{2,1,0:T(1,128)S(1)}, u32[]{:S(2)}, u32[]{:S(2)}) %all-to-all-start.1) | async-done | bytes 1056 | tf_op jit(solution)/shard_map/all_to_all | solution.py:36
  65.7 0.5 broadcast.47
  66.2 0.7 reduce.3
  66.9 0.1 all_to_all.14
  67.0 0.0 copy-done.1
  67.0 0.6 select_divide_fusion
  67.5 418.6 %reduce-scatter.2.cloned.1.call-done = f32[8,2560]{1,0:T(8,128)} async-done(((f32[768,2560]{1,0:T(8,128)}), f32[8,2560]{1,0:T(8,128)}) %reduce-scatter.2.cloned.1.call-update) | async-done | bytes 81936 | tf_op jit(solution)/shard_map/reduce_scatter | solution.py:44
  486.1 1.5 multiply_bitcast_fusion
Async XLA Ops:
  7.2 478.9 %reduce-scatter.2.cloned.1.call-start = ((), (), s32[]{:S(2)}) async-start(), calls=%async_computation.3 | async-start | bytes 7946240 | tf_op jit(solution)/shard_map/reduce_scatter | solution.py:44
  10.3 32.9 %copy-start = (bf16[256,1536]{1,0:T(8,128)(2,1)S(1)}, bf16[256,1536]{1,0:T(8,128)(2,1)}, u32[]{:S(2)}) copy-start(bf16[256,1536]{1,0:T(8,128)(2,1)} %param.8) | copy-start | bytes 2359300
  47.5 0.7 copy-start.2
  52.0 15.0 %copy-start.1 = (f32[256]{0:T(256)S(1)}, f32[256]{0:T(256)}, u32[]{:S(2)}) copy-start(f32[256]{0:T(256)} %param.6) | copy-start | bytes 3076
  52.6 13.1 %all-to-all-start.1 = ((f32[8,1,32]{2,1,0:T(1,128)}), f32[8,1,32]{2,1,0:T(1,128)S(1)}, u32[]{:S(2)}, u32[]{:S(2)}) async-start(f32[8,1,32]{2,1,0:T(1,128)} %all_to_all.12), calls=%async_computation.2 | async-start | bytes 8192 | tf_op jit(solution)/shard_map/all_to_all | solution.py:36
Sparse Core Ops, SparseCore 0:
  47.7 438.3 reduce-scatter.1
where the time goes:
time: 500 us; the launch traced here: 494 us
  waiting for transfers between devices  426 us (85%)
  blocking collectives  32.8 us (7%)
  between operations  14.1 us (3%)
  matrix products  7.98 us (2%)
  other arithmetic  6.09 us (1%)
    reduce_scatter x1, waiting for transfers between devices, body(): lax.psum_scatter(partial_sum, 'edata', scatter_dimension=0, tiled=True)  419 us
    all_to_all x1, blocking collectives, body(): lax.all_to_all(scaled_rows, 'expert', split_axis=0, concat_axis=0, tiled=...  32.8 us
  transfers between devices with their start and end apart: 2, of which 2 were waited for; matrix products, arithmetic and copies ran while one was open for 1% of the time, Pallas kernels for 0%

commit v1 on v0

v1 whole, which is shorter than its diff:
```python
import jax
import jax.numpy as jnp
from jax import lax
from jax.sharding import Mesh, PartitionSpec as P

EXPERT = ("yh", "x")
EDATA = ("y1", "y0", "zz", "z0", "core")
DEVICE = EXPERT + EDATA


def swap(value, axis):
    return lax.ppermute(value, axis, [(0, 1), (1, 0)])


def pick(value, index, axis):
    return lax.dynamic_index_in_dim(value, index, axis, keepdims=False)


def body(grad_out, route_weight, counts, preact, down_weight):
    row_total, feature_count = grad_out.shape
    expert_count = lax.axis_size(EXPERT)
    capacity = row_total // expert_count
    hidden_count = down_weight.shape[1]
    half = feature_count // 2
    quarter = half // 2
    replica_count = lax.axis_size(EDATA)
    core = lax.axis_index("core")
    z0 = lax.axis_index("z0")
    y0 = lax.axis_index("y0")
    size_y1, size_zz = lax.axis_size("y1"), lax.axis_size("zz")
    unit = hidden_count // (replica_count // 2)

    slot_index = lax.broadcasted_iota(jnp.int32, (expert_count, capacity), 1)
    live_rows = (slot_index < counts[:, None]).astype(jnp.float32)
    route_matrix = route_weight.reshape(expert_count, capacity)
    slot_weight = route_matrix * live_rows

    gate_value = preact[:, :hidden_count].astype(jnp.float32)
    up_value = preact[:, hidden_count:].astype(jnp.float32)
    sigmoid_gate = jax.nn.sigmoid(gate_value)
    silu_gate = gate_value * sigmoid_gate
    hidden_act = (silu_gate * up_value).astype(jnp.bfloat16)
    hidden_blocks = hidden_act.reshape(expert_count, capacity, hidden_count)
    other_blocks = swap(hidden_blocks, "core")

    scaled_rows = (
        grad_out.reshape(expert_count, capacity, feature_count) * slot_weight[:, :, None]
    ).astype(jnp.bfloat16)
    outgoing = jnp.stack([scaled_rows[:, :, :half], scaled_rows[:, :, half:]], axis=1)
    arrived = lax.all_to_all(
        outgoing.reshape(expert_count * 2, capacity, half),
        EXPERT + ("core",), split_axis=0, concat_axis=0, tiled=True,
    ).reshape(expert_count, 2, capacity, half)

    first_core = core == 0
    hidden_all = jnp.stack(
        [
            jnp.where(first_core, hidden_blocks, other_blocks),
            jnp.where(first_core, other_blocks, hidden_blocks),
        ],
        axis=1,
    ).reshape(2 * row_total, hidden_count)
    partial_sum = lax.dot_general(
        hidden_all, arrived.reshape(2 * row_total, half), (((0,), (0,)), ((), ())),
        preferred_element_type=jnp.float32,
    )
    parts = partial_sum.reshape(size_y1, 2, size_zz, 2, unit, half)
    part_a, part_b = parts[..., :quarter], parts[..., quarter:]
    sent_a = pick(part_a, 1 - z0, 3).astype(jnp.bfloat16)
    sent_b = pick(part_b, 1 - y0, 1).astype(jnp.bfloat16)
    came_a = swap(sent_a, "z0")
    came_b = swap(sent_b, "y0")

    arrived, sent_a, sent_b = lax.optimization_barrier((arrived, sent_a, sent_b))
    weight_half = lax.dynamic_slice(
        down_weight[0], (0, core * half), (hidden_count, half)
    )
    grad_partial = lax.dot_general(
        arrived.reshape(2 * row_total, half), weight_half, (((1,), (1,)), ((), ())),
        preferred_element_type=jnp.float32,
    ).reshape(expert_count, 2, capacity, hidden_count)
    grad_other = swap(pick(grad_partial, 1 - core, 1), "core")
    grad_hidden = (pick(grad_partial, core, 1) + grad_other).reshape(row_total, hidden_count)
    grad_gate = grad_hidden * up_value * sigmoid_gate * (1.0 + gate_value * (1.0 - sigmoid_gate))
    grad_up = grad_hidden * silu_gate
    grad_rows = jnp.concatenate([grad_gate, grad_up], axis=1).astype(jnp.bfloat16)
    row_score = jnp.sum(grad_hidden * hidden_act.astype(jnp.float32), axis=1)
    returned_score = lax.all_to_all(
        row_score.reshape(expert_count, capacity), EXPERT, split_axis=0, concat_axis=0, tiled=True
    )
    route_grad = live_rows * returned_score / route_matrix

    sum_a = pick(part_a, z0, 3) + came_a.astype(jnp.float32)
    sum_b = pick(part_b, y0, 1) + came_b.astype(jnp.float32)
    sent_a = pick(sum_a, 1 - y0, 1).astype(jnp.bfloat16)
    sent_b = pick(sum_b, 1 - z0, 2).astype(jnp.bfloat16)
    came_a = swap(sent_a, "y0")
    came_b = swap(sent_b, "z0")
    sum_a = pick(sum_a, y0, 1) + came_a.astype(jnp.float32)
    sum_b = pick(sum_b, z0, 2) + came_b.astype(jnp.float32)
    spread = jnp.concatenate([sum_a, sum_b], axis=-1).astype(jnp.bfloat16)
    gathered = lax.all_to_all(
        spread.reshape(size_y1 * size_zz * 2, unit // 2, half),
        ("y1", "zz", "core"), split_axis=0, concat_axis=0, tiled=True,
    ).reshape(size_y1 * size_zz, 2, unit // 2, half)
    total = jnp.sum(gathered.astype(jnp.float32), axis=0) / replica_count
    weight_grad = jnp.concatenate([total[0], total[1]], axis=1)[None]
    return (grad_rows, weight_grad, route_grad.reshape(row_total))


def solution(mesh):
    fine = Mesh(mesh.devices.reshape(2, 4, 2, 2, 6, 2, 2), DEVICE)
    in_specs = (P(DEVICE, None), P(DEVICE), P(DEVICE), P(DEVICE, None), P(EXPERT, None, None))
    out_specs = (P(DEVICE, None), P(EXPERT, EDATA, None), P(DEVICE))
    return jax.shard_map(body, mesh=fine, in_specs=in_specs, out_specs=out_specs, check_vma=False)
```

time: 500 us -> 141 us (0.28)
  waiting for transfers between devices: 426 us -> 60.9 us
  starting transfers between devices: 4.26 us -> 57.8 us
  blocking collectives: 32.8 us -> 0 us
  between operations: 14.1 us -> 0.9 us
  matrix products: 7.98 us -> 2.4 us
  other arithmetic: 6.09 us -> 11.4 us
    reduce_scatter x1 -> x0, waiting for transfers between devices: 419 us -> none  [body(): lax.psum_scatter(partial_sum, 'edata', scatter_dimension=0, tiled=True)]
    all_to_all x1 -> x3, waiting for transfers between devices: 7.9 us -> 55.8 us  [the longest x1 27.9 us: body(): lax.all_to_all(outgoing.reshape(expert_count * 2, capacity, half), EXPERT...]
    all_to_all x1 -> x0, blocking collectives: 32.8 us -> none  [body(): lax.all_to_all(scaled_rows, 'expert', split_axis=0, concat_axis=0, tiled=...]
    all_to_all x1 -> x3, starting transfers between devices: 4.22 us -> 36.4 us  [the longest x1 16.7 us: body(): lax.all_to_all(spread.reshape(size_y1 * size_zz * 2, unit // 2, half), ('...]
    ppermute x0 -> x6, starting transfers between devices: none -> 21.4 us  [swap(): return lax.ppermute(value, axis, [(0, 1), (1, 0)])]
    dot_general x2, matrix products: 7.98 us -> 2.4 us  [the longest x1 1.22 us: body(): lax.dot_general(arrived.reshape(2 * row_total, half), weight_half, (((1,)...]
    ppermute x0 -> x6, waiting for transfers between devices: none -> 5.1 us  [swap(): return lax.ppermute(value, axis, [(0, 1), (1, 0)])]
  transfers between devices with their start and end apart: 2 -> 9, of which waited for: 2 -> 7; matrix products, arithmetic and copies ran while one was open for 1% -> 8% of each run, Pallas kernels for 0% -> 0%
where the time goes in v1:
time: 141 us; the launch traced here: 140 us
  waiting for transfers between devices  60.9 us (43%)
  starting transfers between devices  57.8 us (41%)
  other arithmetic  11.4 us (8%)
  local copies, waits for them, and re-layouts  6.8 us (5%)
  matrix products  2.4 us (2%)
    all_to_all x1, waiting for transfers between devices, body(): lax.all_to_all(outgoing.reshape(expert_count * 2, capacity, half), EXPERT...  27.9 us
    ppermute x6, starting transfers between devices, swap(): return lax.ppermute(value, axis, [(0, 1), (1, 0)])  21.4 us
    all_to_all x1, waiting for transfers between devices, body(): lax.all_to_all(spread.reshape(size_y1 * size_zz * 2, unit // 2, half), ('...  19.9 us
    all_to_all x1, starting transfers between devices, body(): lax.all_to_all(spread.reshape(size_y1 * size_zz * 2, unit // 2, half), ('...  16.7 us
    all_to_all x1, starting transfers between devices, body(): lax.all_to_all(outgoing.reshape(expert_count * 2, capacity, half), EXPERT...  14.1 us
    all_to_all x1, waiting for transfers between devices, body(): lax.all_to_all(row_score.reshape(expert_count, capacity), EXPERT, split_a...  7.99 us
    all_to_all x1, starting transfers between devices, body(): lax.all_to_all(row_score.reshape(expert_count, capacity), EXPERT, split_a...  5.58 us
    ppermute x6, waiting for transfers between devices, swap(): return lax.ppermute(value, axis, [(0, 1), (1, 0)])  5.1 us
  transfers between devices with their start and end apart: 9, of which 7 were waited for; matrix products, arithmetic and copies ran while one was open for 8% of the time, Pallas kernels for 0%

profile of v1, /device:TPU:1, one launch (start us, length us, event | category | flops | bytes accessed | tf_op | source)
XLA Modules:
  0.0 140.3 jit_solution(5061371039318275777)
XLA Ops:
  0.6 0.8 reshape.79
  1.4 0.7 broadcast_select_fusion
  2.1 1.6 %fusion = bf16[8,32,2560]{2,1,0:T(8,128)(2,1)S(1)} fusion(bf16[8,32,2560]{2,1,0:T(8,128)(2,1)} %bitcast.83, f32[8,32]{1,0:T(8,128)S(1)} %broadcast_select_fusion), kind=kLoop, calls=%fused_computation.1 | loop fusion | flops 1966080 | bytes 2622464 | tf_op jit(solution)/shard_map/convert_element_type | solution.py:48
  4.0 1.2 copy.10
  5.1 14.1 %all-to-all-start = ((bf16[16,32,1280]{2,1,0:T(8,128)(2,1)}), bf16[16,32,1280]{2,1,0:T(8,128)(2,1)S(1)}, u32[]{:S(2)}, u32[]{:S(2)}) async-start(bf16[16,32,1280]{2,1,0:T(8,128)(2,1)} %bitcast.3), calls=%async_computation | async-start | bytes 2621440 | tf_op jit(solution)/shard_map/all_to_all | solution.py:50
  19.6 2.1 %collective-permute-start = (bf16[8,32,768]{2,1,0:T(8,128)(2,1)S(1)}, bf16[8,32,768]{2,1,0:T(8,128)(2,1)S(1)}, u32[]{:S(2)}, u32[]{:S(2)}) collective-permute-start(bf16[8,32,768]{2,1,0:T(8,128)(2,1)S(1)} %bitcast.81), channel_id=1, source_target_pairs={{0,1},{1,0},{2,3},{3,2},{4,5},{5,4},{6,7},{7,6},{8,9},{9,8},{10,11... | collective-permute-start | bytes 1179656 | tf_op jit(solution)/shard_map/ppermute | solution.py:12
  21.7 1.5 %collective-permute-done = bf16[8,32,768]{2,1,0:T(8,128)(2,1)S(1)} collective-permute-done((bf16[8,32,768]{2,1,0:T(8,128)(2,1)S(1)}, bf16[8,32,768]{2,1,0:T(8,128)(2,1)S(1)}, u32[]{:S(2)}, u32[]{:S(2)}) %collective-permute-start) | collective-permute-done | bytes 393248 | tf_op jit(solution)/shard_map/ppermute | solution.py:12
  23.6 27.9 %all-to-all-done = bf16[16,32,1280]{2,1,0:T(8,128)(2,1)S(1)} async-done(((bf16[16,32,1280]{2,1,0:T(8,128)(2,1)}), bf16[16,32,1280]{2,1,0:T(8,128)(2,1)S(1)}, u32[]{:S(2)}, u32[]{:S(2)}) %all-to-all-start) | async-done | bytes 1310752 | tf_op jit(solution)/shard_map/all_to_all | solution.py:50
  51.5 1.2 fusion.22
  53.3 2.1 %collective-permute-start.2 = (bf16[2,2,6,16,640]{4,3,2,1,0:T(8,128)(2,1)S(1)}, bf16[2,2,6,16,640]{4,3,2,1,0:T(8,128)(2,1)S(1)}, u32[]{:S(2)}, u32[]{:S(2)}) collective-permute-start(bf16[2,2,6,16,640]{4,3,2,1,0:T(8,128)(2,1)S(1)} %fusion.14), channel_id=1, source_target_pairs={{0,2},{2,0},{1,3},{3,1},{4,6},{6,4},{5,7},{7,5},{8,10},{10,8},{9,1... | collective-permute-start | bytes 1474568 | tf_op jit(solution)/shard_map/ppermute | solution.py:12
  55.4 5.8 %collective-permute-start.4 = (bf16[2,6,2,16,640]{4,3,2,1,0:T(8,128)(2,1)S(1)}, bf16[2,6,2,16,640]{4,3,2,1,0:T(8,128)(2,1)S(1)}, u32[]{:S(2)}, u32[]{:S(2)}) collective-permute-start(bf16[2,6,2,16,640]{4,3,2,1,0:T(8,128)(2,1)S(1)} %fusion.15), channel_id=1, source_target_pairs={{0,24},{24,0},{1,25},{25,1},{2,26},{26,2},{3,27},{27,3},{4,28},{28... | collective-permute-start | bytes 1474568 | tf_op jit(solution)/shard_map/ppermute | solution.py:12
  61.3 1.2 fusion.1
  62.5 1.0 dynamic-slice_bitcast_fusion
  63.5 3.2 %collective-permute-start.1 = (f32[8,32,768]{2,1,0:T(8,128)}, f32[8,32,768]{2,1,0:T(8,128)}, u32[]{:S(2)}, u32[]{:S(2)}) collective-permute-start(f32[8,32,768]{2,1,0:T(8,128)} %dynamic-slice_bitcast_fusion), channel_id=1, source_target_pairs={{0,1},{1,0},{2,3},{3,2},{4,5},{5,4},{6,7},{7,6},{8,9},{9,8},{10,11... | collective-permute-start | bytes 2359304 | tf_op jit(solution)/shard_map/ppermute | solution.py:12
  67.1 0.7 fusion.18
  67.8 5.1 %collective-permute-start.3 = (bf16[2,6,16,640]{3,2,1,0:T(8,128)(2,1)}, bf16[2,6,16,640]{3,2,1,0:T(8,128)(2,1)}, u32[]{:S(2)}, u32[]{:S(2)}) collective-permute-start(bf16[2,6,16,640]{3,2,1,0:T(8,128)(2,1)} %fusion.18), channel_id=1, source_target_pairs={{0,24},{24,0},{1,25},{25,1},{2,26},{26,2},{3,27},{27,3},{4,28},{28... | collective-permute-start | bytes 737288 | tf_op jit(solution)/shard_map/ppermute | solution.py:12
  73.1 0.7 fusion.19
  73.8 3.0 %collective-permute-start.5 = (bf16[2,6,16,640]{3,2,1,0:T(8,128)(2,1)}, bf16[2,6,16,640]{3,2,1,0:T(8,128)(2,1)}, u32[]{:S(2)}, u32[]{:S(2)}) collective-permute-start(bf16[2,6,16,640]{3,2,1,0:T(8,128)(2,1)} %fusion.19), channel_id=1, source_target_pairs={{0,2},{2,0},{1,3},{3,1},{4,6},{6,4},{5,7},{7,5},{8,10},{10,8},{9,1... | collective-permute-start | bytes 737288 | tf_op jit(solution)/shard_map/ppermute | solution.py:12
  76.8 1.4 collective-permute-done.3
  78.2 1.7 %fusion.17 = bf16[2,6,16,640]{3,2,1,0:T(8,128)(2,1)} fusion(bf16[2,6,16,640]{3,2,1,0:T(8,128)(2,1)} %collective-permute-done.3, f32[2,2,6,16,640]{4,3,2,1,0:T(8,128)S(1)} %bitcast_add_fusion.1, s32[]{:T(128)S(6)} %select_n.51), kind=kLoop, calls=%fused_computation.40 | loop fusion | flops 368640 | bytes 983044 | tf_op jit(solution)/shard_map/convert.5
  79.9 2.0 %collective-permute-done.5 = bf16[2,6,16,640]{3,2,1,0:T(8,128)(2,1)} collective-permute-done((bf16[2,6,16,640]{3,2,1,0:T(8,128)(2,1)}, bf16[2,6,16,640]{3,2,1,0:T(8,128)(2,1)}, u32[]{:S(2)}, u32[]{:S(2)}) %collective-permute-start.5) | collective-permute-done | bytes 245792 | tf_op jit(solution)/shard_map/ppermute | solution.py:12
  81.9 1.0 fusion.16
  82.9 1.2 bitcast_add_fusion.2
  84.2 0.6 fusion.7
  84.8 0.7 all_to_all.16
  85.5 5.6 %all-to-all-start.2 = ((f32[8,1,32]{2,1,0:T(1,128)}), f32[8,1,32]{2,1,0:T(1,128)S(1)}, u32[]{:S(2)}, u32[]{:S(2)}) async-start(f32[8,1,32]{2,1,0:T(1,128)} %all_to_all.16), calls=%async_computation.2 | async-start | bytes 8192 | tf_op jit(solution)/shard_map/all_to_all | solution.py:88
  91.1 0.8 pad_maximum_fusion.3
  91.9 8.0 %all-to-all-done.2 = f32[8,1,32]{2,1,0:T(1,128)S(1)} async-done(((f32[8,1,32]{2,1,0:T(1,128)}), f32[8,1,32]{2,1,0:T(1,128)S(1)}, u32[]{:S(2)}, u32[]{:S(2)}) %all-to-all-start.2) | async-done | bytes 1056 | tf_op jit(solution)/shard_map/all_to_all | solution.py:88
  99.9 16.7 %all-to-all-start.1 = ((bf16[24,8,1280]{2,1,0:T(8,128)(2,1)}), bf16[24,8,1280]{2,1,0:T(8,128)(2,1)S(1)}, u32[]{:S(2)}, u32[]{:S(2)}) async-start(bf16[24,8,1280]{2,1,0:T(8,128)(2,1)} %pad_maximum_fusion.3), calls=%async_computation.1 | async-start | bytes 983040 | tf_op jit(solution)/shard_map/all_to_all | solution.py:102
  116.8 0.9 pad_maximum_fusion.2
  118.3 0.7 reduce.3
  119.6 19.9 %all-to-all-done.1 = bf16[24,8,1280]{2,1,0:T(8,128)(2,1)S(1)} async-done(((bf16[24,8,1280]{2,1,0:T(8,128)(2,1)}), bf16[24,8,1280]{2,1,0:T(8,128)(2,1)S(1)}, u32[]{:S(2)}, u32[]{:S(2)}) %all-to-all-start.1) | async-done | bytes 491552 | tf_op jit(solution)/shard_map/all_to_all | solution.py:102
  (35 shorter events, 4.1 us)
Async XLA Ops:
  5.1 14.1 %copy-start = (bf16[256,1536]{1,0:T(8,128)(2,1)S(1)}, bf16[256,1536]{1,0:T(8,128)(2,1)}, u32[]{:S(2)}) copy-start(bf16[256,1536]{1,0:T(8,128)(2,1)} %param.8) | copy-start | bytes 2359300
  5.1 46.4 %all-to-all-start = ((bf16[16,32,1280]{2,1,0:T(8,128)(2,1)}), bf16[16,32,1280]{2,1,0:T(8,128)(2,1)S(1)}, u32[]{:S(2)}, u32[]{:S(2)}) async-start(bf16[16,32,1280]{2,1,0:T(8,128)(2,1)} %bitcast.3), calls=%async_computation | async-start | bytes 2621440 | tf_op jit(solution)/shard_map/all_to_all | solution.py:50
  19.6 3.6 %collective-permute-start = (bf16[8,32,768]{2,1,0:T(8,128)(2,1)S(1)}, bf16[8,32,768]{2,1,0:T(8,128)(2,1)S(1)}, u32[]{:S(2)}, u32[]{:S(2)}) collective-permute-start(bf16[8,32,768]{2,1,0:T(8,128)(2,1)S(1)} %bitcast.81), channel_id=1, source_target_pairs={{0,1},{1,0},{2,3},{3,2},{4,5},{5,4},{6,7},{7,6},{8,9},{9,8},{10,11... | collective-permute-start | bytes 1179656 | tf_op jit(solution)/shard_map/ppermute | solution.py:12
  52.7 8.6 %copy-start.5 = (bf16[1,768,2560]{2,1,0:T(8,128)(2,1)S(1)}, bf16[1,768,2560]{2,1,0:T(8,128)(2,1)}, u32[]{:S(2)}) copy-start(bf16[1,768,2560]{2,1,0:T(8,128)(2,1)} %param.9) | copy-start | bytes 11796484
  53.3 13.6 %collective-permute-start.2 = (bf16[2,2,6,16,640]{4,3,2,1,0:T(8,128)(2,1)S(1)}, bf16[2,2,6,16,640]{4,3,2,1,0:T(8,128)(2,1)S(1)}, u32[]{:S(2)}, u32[]{:S(2)}) collective-permute-start(bf16[2,2,6,16,640]{4,3,2,1,0:T(8,128)(2,1)S(1)} %fusion.14), channel_id=1, source_target_pairs={{0,2},{2,0},{1,3},{3,1},{4,6},{6,4},{5,7},{7,5},{8,10},{10,8},{9,1... | collective-permute-start | bytes 1474568 | tf_op jit(solution)/shard_map/ppermute | solution.py:12
  55.4 17.5 %collective-permute-start.4 = (bf16[2,6,2,16,640]{4,3,2,1,0:T(8,128)(2,1)S(1)}, bf16[2,6,2,16,640]{4,3,2,1,0:T(8,128)(2,1)S(1)}, u32[]{:S(2)}, u32[]{:S(2)}) collective-permute-start(bf16[2,6,2,16,640]{4,3,2,1,0:T(8,128)(2,1)S(1)} %fusion.15), channel_id=1, source_target_pairs={{0,24},{24,0},{1,25},{25,1},{2,26},{26,2},{3,27},{27,3},{4,28},{28... | collective-permute-start | bytes 1474568 | tf_op jit(solution)/shard_map/ppermute | solution.py:12
  63.5 19.4 %collective-permute-start.1 = (f32[8,32,768]{2,1,0:T(8,128)}, f32[8,32,768]{2,1,0:T(8,128)}, u32[]{:S(2)}, u32[]{:S(2)}) collective-permute-start(f32[8,32,768]{2,1,0:T(8,128)} %dynamic-slice_bitcast_fusion), channel_id=1, source_target_pairs={{0,1},{1,0},{2,3},{3,2},{4,5},{5,4},{6,7},{7,6},{8,9},{9,8},{10,11... | collective-permute-start | bytes 2359304 | tf_op jit(solution)/shard_map/ppermute | solution.py:12
  67.8 10.4 %collective-permute-start.3 = (bf16[2,6,16,640]{3,2,1,0:T(8,128)(2,1)}, bf16[2,6,16,640]{3,2,1,0:T(8,128)(2,1)}, u32[]{:S(2)}, u32[]{:S(2)}) collective-permute-start(bf16[2,6,16,640]{3,2,1,0:T(8,128)(2,1)} %fusion.18), channel_id=1, source_target_pairs={{0,24},{24,0},{1,25},{25,1},{2,26},{26,2},{3,27},{27,3},{4,28},{28... | collective-permute-start | bytes 737288 | tf_op jit(solution)/shard_map/ppermute | solution.py:12
  73.8 8.1 %collective-permute-start.5 = (bf16[2,6,16,640]{3,2,1,0:T(8,128)(2,1)}, bf16[2,6,16,640]{3,2,1,0:T(8,128)(2,1)}, u32[]{:S(2)}, u32[]{:S(2)}) collective-permute-start(bf16[2,6,16,640]{3,2,1,0:T(8,128)(2,1)} %fusion.19), channel_id=1, source_target_pairs={{0,2},{2,0},{1,3},{3,1},{4,6},{6,4},{5,7},{7,5},{8,10},{10,8},{9,1... | collective-permute-start | bytes 737288 | tf_op jit(solution)/shard_map/ppermute | solution.py:12
  79.9 4.2 %copy-start.1 = (bf16[256,1536]{1,0:T(8,128)(2,1)S(1)}, bf16[256,1536]{1,0:T(8,128)(2,1)}, u32[]{:S(2)}) copy-start(bf16[256,1536]{1,0:T(8,128)(2,1)} %param.8) | copy-start | bytes 2359300
  84.1 6.9 %copy-start.2 = (bf16[2,6,16,640]{3,2,1,0:T(8,128)(2,1)S(1)}, bf16[2,6,16,640]{3,2,1,0:T(8,128)(2,1)}, u32[]{:S(2)}) copy-start(bf16[2,6,16,640]{3,2,1,0:T(8,128)(2,1)} %fusion.17) | copy-start | bytes 737284
  84.8 31.8 %copy-start.4 = (s32[8]{0:T(128)S(1)}, s32[8]{0:T(128)}, u32[]{:S(2)}) copy-start(s32[8]{0:T(128)} %param.7) | copy-start | bytes 100
  85.5 14.4 %all-to-all-start.2 = ((f32[8,1,32]{2,1,0:T(1,128)}), f32[8,1,32]{2,1,0:T(1,128)S(1)}, u32[]{:S(2)}, u32[]{:S(2)}) async-start(f32[8,1,32]{2,1,0:T(1,128)} %all_to_all.16), calls=%async_computation.2 | async-start | bytes 8192 | tf_op jit(solution)/shard_map/all_to_all | solution.py:88
  91.1 27.9 %copy-start.3 = (f32[256]{0:T(256)S(1)}, f32[256]{0:T(256)}, u32[]{:S(2)}) copy-start(f32[256]{0:T(256)} %param.6) | copy-start | bytes 3076
  99.9 39.6 %all-to-all-start.1 = ((bf16[24,8,1280]{2,1,0:T(8,128)(2,1)}), bf16[24,8,1280]{2,1,0:T(8,128)(2,1)S(1)}, u32[]{:S(2)}, u32[]{:S(2)}) async-start(bf16[24,8,1280]{2,1,0:T(8,128)(2,1)} %pad_maximum_fusion.3), calls=%async_computation.1 | async-start | bytes 983040 | tf_op jit(solution)/shard_map/all_to_all | solution.py:102

commit v2 on v1

--- a/solution.py
+++ b/solution.py
@@ -4,7 +4,8 @@
 from jax.sharding import Mesh, PartitionSpec as P
 
 EXPERT = ("yh", "x")
-EDATA = ("y1", "y0", "zz", "z0", "core")
+EDATA = ("y1", "y0", "zc", "z1", "z0", "core")
+ROWS = ("y1", "y0", "zc", "z1", "z0")
 DEVICE = EXPERT + EDATA
 
 
@@ -16,6 +17,20 @@
     return lax.dynamic_index_in_dim(value, index, axis, keepdims=False)
 
 
+class Piece:
+    def __init__(self, value, dims):
+        self.value, self.dims = value, dims
+
+    def send(self, axis):
+        self.axis, self.at = axis, self.dims.index(axis)
+        self.sent = pick(self.value, 1 - lax.axis_index(axis), self.at).astype(jnp.bfloat16)
+        self.came = swap(self.sent, axis)
+
+    def receive(self):
+        self.value = pick(self.value, lax.axis_index(self.axis), self.at) + self.came.astype(jnp.float32)
+        self.dims = self.dims[: self.at] + self.dims[self.at + 1 :]
+
+
 def body(grad_out, route_weight, counts, preact, down_weight):
     row_total, feature_count = grad_out.shape
     expert_count = lax.axis_size(EXPERT)
@@ -25,9 +40,7 @@
     quarter = half // 2
     replica_count = lax.axis_size(EDATA)
     core = lax.axis_index("core")
-    z0 = lax.axis_index("z0")
-    y0 = lax.axis_index("y0")
-    size_y1, size_zz = lax.axis_size("y1"), lax.axis_size("zz")
+    cube_count = lax.axis_size("zc")
     unit = hidden_count // (replica_count // 2)
 
     slot_index = lax.broadcasted_iota(jnp.int32, (expert_count, capacity), 1)
@@ -64,14 +77,12 @@
         hidden_all, arrived.reshape(2 * row_total, half), (((0,), (0,)), ((), ())),
         preferred_element_type=jnp.float32,
     )
-    parts = partial_sum.reshape(size_y1, 2, size_zz, 2, unit, half)
-    part_a, part_b = parts[..., :quarter], parts[..., quarter:]
-    sent_a = pick(part_a, 1 - z0, 3).astype(jnp.bfloat16)
-    sent_b = pick(part_b, 1 - y0, 1).astype(jnp.bfloat16)
-    came_a = swap(sent_a, "z0")
-    came_b = swap(sent_b, "y0")
+    parts = partial_sum.reshape([lax.axis_size(axis) for axis in ROWS] + [unit, half])
+    piece_a, piece_b = Piece(parts[..., :quarter], ROWS), Piece(parts[..., quarter:], ROWS)
+    piece_a.send("z0")
+    piece_b.send("y0")
 
-    arrived, sent_a, sent_b = lax.optimization_barrier((arrived, sent_a, sent_b))
+    arrived, _, _ = lax.optimization_barrier((arrived, piece_a.sent, piece_b.sent))
     weight_half = lax.dynamic_slice(
         down_weight[0], (0, core * half), (hidden_count, half)
     )
@@ -85,31 +96,31 @@
     grad_up = grad_hidden * silu_gate
     grad_rows = jnp.concatenate([grad_gate, grad_up], axis=1).astype(jnp.bfloat16)
     row_score = jnp.sum(grad_hidden * hidden_act.astype(jnp.float32), axis=1)
+    for next_a, next_b in (("y0", "z0"), ("z1", "y1"), ("y1", "z1"), (None, None)):
+        if next_a == "z1":
+            piece_a.came, row_score = lax.optimization_barrier((piece_a.came, row_score))
+        piece_a.receive()
+        piece_b.receive()
+        if next_a is not None:
+            piece_a.send(next_a)
+            piece_b.send(next_b)
     returned_score = lax.all_to_all(
         row_score.reshape(expert_count, capacity), EXPERT, split_axis=0, concat_axis=0, tiled=True
     )
     route_grad = live_rows * returned_score / route_matrix
 
-    sum_a = pick(part_a, z0, 3) + came_a.astype(jnp.float32)
-    sum_b = pick(part_b, y0, 1) + came_b.astype(jnp.float32)
-    sent_a = pick(sum_a, 1 - y0, 1).astype(jnp.bfloat16)
-    sent_b = pick(sum_b, 1 - z0, 2).astype(jnp.bfloat16)
-    came_a = swap(sent_a, "y0")
-    came_b = swap(sent_b, "z0")
-    sum_a = pick(sum_a, y0, 1) + came_a.astype(jnp.float32)
-    sum_b = pick(sum_b, z0, 2) + came_b.astype(jnp.float32)
-    spread = jnp.concatenate([sum_a, sum_b], axis=-1).astype(jnp.bfloat16)
+    spread = jnp.concatenate([piece_a.value, piece_b.value], axis=-1).astype(jnp.bfloat16)
     gathered = lax.all_to_all(
-        spread.reshape(size_y1 * size_zz * 2, unit // 2, half),
-        ("y1", "zz", "core"), split_axis=0, concat_axis=0, tiled=True,
-    ).reshape(size_y1 * size_zz, 2, unit // 2, half)
+        spread.reshape(cube_count * 2, unit // 2, half),
+        ("zc", "core"), split_axis=0, concat_axis=0, tiled=True,
+    ).reshape(cube_count, 2, unit // 2, half)
     total = jnp.sum(gathered.astype(jnp.float32), axis=0) / replica_count
     weight_grad = jnp.concatenate([total[0], total[1]], axis=1)[None]
     return (grad_rows, weight_grad, route_grad.reshape(row_total))
 
 
 def solution(mesh):
-    fine = Mesh(mesh.devices.reshape(2, 4, 2, 2, 6, 2, 2), DEVICE)
+    fine = Mesh(mesh.devices.reshape(2, 4, 2, 2, 3, 2, 2, 2), DEVICE)
     in_specs = (P(DEVICE, None), P(DEVICE), P(DEVICE), P(DEVICE, None), P(EXPERT, None, None))
     out_specs = (P(DEVICE, None), P(EXPERT, EDATA, None), P(DEVICE))
     return jax.shard_map(body, mesh=fine, in_specs=in_specs, out_specs=out_specs, check_vma=False)

time: 141 us -> 128 us (0.908)
  waiting for transfers between devices: 60.9 us -> 40 us
  starting transfers between devices: 57.8 us -> 68.7 us
  other arithmetic: 11.4 us -> 7.6 us
    all_to_all x1, waiting for transfers between devices: 19.9 us -> 4.96 us  [body(): lax.all_to_all(spread.reshape(cube_count * 2, unit // 2, half), ('zc', 'c...]
    ppermute x6 -> x10, starting transfers between devices: 21.4 us -> 34.4 us  [swap(): return lax.ppermute(value, axis, [(0, 1), (1, 0)])]
    all_to_all x1, waiting for transfers between devices: 7.99 us -> 0.01 us  [body(): lax.all_to_all(row_score.reshape(expert_count, capacity), EXPERT, split_a...]
    ppermute x6 -> x10, waiting for transfers between devices: 5.1 us -> 8 us  [swap(): return lax.ppermute(value, axis, [(0, 1), (1, 0)])]
    another operation x3, other arithmetic: 3.33 us -> 0.68 us
  transfers between devices with their start and end apart: 9 -> 13, of which waited for: 7 -> 6; matrix products, arithmetic and copies ran while one was open for 8% -> 6% of each run, Pallas kernels for 0% -> 0%
where the time goes in v2:
time: 128 us; the launch traced here: 126 us
  starting transfers between devices  68.7 us (54%)
  waiting for transfers between devices  40 us (31%)
  other arithmetic  7.6 us (6%)
  local copies, waits for them, and re-layouts  5.41 us (4%)
  matrix products  3.54 us (3%)
    ppermute x10, starting transfers between devices, swap(): return lax.ppermute(value, axis, [(0, 1), (1, 0)])  34.4 us
    all_to_all x1, waiting for transfers between devices, body(): lax.all_to_all(outgoing.reshape(expert_count * 2, capacity, half), EXPERT...  27.1 us
    all_to_all x1, starting transfers between devices, body(): lax.all_to_all(spread.reshape(cube_count * 2, unit // 2, half), ('zc', 'c...  15.3 us
    all_to_all x1, starting transfers between devices, body(): lax.all_to_all(outgoing.reshape(expert_count * 2, capacity, half), EXPERT...  14.1 us
    ppermute x10, waiting for transfers between devices, swap(): return lax.ppermute(value, axis, [(0, 1), (1, 0)])  8 us
    all_to_all x1, waiting for transfers between devices, body(): lax.all_to_all(spread.reshape(cube_count * 2, unit // 2, half), ('zc', 'c...  4.96 us
    all_to_all x1, starting transfers between devices, body(): lax.all_to_all(row_score.reshape(expert_count, capacity), EXPERT, split_a...  4.91 us
  transfers between devices with their start and end apart: 13, of which 6 were waited for; matrix products, arithmetic and copies ran while one was open for 6% of the time, Pallas kernels for 0%

profile of v2, /device:TPU:1, one launch (start us, length us, event | category | flops | bytes accessed | tf_op | source)
XLA Modules:
  0.0 126.4 jit_solution(6991556249324236407)
XLA Ops:
  0.6 0.8 reshape.83
  1.4 0.7 broadcast_select_fusion
  2.1 1.6 %fusion = bf16[8,32,2560]{2,1,0:T(8,128)(2,1)S(1)} fusion(bf16[8,32,2560]{2,1,0:T(8,128)(2,1)} %bitcast.95, f32[8,32]{1,0:T(8,128)S(1)} %broadcast_select_fusion), kind=kLoop, calls=%fused_computation.1 | loop fusion | flops 1966080 | bytes 2622464 | tf_op jit(solution)/shard_map/convert_element_type | solution.py:61
  3.9 1.2 copy.10
  5.1 14.1 %all-to-all-start = ((bf16[16,32,1280]{2,1,0:T(8,128)(2,1)}), bf16[16,32,1280]{2,1,0:T(8,128)(2,1)S(1)}, u32[]{:S(2)}, u32[]{:S(2)}) async-start(bf16[16,32,1280]{2,1,0:T(8,128)(2,1)} %bitcast.3), calls=%async_computation | async-start | bytes 2621440 | tf_op jit(solution)/shard_map/all_to_all | solution.py:63
  19.5 2.1 %collective-permute-start = (bf16[8,32,768]{2,1,0:T(8,128)(2,1)S(1)}, bf16[8,32,768]{2,1,0:T(8,128)(2,1)S(1)}, u32[]{:S(2)}, u32[]{:S(2)}) collective-permute-start(bf16[8,32,768]{2,1,0:T(8,128)(2,1)S(1)} %bitcast.93), channel_id=1, source_target_pairs={{0,1},{1,0},{2,3},{3,2},{4,5},{5,4},{6,7},{7,6},{8,9},{9,8},{10,11... | collective-permute-start | bytes 1179656 | tf_op jit(solution)/shard_map/ppermute | solution.py:13
  21.8 1.3 %collective-permute-done = bf16[8,32,768]{2,1,0:T(8,128)(2,1)S(1)} collective-permute-done((bf16[8,32,768]{2,1,0:T(8,128)(2,1)S(1)}, bf16[8,32,768]{2,1,0:T(8,128)(2,1)S(1)}, u32[]{:S(2)}, u32[]{:S(2)}) %collective-permute-start) | collective-permute-done | bytes 393248 | tf_op jit(solution)/shard_map/ppermute | solution.py:13
  23.3 1.2 copy.12
  24.4 27.1 %all-to-all-done = bf16[16,32,1280]{2,1,0:T(8,128)(2,1)S(1)} async-done(((bf16[16,32,1280]{2,1,0:T(8,128)(2,1)}), bf16[16,32,1280]{2,1,0:T(8,128)(2,1)S(1)}, u32[]{:S(2)}, u32[]{:S(2)}) %all-to-all-start) | async-done | bytes 1310752 | tf_op jit(solution)/shard_map/all_to_all | solution.py:63
  51.5 2.3 %fusion.26 = f32[2,2,3,2,2,16,1280]{6,5,4,3,2,1,0:T(8,128)S(1)} fusion(bf16[2,2,3,2,2,16,512]{6,5,4,3,2,1,0:T(8,128)(2,1)} %bitcast.98, bf16[512,1280,1,1,1,1,1]{1,0,6,5,4,3,2:T(8,128)(2,1)S(1)} %bitcast.96), kind=kOutput, calls=%fused_computation.68 | convolution fusion | flops 1006632960 | bytes 6029312 | tf_op jit(solution)/shard_map/dot_general | solution.py:76
  54.4 3.8 %collective-permute-start.6 = (bf16[2,3,2,2,16,640]{5,4,3,2,1,0:T(8,128)(2,1)S(1)}, bf16[2,3,2,2,16,640]{5,4,3,2,1,0:T(8,128)(2,1)S(1)}, u32[]{:S(2)}, u32[]{:S(2)}) collective-permute-start(bf16[2,3,2,2,16,640]{5,4,3,2,1,0:T(8,128)(2,1)S(1)} %fusion.15), channel_id=1, source_target_pairs={{0,24},{24,0},{1,25},{25,1},{2,26},{26,2},{3,27},{27,3},{4,28},{28... | collective-permute-start | bytes 1474568 | tf_op jit(solution)/shard_map/ppermute | solution.py:13
  58.4 4.0 %collective-permute-start.2 = (bf16[2,2,3,2,16,640]{5,4,3,2,1,0:T(8,128)(2,1)S(1)}, bf16[2,2,3,2,16,640]{5,4,3,2,1,0:T(8,128)(2,1)S(1)}, u32[]{:S(2)}, u32[]{:S(2)}) collective-permute-start(bf16[2,2,3,2,16,640]{5,4,3,2,1,0:T(8,128)(2,1)S(1)} %fusion.14), channel_id=1, source_target_pairs={{0,2},{2,0},{1,3},{3,1},{4,6},{6,4},{5,7},{7,5},{8,10},{10,8},{9,1... | collective-permute-start | bytes 1474568 | tf_op jit(solution)/shard_map/ppermute | solution.py:13
  62.4 1.2 fusion.1
  63.7 3.2 %collective-permute-start.1 = (f32[8,32,768]{2,1,0:T(8,128)S(1)}, f32[8,32,768]{2,1,0:T(8,128)S(1)}, u32[]{:S(2)}, u32[]{:S(2)}) collective-permute-start(f32[8,32,768]{2,1,0:T(8,128)S(1)} %dynamic-slice_bitcast_fusion), channel_id=1, source_target_pairs={{0,1},{1,0},{2,3},{3,2},{4,5},{5,4},{6,7},{7,6},{8,9},{9,8},{10,11... | collective-permute-start | bytes 2359304 | tf_op jit(solution)/shard_map/ppermute | solution.py:13
  66.9 2.2 %collective-permute-done.6 = bf16[2,3,2,2,16,640]{5,4,3,2,1,0:T(8,128)(2,1)S(1)} collective-permute-done((bf16[2,3,2,2,16,640]{5,4,3,2,1,0:T(8,128)(2,1)S(1)}, bf16[2,3,2,2,16,640]{5,4,3,2,1,0:T(8,128)(2,1)S(1)}, u32[]{:S(2)}, u32[]{:S(2)}) %collective-permute-start.6) | collective-permute-done | bytes 491552 | tf_op jit(solution)/shard_map/ppermute | solution.py:13
  69.2 4.1 %collective-permute-start.7 = (bf16[2,3,2,16,640]{4,3,2,1,0:T(8,128)(2,1)S(1)}, bf16[2,3,2,16,640]{4,3,2,1,0:T(8,128)(2,1)S(1)}, u32[]{:S(2)}, u32[]{:S(2)}) collective-permute-start(bf16[2,3,2,16,640]{4,3,2,1,0:T(8,128)(2,1)S(1)} %fusion.17), channel_id=1, source_target_pairs={{0,2},{2,0},{1,3},{3,1},{4,6},{6,4},{5,7},{7,5},{8,10},{10,8},{9,1... | collective-permute-start | bytes 737288 | tf_op jit(solution)/shard_map/ppermute | solution.py:13
  73.5 3.0 %collective-permute-start.3 = (bf16[2,3,2,16,640]{4,3,2,1,0:T(8,128)(2,1)S(1)}, bf16[2,3,2,16,640]{4,3,2,1,0:T(8,128)(2,1)S(1)}, u32[]{:S(2)}, u32[]{:S(2)}) collective-permute-start(bf16[2,3,2,16,640]{4,3,2,1,0:T(8,128)(2,1)S(1)} %fusion.16), channel_id=1, source_target_pairs={{0,24},{24,0},{1,25},{25,1},{2,26},{26,2},{3,27},{27,3},{4,28},{28... | collective-permute-start | bytes 737288 | tf_op jit(solution)/shard_map/ppermute | solution.py:13
  76.6 1.7 %collective-permute-done.7 = bf16[2,3,2,16,640]{4,3,2,1,0:T(8,128)(2,1)S(1)} collective-permute-done((bf16[2,3,2,16,640]{4,3,2,1,0:T(8,128)(2,1)S(1)}, bf16[2,3,2,16,640]{4,3,2,1,0:T(8,128)(2,1)S(1)}, u32[]{:S(2)}, u32[]{:S(2)}) %collective-permute-start.7) | collective-permute-done | bytes 245792 | tf_op jit(solution)/shard_map/ppermute | solution.py:13
  78.4 2.3 %collective-permute-start.8 = (bf16[3,2,16,640]{3,2,1,0:T(8,128)(2,1)S(1)}, bf16[3,2,16,640]{3,2,1,0:T(8,128)(2,1)S(1)}, u32[]{:S(2)}, u32[]{:S(2)}) collective-permute-start(bf16[3,2,16,640]{3,2,1,0:T(8,128)(2,1)S(1)} %fusion.19), channel_id=1, source_target_pairs={{0,48},{48,0},{1,49},{49,1},{2,50},{50,2},{3,51},{51,3},{4,52},{52... | collective-permute-start | bytes 368648 | tf_op jit(solution)/shard_map/ppermute | solution.py:13
  80.9 0.6 fusion.7
  81.6 5.8 %collective-permute-start.4 = (bf16[2,3,16,640]{3,2,1,0:T(8,128)(2,1)S(1)}, bf16[2,3,16,640]{3,2,1,0:T(8,128)(2,1)S(1)}, u32[]{:S(2)}, u32[]{:S(2)}) collective-permute-start(bf16[2,3,16,640]{3,2,1,0:T(8,128)(2,1)S(1)} %fusion.18), channel_id=1, source_target_pairs={{0,4},{4,0},{1,5},{5,1},{2,6},{6,2},{3,7},{7,3},{8,12},{12,8},{9,1... | collective-permute-start | bytes 368648 | tf_op jit(solution)/shard_map/ppermute | solution.py:13
  87.4 0.7 all_to_all.16
  88.1 4.9 %all-to-all-start.2 = ((f32[8,1,32]{2,1,0:T(1,128)}), f32[8,1,32]{2,1,0:T(1,128)S(1)}, u32[]{:S(2)}, u32[]{:S(2)}) async-start(f32[8,1,32]{2,1,0:T(1,128)} %all_to_all.16), calls=%async_computation.2 | async-start | bytes 8192 | tf_op jit(solution)/shard_map/all_to_all | solution.py:107
  93.1 1.9 %collective-permute-start.9 = (bf16[3,16,640]{2,1,0:T(8,128)(2,1)S(1)}, bf16[3,16,640]{2,1,0:T(8,128)(2,1)S(1)}, u32[]{:S(2)}, u32[]{:S(2)}) collective-permute-start(bf16[3,16,640]{2,1,0:T(8,128)(2,1)S(1)} %fusion.23), channel_id=1, source_target_pairs={{0,4},{4,0},{1,5},{5,1},{2,6},{6,2},{3,7},{7,3},{8,12},{12,8},{9,1... | collective-permute-start | bytes 184328 | tf_op jit(solution)/shard_map/ppermute | solution.py:13
  95.1 4.0 %collective-permute-start.5 = (bf16[3,16,640]{2,1,0:T(8,128)(2,1)S(1)}, bf16[3,16,640]{2,1,0:T(8,128)(2,1)S(1)}, u32[]{:S(2)}, u32[]{:S(2)}) collective-permute-start(bf16[3,16,640]{2,1,0:T(8,128)(2,1)S(1)} %fusion.22), channel_id=1, source_target_pairs={{0,48},{48,0},{1,49},{49,1},{2,50},{50,2},{3,51},{51,3},{4,52},{52... | collective-permute-start | bytes 184328 | tf_op jit(solution)/shard_map/ppermute | solution.py:13
  99.1 2.8 %collective-permute-done.5 = bf16[3,16,640]{2,1,0:T(8,128)(2,1)S(1)} collective-permute-done((bf16[3,16,640]{2,1,0:T(8,128)(2,1)S(1)}, bf16[3,16,640]{2,1,0:T(8,128)(2,1)S(1)}, u32[]{:S(2)}, u32[]{:S(2)}) %collective-permute-start.5) | collective-permute-done | bytes 61472 | tf_op jit(solution)/shard_map/ppermute | solution.py:13
  101.9 0.7 pad_maximum_fusion.3
  102.6 15.3 %all-to-all-start.1 = ((bf16[6,8,1280]{2,1,0:T(8,128)(2,1)}), bf16[6,8,1280]{2,1,0:T(8,128)(2,1)S(1)}, u32[]{:S(2)}, u32[]{:S(2)}) async-start(bf16[6,8,1280]{2,1,0:T(8,128)(2,1)} %pad_maximum_fusion.3), calls=%async_computation.1 | async-start | bytes 245760 | tf_op jit(solution)/shard_map/all_to_all | solution.py:113
  117.9 0.9 pad_maximum_fusion.2
  119.4 0.7 reduce.3
  120.7 5.0 %all-to-all-done.1 = bf16[6,8,1280]{2,1,0:T(8,128)(2,1)S(1)} async-done(((bf16[6,8,1280]{2,1,0:T(8,128)(2,1)}), bf16[6,8,1280]{2,1,0:T(8,128)(2,1)S(1)}, u32[]{:S(2)}, u32[]{:S(2)}) %all-to-all-start.1) | async-done | bytes 122912 | tf_op jit(solution)/shard_map/all_to_all | solution.py:113
  125.7 0.6 maximum_bitcast_fusion
  (47 shorter events, 3.4 us)
Async XLA Ops:
  5.1 14.1 %copy-start = (bf16[256,1536]{1,0:T(8,128)(2,1)S(1)}, bf16[256,1536]{1,0:T(8,128)(2,1)}, u32[]{:S(2)}) copy-start(bf16[256,1536]{1,0:T(8,128)(2,1)} %param.8) | copy-start | bytes 2359300
  5.1 16.6 %copy-start.2 = (s32[8]{0:T(128)S(1)}, s32[8]{0:T(128)}, u32[]{:S(2)}) copy-start(s32[8]{0:T(128)} %param.7) | copy-start | bytes 100
  5.1 46.4 %all-to-all-start = ((bf16[16,32,1280]{2,1,0:T(8,128)(2,1)}), bf16[16,32,1280]{2,1,0:T(8,128)(2,1)S(1)}, u32[]{:S(2)}, u32[]{:S(2)}) async-start(bf16[16,32,1280]{2,1,0:T(8,128)(2,1)} %bitcast.3), calls=%async_computation | async-start | bytes 2621440 | tf_op jit(solution)/shard_map/all_to_all | solution.py:63
  19.5 3.6 %collective-permute-start = (bf16[8,32,768]{2,1,0:T(8,128)(2,1)S(1)}, bf16[8,32,768]{2,1,0:T(8,128)(2,1)S(1)}, u32[]{:S(2)}, u32[]{:S(2)}) collective-permute-start(bf16[8,32,768]{2,1,0:T(8,128)(2,1)S(1)} %bitcast.93), channel_id=1, source_target_pairs={{0,1},{1,0},{2,3},{3,2},{4,5},{5,4},{6,7},{7,6},{8,9},{9,8},{10,11... | collective-permute-start | bytes 1179656 | tf_op jit(solution)/shard_map/ppermute | solution.py:13
  53.8 8.5 %copy-start.3 = (bf16[1,768,2560]{2,1,0:T(8,128)(2,1)S(1)}, bf16[1,768,2560]{2,1,0:T(8,128)(2,1)}, u32[]{:S(2)}) copy-start(bf16[1,768,2560]{2,1,0:T(8,128)(2,1)} %param.9) | copy-start | bytes 11796484
  54.4 14.6 %collective-permute-start.6 = (bf16[2,3,2,2,16,640]{5,4,3,2,1,0:T(8,128)(2,1)S(1)}, bf16[2,3,2,2,16,640]{5,4,3,2,1,0:T(8,128)(2,1)S(1)}, u32[]{:S(2)}, u32[]{:S(2)}) collective-permute-start(bf16[2,3,2,2,16,640]{5,4,3,2,1,0:T(8,128)(2,1)S(1)} %fusion.15), channel_id=1, source_target_pairs={{0,24},{24,0},{1,25},{25,1},{2,26},{26,2},{3,27},{27,3},{4,28},{28... | collective-permute-start | bytes 1474568 | tf_op jit(solution)/shard_map/ppermute | solution.py:13
  58.4 15.0 %collective-permute-start.2 = (bf16[2,2,3,2,16,640]{5,4,3,2,1,0:T(8,128)(2,1)S(1)}, bf16[2,2,3,2,16,640]{5,4,3,2,1,0:T(8,128)(2,1)S(1)}, u32[]{:S(2)}, u32[]{:S(2)}) collective-permute-start(bf16[2,2,3,2,16,640]{5,4,3,2,1,0:T(8,128)(2,1)S(1)} %fusion.14), channel_id=1, source_target_pairs={{0,2},{2,0},{1,3},{3,1},{4,6},{6,4},{5,7},{7,5},{8,10},{10,8},{9,1... | collective-permute-start | bytes 1474568 | tf_op jit(solution)/shard_map/ppermute | solution.py:13
  63.7 17.1 %collective-permute-start.1 = (f32[8,32,768]{2,1,0:T(8,128)S(1)}, f32[8,32,768]{2,1,0:T(8,128)S(1)}, u32[]{:S(2)}, u32[]{:S(2)}) collective-permute-start(f32[8,32,768]{2,1,0:T(8,128)S(1)} %dynamic-slice_bitcast_fusion), channel_id=1, source_target_pairs={{0,1},{1,0},{2,3},{3,2},{4,5},{5,4},{6,7},{7,6},{8,9},{9,8},{10,11... | collective-permute-start | bytes 2359304 | tf_op jit(solution)/shard_map/ppermute | solution.py:13
  69.2 9.1 %collective-permute-start.7 = (bf16[2,3,2,16,640]{4,3,2,1,0:T(8,128)(2,1)S(1)}, bf16[2,3,2,16,640]{4,3,2,1,0:T(8,128)(2,1)S(1)}, u32[]{:S(2)}, u32[]{:S(2)}) collective-permute-start(bf16[2,3,2,16,640]{4,3,2,1,0:T(8,128)(2,1)S(1)} %fusion.17), channel_id=1, source_target_pairs={{0,2},{2,0},{1,3},{3,1},{4,6},{6,4},{5,7},{7,5},{8,10},{10,8},{9,1... | collective-permute-start | bytes 737288 | tf_op jit(solution)/shard_map/ppermute | solution.py:13
  73.5 8.0 %collective-permute-start.3 = (bf16[2,3,2,16,640]{4,3,2,1,0:T(8,128)(2,1)S(1)}, bf16[2,3,2,16,640]{4,3,2,1,0:T(8,128)(2,1)S(1)}, u32[]{:S(2)}, u32[]{:S(2)}) collective-permute-start(bf16[2,3,2,16,640]{4,3,2,1,0:T(8,128)(2,1)S(1)} %fusion.16), channel_id=1, source_target_pairs={{0,24},{24,0},{1,25},{25,1},{2,26},{26,2},{3,27},{27,3},{4,28},{28... | collective-permute-start | bytes 737288 | tf_op jit(solution)/shard_map/ppermute | solution.py:13
  78.4 14.6 %collective-permute-start.8 = (bf16[3,2,16,640]{3,2,1,0:T(8,128)(2,1)S(1)}, bf16[3,2,16,640]{3,2,1,0:T(8,128)(2,1)S(1)}, u32[]{:S(2)}, u32[]{:S(2)}) collective-permute-start(bf16[3,2,16,640]{3,2,1,0:T(8,128)(2,1)S(1)} %fusion.19), channel_id=1, source_target_pairs={{0,48},{48,0},{1,49},{49,1},{2,50},{50,2},{3,51},{51,3},{4,52},{52... | collective-permute-start | bytes 368648 | tf_op jit(solution)/shard_map/ppermute | solution.py:13
  81.6 13.4 %collective-permute-start.4 = (bf16[2,3,16,640]{3,2,1,0:T(8,128)(2,1)S(1)}, bf16[2,3,16,640]{3,2,1,0:T(8,128)(2,1)S(1)}, u32[]{:S(2)}, u32[]{:S(2)}) collective-permute-start(bf16[2,3,16,640]{3,2,1,0:T(8,128)(2,1)S(1)} %fusion.18), channel_id=1, source_target_pairs={{0,4},{4,0},{1,5},{5,1},{2,6},{6,2},{3,7},{7,3},{8,12},{12,8},{9,1... | collective-permute-start | bytes 368648 | tf_op jit(solution)/shard_map/ppermute | solution.py:13
  88.1 14.5 %all-to-all-start.2 = ((f32[8,1,32]{2,1,0:T(1,128)}), f32[8,1,32]{2,1,0:T(1,128)S(1)}, u32[]{:S(2)}, u32[]{:S(2)}) async-start(f32[8,1,32]{2,1,0:T(1,128)} %all_to_all.16), calls=%async_computation.2 | async-start | bytes 8192 | tf_op jit(solution)/shard_map/all_to_all | solution.py:107
  93.1 27.0 %copy-start.1 = (f32[256]{0:T(256)S(1)}, f32[256]{0:T(256)}, u32[]{:S(2)}) copy-start(f32[256]{0:T(256)} %param.6) | copy-start | bytes 3076
  93.1 6.0 %collective-permute-start.9 = (bf16[3,16,640]{2,1,0:T(8,128)(2,1)S(1)}, bf16[3,16,640]{2,1,0:T(8,128)(2,1)S(1)}, u32[]{:S(2)}, u32[]{:S(2)}) collective-permute-start(bf16[3,16,640]{2,1,0:T(8,128)(2,1)S(1)} %fusion.23), channel_id=1, source_target_pairs={{0,4},{4,0},{1,5},{5,1},{2,6},{6,2},{3,7},{7,3},{8,12},{12,8},{9,1... | collective-permute-start | bytes 184328 | tf_op jit(solution)/shard_map/ppermute | solution.py:13
  95.1 6.8 %collective-permute-start.5 = (bf16[3,16,640]{2,1,0:T(8,128)(2,1)S(1)}, bf16[3,16,640]{2,1,0:T(8,128)(2,1)S(1)}, u32[]{:S(2)}, u32[]{:S(2)}) collective-permute-start(bf16[3,16,640]{2,1,0:T(8,128)(2,1)S(1)} %fusion.22), channel_id=1, source_target_pairs={{0,48},{48,0},{1,49},{49,1},{2,50},{50,2},{3,51},{51,3},{4,52},{52... | collective-permute-start | bytes 184328 | tf_op jit(solution)/shard_map/ppermute | solution.py:13
  102.6 23.1 %all-to-all-start.1 = ((bf16[6,8,1280]{2,1,0:T(8,128)(2,1)}), bf16[6,8,1280]{2,1,0:T(8,128)(2,1)S(1)}, u32[]{:S(2)}, u32[]{:S(2)}) async-start(bf16[6,8,1280]{2,1,0:T(8,128)(2,1)} %pad_maximum_fusion.3), calls=%async_computation.1 | async-start | bytes 245760 | tf_op jit(solution)/shard_map/all_to_all | solution.py:113

commit v3 on v2

v3 whole, which is shorter than its diff:
```python
import jax
import jax.numpy as jnp
from jax import lax
from jax.experimental import pallas as pl
from jax.experimental.pallas import tpu as pltpu
from jax.sharding import Mesh, PartitionSpec as P

EXPERT = ("yh", "x")
EDATA = ("y1", "y0", "zc", "z1", "z0", "core")
DEVICE = EXPERT + EDATA
CUBE = ("y1", "y0", "z1", "z0", "core")
STAGES = (("z0", "y0"), ("y0", "z0"), ("z1", "y1"), ("y1", "z1"))


def swap(value, axis):
    return lax.ppermute(value, axis, [(0, 1), (1, 0)])


def pick(value, index, axis):
    return lax.dynamic_index_in_dim(value, index, axis, keepdims=False)


def stage_pairs(stage):
    pairs = []
    for source in range(32):
        axis = STAGES[stage][source % 2]
        pairs.append((source, source ^ (16 >> CUBE.index(axis))))
    return pairs


def block_order(cube_count):
    block = jnp.arange(16 * cube_count, dtype=jnp.int32)
    cube = block % cube_count
    orders = []
    for core in range(2):
        place = {}
        for stage in range(4):
            axis = STAGES[stage][core]
            place[axis] = lax.axis_index(axis) ^ (block // cube_count // (8 >> stage) % 2)
        orders.append(
            (((place["y1"] * 2 + place["y0"]) * cube_count + cube) * 2 + place["z1"]) * 2 + place["z0"]
        )
    return jnp.where(lax.axis_index("core") == 0, orders[0], orders[1]).astype(jnp.int32)


def reorder_kernel(order_ref, source_ref, out_ref):
    count = order_ref.shape[0]
    unit = source_ref.shape[0] // count
    for block in range(count):
        start = pl.multiple_of(order_ref[block] * unit, unit)
        out_ref[block * unit : (block + 1) * unit, :] = source_ref[pl.ds(start, unit), :]


def reorder(source, order):
    return pl.pallas_call(
        reorder_kernel,
        out_shape=jax.ShapeDtypeStruct(source.shape, source.dtype),
        in_specs=[pl.BlockSpec(memory_space=pltpu.SMEM), pl.BlockSpec(memory_space=pltpu.VMEM)],
        out_specs=pl.BlockSpec(memory_space=pltpu.VMEM),
        compiler_params=pltpu.CompilerParams(vmem_limit_bytes=16 * 2**20),
        cost_estimate=pl.CostEstimate(flops=0, bytes_accessed=2 * 2 * source.size, transcendentals=0),
    )(order, source)


def scale_kernel(counts_ref, route_ref, grad_ref, out_ref):
    step = pl.program_id(0)
    blocks, _, capacity, half = out_ref.shape
    slots = route_ref.shape[1]
    slot = lax.broadcasted_iota(jnp.int32, (capacity, slots), 1)
    row = lax.broadcasted_iota(jnp.int32, (capacity, slots), 0)
    for block in range(blocks):
        expert = step * blocks + block
        own = (slot == row + expert * capacity) & (row < counts_ref[expert])
        slot_weight = jnp.sum(jnp.where(own, route_ref[...], 0.0), axis=1, keepdims=True)
        rows = grad_ref[block * capacity : (block + 1) * capacity, :].astype(jnp.float32) * slot_weight
        rows = rows.astype(jnp.bfloat16)
        out_ref[block, 0] = rows[:, :half]
        out_ref[block, 1] = rows[:, half:]


def scale(counts, route_weight, grad_out):
    row_total, feature_count = grad_out.shape
    expert_count = counts.shape[0]
    capacity = row_total // expert_count
    half = feature_count // 2
    blocks = 2
    return pl.pallas_call(
        scale_kernel,
        grid=(expert_count // blocks,),
        out_shape=jax.ShapeDtypeStruct((expert_count, 2, capacity, half), jnp.bfloat16),
        in_specs=[
            pl.BlockSpec(memory_space=pltpu.SMEM),
            pl.BlockSpec((1, row_total), lambda step: (0, 0)),
            pl.BlockSpec((blocks * capacity, feature_count), lambda step: (step, 0)),
        ],
        out_specs=pl.BlockSpec((blocks, 2, capacity, half), lambda step: (step, 0, 0, 0)),
        compiler_params=pltpu.CompilerParams(vmem_limit_bytes=16 * 2**20),
        cost_estimate=pl.CostEstimate(
            flops=grad_out.size, bytes_accessed=4 * grad_out.size, transcendentals=0
        ),
    )(counts, route_weight.reshape(1, row_total), grad_out)


def body(grad_out, route_weight, counts, preact, down_weight):
    row_total, feature_count = grad_out.shape
    expert_count = lax.axis_size(EXPERT)
    capacity = row_total // expert_count
    hidden_count = down_weight.shape[1]
    half = feature_count // 2
    replica_count = lax.axis_size(EDATA)
    core = lax.axis_index("core")
    cube_count = lax.axis_size("zc")

    outgoing = scale(counts, route_weight, grad_out)
    arrived = lax.all_to_all(
        outgoing.reshape(expert_count * 2, capacity, half),
        EXPERT + ("core",), split_axis=0, concat_axis=0, tiled=True,
    ).reshape(expert_count, 2, capacity, half)

    gate_value = preact[:, :hidden_count].astype(jnp.float32)
    up_value = preact[:, hidden_count:].astype(jnp.float32)
    sigmoid_gate = jax.nn.sigmoid(gate_value)
    silu_gate = gate_value * sigmoid_gate
    hidden_act = (silu_gate * up_value).astype(jnp.bfloat16)
    hidden_blocks = hidden_act.reshape(expert_count, capacity, hidden_count)
    other_blocks = swap(hidden_blocks, "core")
    first_core = core == 0
    hidden_all = jnp.stack(
        [
            jnp.where(first_core, hidden_blocks, other_blocks),
            jnp.where(first_core, other_blocks, hidden_blocks),
        ],
        axis=1,
    ).reshape(2 * row_total, hidden_count)
    hidden_units = reorder(hidden_all.T, block_order(cube_count))

    def product(units, rows):
        return lax.dot_general(
            units, rows.reshape(2 * row_total, half), (((1,), (0,)), ((), ())),
            preferred_element_type=jnp.float32,
        )

    rows_left = hidden_count // 2
    sent = product(hidden_units[rows_left:], arrived).astype(jnp.bfloat16)
    came = lax.ppermute(sent, CUBE, stage_pairs(0))
    arrived, _ = lax.optimization_barrier((arrived, sent))
    kept = product(hidden_units[:rows_left], arrived)
    came, kept = lax.optimization_barrier((came, kept))

    weight_half = lax.dynamic_slice(
        down_weight[0], (0, core * half), (hidden_count, half)
    )
    grad_partial = lax.dot_general(
        arrived.reshape(2 * row_total, half), weight_half, (((1,), (1,)), ((), ())),
        preferred_element_type=jnp.float32,
    ).reshape(expert_count, 2, capacity, hidden_count)
    grad_other = swap(pick(grad_partial, 1 - core, 1), "core")
    grad_hidden = (pick(grad_partial, core, 1) + grad_other).reshape(row_total, hidden_count)
    grad_gate = grad_hidden * up_value * sigmoid_gate * (1.0 + gate_value * (1.0 - sigmoid_gate))
    grad_up = grad_hidden * silu_gate
    grad_rows = jnp.concatenate([grad_gate, grad_up], axis=1).astype(jnp.bfloat16)
    row_score = jnp.sum(grad_hidden * hidden_act.astype(jnp.float32), axis=1)

    for stage in range(1, 4):
        total = kept + came.astype(jnp.float32)
        rows_left //= 2
        sent = total[rows_left:].astype(jnp.bfloat16)
        kept = total[:rows_left]
        came = lax.ppermute(sent, CUBE, stage_pairs(stage))
        if stage == 1:
            came, row_score = lax.optimization_barrier((came, row_score))
            returned_score = lax.all_to_all(
                row_score.reshape(expert_count, capacity), EXPERT, split_axis=0, concat_axis=0, tiled=True
            )
    slot_index = lax.broadcasted_iota(jnp.int32, (expert_count, capacity), 1)
    live_rows = (slot_index < counts[:, None]).astype(jnp.float32)
    route_grad = live_rows * returned_score / route_weight.reshape(expert_count, capacity)

    spread = (kept + came.astype(jnp.float32)).astype(jnp.bfloat16)
    gathered = lax.all_to_all(
        spread.reshape(cube_count * 2, rows_left // (2 * cube_count), half),
        ("zc", "core"), split_axis=0, concat_axis=0, tiled=True,
    ).reshape(cube_count, 2, rows_left // (2 * cube_count), half)
    total = jnp.sum(gathered.astype(jnp.float32), axis=0) / replica_count
    weight_grad = jnp.concatenate([total[0], total[1]], axis=1)[None]
    return (grad_rows, weight_grad, route_grad.reshape(row_total))


def solution(mesh):
    fine = Mesh(mesh.devices.reshape(2, 4, 2, 2, 3, 2, 2, 2), DEVICE)
    in_specs = (P(DEVICE, None), P(DEVICE), P(DEVICE), P(DEVICE, None), P(EXPERT, None, None))
    out_specs = (P(DEVICE, None), P(EXPERT, EDATA, None), P(DEVICE))
    return jax.shard_map(body, mesh=fine, in_specs=in_specs, out_specs=out_specs, check_vma=False)
```

time: 128 us -> 136 us (1.062); the launches traced: 126 us -> 136 us
  waiting for transfers between devices: 40 us -> 61.6 us
  starting transfers between devices: 68.7 us -> 55.3 us
  Pallas kernels: 0 us -> 3.05 us
    ppermute x10 -> x2, starting transfers between devices: 34.4 us -> 5.31 us  [swap(): return lax.ppermute(value, axis, [(0, 1), (1, 0)])]
    ppermute x0 -> x4, waiting for transfers between devices: none -> 18.3 us  [the longest x3 13.2 us: body(): came = lax.ppermute(sent, CUBE, stage_pairs(stage))]
    ppermute x0 -> x4, starting transfers between devices: none -> 16.7 us  [the longest x3 13 us: body(): came = lax.ppermute(sent, CUBE, stage_pairs(stage))]
    all_to_all x1, waiting for transfers between devices: 0.01 us -> 8.15 us  [body(): lax.all_to_all(row_score.reshape(expert_count, capacity), EXPERT, split_a...]
    ppermute x10 -> x2, waiting for transfers between devices: 8 us -> 1.42 us  [swap(): return lax.ppermute(value, axis, [(0, 1), (1, 0)])]
    pallas_call x0 -> x2, Pallas kernels: none -> 3.05 us  [the longest x1 2.44 us: scale(): pl.pallas_call(scale_kernel, grid=(expert_count // blocks,), out_shape=ja...]
    unnamed x8 -> x14, local copies, waits for them, and re-layouts: 0.02 us -> 2.67 us
    convert_element_type x1 -> x0, other arithmetic: 1.6 us -> none  [body(): scaled_rows = (grad_out.reshape(expert_count, capacity, feature_count) *...]
  transfers between devices with their start and end apart: 13 -> 9, of which waited for: 6 -> 7; matrix products, arithmetic and copies ran while one was open for 6% -> 7% of each run, Pallas kernels for 0% -> 0%
where the time goes in v3:
time: 136 us
  waiting for transfers between devices  61.6 us (45%)
  starting transfers between devices  55.3 us (41%)
  other arithmetic  6.3 us (5%)
  local copies, waits for them, and re-layouts  4.52 us (3%)
  matrix products  4.12 us (3%)
  Pallas kernels  3.05 us (2%)
    all_to_all x1, waiting for transfers between devices, body(): lax.all_to_all(outgoing.reshape(expert_count * 2, capacity, half), EXPERT...  27.3 us
    all_to_all x1, starting transfers between devices, body(): lax.all_to_all(spread.reshape(cube_count * 2, rows_left // (2 * cube_coun...  15.8 us
    all_to_all x1, starting transfers between devices, body(): lax.all_to_all(outgoing.reshape(expert_count * 2, capacity, half), EXPERT...  14.1 us
    ppermute x3, waiting for transfers between devices, body(): came = lax.ppermute(sent, CUBE, stage_pairs(stage))  13.2 us
    ppermute x3, starting transfers between devices, body(): came = lax.ppermute(sent, CUBE, stage_pairs(stage))  13 us
    all_to_all x1, waiting for transfers between devices, body(): lax.all_to_all(row_score.reshape(expert_count, capacity), EXPERT, split_a...  8.15 us
    all_to_all x1, waiting for transfers between devices, body(): lax.all_to_all(spread.reshape(cube_count * 2, rows_left // (2 * cube_coun...  6.44 us
    ppermute x2, starting transfers between devices, swap(): return lax.ppermute(value, axis, [(0, 1), (1, 0)])  5.31 us
  transfers between devices with their start and end apart: 9, of which 7 were waited for; matrix products, arithmetic and copies ran while one was open for 7% of the time, Pallas kernels for 0%

profile of v3, /device:TPU:1, one launch (start us, length us, event | category | flops | bytes accessed | tf_op | source)
XLA Modules:
  0.0 135.9 jit_solution(2329411844594893466)
XLA Ops:
  0.6 1.3 copy-done
  1.9 0.7 copy-done.1
  2.6 0.7 copy-done.3
  3.3 2.4 %shard_map.76 = bf16[8,2,32,1280]{3,2,1,0:T(8,128)(2,1)} custom-call(s32[8]{0:T(128)S(1)} %copy-done.3, f32[1,256]{1,0:T(1,128)S(1)} %bitcast.45, bf16[256,2560]{1,0:T(8,128)(2,1)S(1)} %copy-done), custom_call_target="tpu_custom_call" | custom-call | flops 655360 | bytes 2621440 | tf_op jit(solution)/shard_map/pallas_call | solution.py:87
  5.7 14.1 %all-to-all-start = ((bf16[16,32,1280]{2,1,0:T(8,128)(2,1)}), bf16[16,32,1280]{2,1,0:T(8,128)(2,1)S(1)}, u32[]{:S(2)}, u32[]{:S(2)}) async-start(bf16[16,32,1280]{2,1,0:T(8,128)(2,1)} %bitcast.1), calls=%async_computation | async-start | bytes 2621440 | tf_op jit(solution)/shard_map/all_to_all | solution.py:115
  20.1 2.1 %collective-permute-start = (bf16[8,32,768]{2,1,0:T(8,128)(2,1)S(1)}, bf16[8,32,768]{2,1,0:T(8,128)(2,1)S(1)}, u32[]{:S(2)}, u32[]{:S(2)}) collective-permute-start(bf16[8,32,768]{2,1,0:T(8,128)(2,1)S(1)} %bitcast.50), channel_id=1, source_target_pairs={{0,1},{1,0},{2,3},{3,2},{4,5},{5,4},{6,7},{7,6},{8,9},{9,8},{10,11... | collective-permute-start | bytes 1179656 | tf_op jit(solution)/shard_map/ppermute | solution.py:16
  22.3 1.4 %collective-permute-done = bf16[8,32,768]{2,1,0:T(8,128)(2,1)S(1)} collective-permute-done((bf16[8,32,768]{2,1,0:T(8,128)(2,1)S(1)}, bf16[8,32,768]{2,1,0:T(8,128)(2,1)S(1)}, u32[]{:S(2)}, u32[]{:S(2)}) %collective-permute-start) | collective-permute-done | bytes 393248 | tf_op jit(solution)/shard_map/ppermute | solution.py:16
  24.2 0.6 shard_map.77
  24.9 27.3 %all-to-all-done = bf16[16,32,1280]{2,1,0:T(8,128)(2,1)S(1)} async-done(((bf16[16,32,1280]{2,1,0:T(8,128)(2,1)}), bf16[16,32,1280]{2,1,0:T(8,128)(2,1)S(1)}, u32[]{:S(2)}, u32[]{:S(2)}) %all-to-all-start) | async-done | bytes 1310752 | tf_op jit(solution)/shard_map/all_to_all | solution.py:115
  52.1 0.7 convolution_convert_fusion
  52.8 3.7 %collective-permute-start.2 = (bf16[384,1280]{1,0:T(8,128)(2,1)S(1)}, bf16[384,1280]{1,0:T(8,128)(2,1)}, u32[]{:S(2)}, u32[]{:S(2)}) collective-permute-start(bf16[384,1280]{1,0:T(8,128)(2,1)S(1)} %convolution_convert_fusion), channel_id=1, source_target_pairs={{0,2},{1,25},{2,0},{3,27},{4,6},{5,29},{6,4},{7,31},{24,26},{25,1}... | collective-permute-start | bytes 2949128 | tf_op jit(solution)/shard_map/ppermute | solution.py:145
  56.5 2.8 %fusion = f32[8,2,32,768]{3,2,1,0:T(8,128)S(1)} fusion(bf16[8,2,32,1280]{3,2,1,0:T(8,128)(2,1)S(1)} %bitcast.47, bf16[1,768,2560]{2,1,0:T(8,128)(2,1)} %param.9, s32[]{:T(128)S(6)} %select_n.131), kind=kOutput, calls=%fused_computation.1 | convolution fusion | flops 1006632960 | bytes 4849668 | tf_op jit(solution)/shard_map/dot_general | solution.py:153
  59.4 3.2 %collective-permute-start.1 = (f32[8,32,768]{2,1,0:T(8,128)S(1)}, f32[8,32,768]{2,1,0:T(8,128)S(1)}, u32[]{:S(2)}, u32[]{:S(2)}) collective-permute-start(f32[8,32,768]{2,1,0:T(8,128)S(1)} %dynamic-slice_bitcast_fusion), channel_id=1, source_target_pairs={{0,1},{1,0},{2,3},{3,2},{4,5},{5,4},{6,7},{7,6},{8,9},{9,8},{10,11... | collective-permute-start | bytes 2359304 | tf_op jit(solution)/shard_map/ppermute | solution.py:16
  62.6 0.7 fusion.13
  63.3 5.2 %collective-permute-done.2 = bf16[384,1280]{1,0:T(8,128)(2,1)} collective-permute-done((bf16[384,1280]{1,0:T(8,128)(2,1)S(1)}, bf16[384,1280]{1,0:T(8,128)(2,1)}, u32[]{:S(2)}, u32[]{:S(2)}) %collective-permute-start.2) | collective-permute-done | bytes 983072 | tf_op jit(solution)/shard_map/ppermute | solution.py:145
  68.4 1.4 %convert_add_fusion = f32[384,1280]{1,0:T(8,128)S(1)} fusion(f32[384,1280]{1,0:T(8,128)S(1)} %fusion.13, bf16[384,1280]{1,0:T(8,128)(2,1)} %collective-permute-done.2), kind=kLoop, calls=%fused_computation.3 | loop fusion | flops 983040 | bytes 4915200 | tf_op jit(solution)/shard_map/add | solution.py:165
  69.9 4.1 %collective-permute-start.3 = (bf16[192,1280]{1,0:T(8,128)(2,1)S(1)}, bf16[192,1280]{1,0:T(8,128)(2,1)S(1)}, u32[]{:S(2)}, u32[]{:S(2)}) collective-permute-start(bf16[192,1280]{1,0:T(8,128)(2,1)S(1)} %slice.85), channel_id=1, source_target_pairs={{0,24},{1,3},{2,26},{3,1},{4,28},{5,7},{6,30},{7,5},{24,0},{25,27}... | collective-permute-start | bytes 1474568 | tf_op jit(solution)/shard_map/ppermute | solution.py:169
  74.2 0.6 fusion.6
  74.8 5.7 %collective-permute-done.3 = bf16[192,1280]{1,0:T(8,128)(2,1)S(1)} collective-permute-done((bf16[192,1280]{1,0:T(8,128)(2,1)S(1)}, bf16[192,1280]{1,0:T(8,128)(2,1)S(1)}, u32[]{:S(2)}, u32[]{:S(2)}) %collective-permute-start.3) | collective-permute-done | bytes 491552 | tf_op jit(solution)/shard_map/ppermute | solution.py:169
  80.7 3.3 %collective-permute-start.4 = (bf16[96,1280]{1,0:T(8,128)(2,1)S(1)}, bf16[96,1280]{1,0:T(8,128)(2,1)S(1)}, u32[]{:S(2)}, u32[]{:S(2)}) collective-permute-start(bf16[96,1280]{1,0:T(8,128)(2,1)S(1)} %slice.86), channel_id=1, source_target_pairs={{0,4},{1,49},{2,6},{3,51},{4,0},{5,53},{6,2},{7,55},{24,28},{25,73... | collective-permute-start | bytes 737288 | tf_op jit(solution)/shard_map/ppermute | solution.py:169
  84.0 7.4 %collective-permute-done.4 = bf16[96,1280]{1,0:T(8,128)(2,1)S(1)} collective-permute-done((bf16[96,1280]{1,0:T(8,128)(2,1)S(1)}, bf16[96,1280]{1,0:T(8,128)(2,1)S(1)}, u32[]{:S(2)}, u32[]{:S(2)}) %collective-permute-start.4) | collective-permute-done | bytes 245792 | tf_op jit(solution)/shard_map/ppermute | solution.py:169
  91.5 5.6 %collective-permute-start.5 = (bf16[48,1280]{1,0:T(8,128)(2,1)S(1)}, bf16[48,1280]{1,0:T(8,128)(2,1)S(1)}, u32[]{:S(2)}, u32[]{:S(2)}) collective-permute-start(bf16[48,1280]{1,0:T(8,128)(2,1)S(1)} %slice.87), channel_id=1, source_target_pairs={{0,48},{1,5},{2,50},{3,7},{4,52},{5,1},{6,54},{7,3},{24,72},{25,29... | collective-permute-start | bytes 368648 | tf_op jit(solution)/shard_map/ppermute | solution.py:169
  97.3 0.7 all_to_all.16
  98.0 3.4 %all-to-all-start.2 = ((f32[8,1,32]{2,1,0:T(1,128)}), f32[8,1,32]{2,1,0:T(1,128)S(1)}, u32[]{:S(2)}, u32[]{:S(2)}) async-start(f32[8,1,32]{2,1,0:T(1,128)} %all_to_all.16), calls=%async_computation.2 | async-start | bytes 8192 | tf_op jit(solution)/shard_map/all_to_all | solution.py:172
  101.3 0.7 fusion.17
  102.0 8.2 %all-to-all-done.2 = f32[8,1,32]{2,1,0:T(1,128)S(1)} async-done(((f32[8,1,32]{2,1,0:T(1,128)}), f32[8,1,32]{2,1,0:T(1,128)S(1)}, u32[]{:S(2)}, u32[]{:S(2)}) %all-to-all-start.2) | async-done | bytes 1056 | tf_op jit(solution)/shard_map/all_to_all | solution.py:172
  110.2 15.8 %all-to-all-start.1 = ((bf16[6,8,1280]{2,1,0:T(8,128)(2,1)}), bf16[6,8,1280]{2,1,0:T(8,128)(2,1)S(1)}, u32[]{:S(2)}, u32[]{:S(2)}) async-start(bf16[6,8,1280]{2,1,0:T(8,128)(2,1)} %fusion.17), calls=%async_computation.1 | async-start | bytes 245760 | tf_op jit(solution)/shard_map/all_to_all | solution.py:180
  126.0 0.9 pad_maximum_fusion.1
  127.4 0.7 reduce.3
  128.1 0.6 select_divide_fusion
  128.7 6.4 %all-to-all-done.1 = bf16[6,8,1280]{2,1,0:T(8,128)(2,1)S(1)} async-done(((bf16[6,8,1280]{2,1,0:T(8,128)(2,1)}), bf16[6,8,1280]{2,1,0:T(8,128)(2,1)S(1)}, u32[]{:S(2)}, u32[]{:S(2)}) %all-to-all-start.1) | async-done | bytes 122912 | tf_op jit(solution)/shard_map/all_to_all | solution.py:180
  135.2 0.6 maximum_bitcast_fusion
  (33 shorter events, 2.0 us)
Async XLA Ops:
  0.6 1.3 copy-start
  1.9 0.7 copy-start.1
  2.6 0.7 copy-start.3
  5.7 14.1 %copy-start.5 = (bf16[256,1536]{1,0:T(8,128)(2,1)S(1)}, bf16[256,1536]{1,0:T(8,128)(2,1)}, u32[]{:S(2)}) copy-start(bf16[256,1536]{1,0:T(8,128)(2,1)} %param.8) | copy-start | bytes 2359300
  5.7 46.4 %all-to-all-start = ((bf16[16,32,1280]{2,1,0:T(8,128)(2,1)}), bf16[16,32,1280]{2,1,0:T(8,128)(2,1)S(1)}, u32[]{:S(2)}, u32[]{:S(2)}) async-start(bf16[16,32,1280]{2,1,0:T(8,128)(2,1)} %bitcast.1), calls=%async_computation | async-start | bytes 2621440 | tf_op jit(solution)/shard_map/all_to_all | solution.py:115
  20.1 3.6 %collective-permute-start = (bf16[8,32,768]{2,1,0:T(8,128)(2,1)S(1)}, bf16[8,32,768]{2,1,0:T(8,128)(2,1)S(1)}, u32[]{:S(2)}, u32[]{:S(2)}) collective-permute-start(bf16[8,32,768]{2,1,0:T(8,128)(2,1)S(1)} %bitcast.50), channel_id=1, source_target_pairs={{0,1},{1,0},{2,3},{3,2},{4,5},{5,4},{6,7},{7,6},{8,9},{9,8},{10,11... | collective-permute-start | bytes 1179656 | tf_op jit(solution)/shard_map/ppermute | solution.py:16
  52.8 15.6 %collective-permute-start.2 = (bf16[384,1280]{1,0:T(8,128)(2,1)S(1)}, bf16[384,1280]{1,0:T(8,128)(2,1)}, u32[]{:S(2)}, u32[]{:S(2)}) collective-permute-start(bf16[384,1280]{1,0:T(8,128)(2,1)S(1)} %convolution_convert_fusion), channel_id=1, source_target_pairs={{0,2},{1,25},{2,0},{3,27},{4,6},{5,29},{6,4},{7,31},{24,26},{25,1}... | collective-permute-start | bytes 2949128 | tf_op jit(solution)/shard_map/ppermute | solution.py:145
  59.4 14.6 %collective-permute-start.1 = (f32[8,32,768]{2,1,0:T(8,128)S(1)}, f32[8,32,768]{2,1,0:T(8,128)S(1)}, u32[]{:S(2)}, u32[]{:S(2)}) collective-permute-start(f32[8,32,768]{2,1,0:T(8,128)S(1)} %dynamic-slice_bitcast_fusion), channel_id=1, source_target_pairs={{0,1},{1,0},{2,3},{3,2},{4,5},{5,4},{6,7},{7,6},{8,9},{9,8},{10,11... | collective-permute-start | bytes 2359304 | tf_op jit(solution)/shard_map/ppermute | solution.py:16
  69.8 4.3 %copy-start.6 = (bf16[256,1536]{1,0:T(8,128)(2,1)S(1)}, bf16[256,1536]{1,0:T(8,128)(2,1)}, u32[]{:S(2)}) copy-start(bf16[256,1536]{1,0:T(8,128)(2,1)} %param.8) | copy-start | bytes 2359300
  69.9 10.6 %collective-permute-start.3 = (bf16[192,1280]{1,0:T(8,128)(2,1)S(1)}, bf16[192,1280]{1,0:T(8,128)(2,1)S(1)}, u32[]{:S(2)}, u32[]{:S(2)}) collective-permute-start(bf16[192,1280]{1,0:T(8,128)(2,1)S(1)} %slice.85), channel_id=1, source_target_pairs={{0,24},{1,3},{2,26},{3,1},{4,28},{5,7},{6,30},{7,5},{24,0},{25,27}... | collective-permute-start | bytes 1474568 | tf_op jit(solution)/shard_map/ppermute | solution.py:169
  80.6 16.5 %copy-start.4 = (s32[8]{0:T(128)S(1)}, s32[8]{0:T(128)}, u32[]{:S(2)}) copy-start(s32[8]{0:T(128)} %counts_ref.1) | copy-start | bytes 100
  80.7 10.8 %collective-permute-start.4 = (bf16[96,1280]{1,0:T(8,128)(2,1)S(1)}, bf16[96,1280]{1,0:T(8,128)(2,1)S(1)}, u32[]{:S(2)}, u32[]{:S(2)}) collective-permute-start(bf16[96,1280]{1,0:T(8,128)(2,1)S(1)} %slice.86), channel_id=1, source_target_pairs={{0,4},{1,49},{2,6},{3,51},{4,0},{5,53},{6,2},{7,55},{24,28},{25,73... | collective-permute-start | bytes 737288 | tf_op jit(solution)/shard_map/ppermute | solution.py:169
  91.5 36.6 %copy-start.2 = (f32[256]{0:T(256)S(1)}, f32[256]{0:T(256)}, u32[]{:S(2)}) copy-start(f32[256]{0:T(256)} %param.6) | copy-start | bytes 3076
  91.5 9.8 %collective-permute-start.5 = (bf16[48,1280]{1,0:T(8,128)(2,1)S(1)}, bf16[48,1280]{1,0:T(8,128)(2,1)S(1)}, u32[]{:S(2)}, u32[]{:S(2)}) collective-permute-start(bf16[48,1280]{1,0:T(8,128)(2,1)S(1)} %slice.87), channel_id=1, source_target_pairs={{0,48},{1,5},{2,50},{3,7},{4,52},{5,1},{6,54},{7,3},{24,72},{25,29... | collective-permute-start | bytes 368648 | tf_op jit(solution)/shard_map/ppermute | solution.py:169
  98.0 12.2 %all-to-all-start.2 = ((f32[8,1,32]{2,1,0:T(1,128)}), f32[8,1,32]{2,1,0:T(1,128)S(1)}, u32[]{:S(2)}, u32[]{:S(2)}) async-start(f32[8,1,32]{2,1,0:T(1,128)} %all_to_all.16), calls=%async_computation.2 | async-start | bytes 8192 | tf_op jit(solution)/shard_map/all_to_all | solution.py:172
  110.2 25.0 %all-to-all-start.1 = ((bf16[6,8,1280]{2,1,0:T(8,128)(2,1)}), bf16[6,8,1280]{2,1,0:T(8,128)(2,1)S(1)}, u32[]{:S(2)}, u32[]{:S(2)}) async-start(bf16[6,8,1280]{2,1,0:T(8,128)(2,1)} %fusion.17), calls=%async_computation.1 | async-start | bytes 245760 | tf_op jit(solution)/shard_map/all_to_all | solution.py:180

commit v4 on v3

--- a/solution.py
+++ b/solution.py
@@ -9,7 +9,8 @@
 EDATA = ("y1", "y0", "zc", "z1", "z0", "core")
 DEVICE = EXPERT + EDATA
 CUBE = ("y1", "y0", "z1", "z0", "core")
-STAGES = (("z0", "y0"), ("y0", "z0"), ("z1", "y1"), ("y1", "z1"))
+STAGES = (("z0", "y0"), ("y0", "z0"))
+REST = ("y1", "zc", "z1", "core")
 
 
 def swap(value, axis):
@@ -29,16 +30,17 @@
 
 
 def block_order(cube_count):
-    block = jnp.arange(16 * cube_count, dtype=jnp.int32)
-    cube = block % cube_count
+    rest = 4 * cube_count
+    block = jnp.arange(4 * rest, dtype=jnp.int32)
+    place_y1, place_cube, place_z1 = block % rest // (rest // 2), block % (rest // 2) // 2, block % 2
     orders = []
     for core in range(2):
         place = {}
-        for stage in range(4):
+        for stage in range(2):
             axis = STAGES[stage][core]
-            place[axis] = lax.axis_index(axis) ^ (block // cube_count // (8 >> stage) % 2)
+            place[axis] = lax.axis_index(axis) ^ (block // rest // (2 >> stage) % 2)
         orders.append(
-            (((place["y1"] * 2 + place["y0"]) * cube_count + cube) * 2 + place["z1"]) * 2 + place["z0"]
+            (((place_y1 * 2 + place["y0"]) * cube_count + place_cube) * 2 + place_z1) * 2 + place["z0"]
         )
     return jnp.where(lax.axis_index("core") == 0, orders[0], orders[1]).astype(jnp.int32)
 
@@ -94,7 +96,7 @@
             pl.BlockSpec((blocks * capacity, feature_count), lambda step: (step, 0)),
         ],
         out_specs=pl.BlockSpec((blocks, 2, capacity, half), lambda step: (step, 0, 0, 0)),
-        compiler_params=pltpu.CompilerParams(vmem_limit_bytes=16 * 2**20),
+        compiler_params=pltpu.CompilerParams(vmem_limit_bytes=60 * 2**20),
         cost_estimate=pl.CostEstimate(
             flops=grad_out.size, bytes_accessed=4 * grad_out.size, transcendentals=0
         ),
@@ -145,7 +147,6 @@
     came = lax.ppermute(sent, CUBE, stage_pairs(0))
     arrived, _ = lax.optimization_barrier((arrived, sent))
     kept = product(hidden_units[:rows_left], arrived)
-    came, kept = lax.optimization_barrier((came, kept))
 
     weight_half = lax.dynamic_slice(
         down_weight[0], (0, core * half), (hidden_count, half)
@@ -161,26 +162,25 @@
     grad_rows = jnp.concatenate([grad_gate, grad_up], axis=1).astype(jnp.bfloat16)
     row_score = jnp.sum(grad_hidden * hidden_act.astype(jnp.float32), axis=1)
 
-    for stage in range(1, 4):
-        total = kept + came.astype(jnp.float32)
-        rows_left //= 2
-        sent = total[rows_left:].astype(jnp.bfloat16)
-        kept = total[:rows_left]
-        came = lax.ppermute(sent, CUBE, stage_pairs(stage))
-        if stage == 1:
-            came, row_score = lax.optimization_barrier((came, row_score))
-            returned_score = lax.all_to_all(
-                row_score.reshape(expert_count, capacity), EXPERT, split_axis=0, concat_axis=0, tiled=True
-            )
+    came, kept = lax.optimization_barrier((came, kept))
+    total = kept + came.astype(jnp.float32)
+    rows_left //= 2
+    sent = total[rows_left:].astype(jnp.bfloat16)
+    kept = total[:rows_left]
+    came = lax.ppermute(sent, CUBE, stage_pairs(1))
+    came, row_score = lax.optimization_barrier((came, row_score))
+    spread = (kept + came.astype(jnp.float32)).astype(jnp.bfloat16)
+    unit = rows_left // lax.axis_size(REST)
+    spread, row_score = lax.optimization_barrier((spread, row_score))
+    gathered = lax.all_to_all(
+        spread.reshape(-1, unit, half), REST, split_axis=0, concat_axis=0, tiled=True
+    ).reshape(-1, 2, unit, half)
+    all_scores = lax.all_gather(row_score.reshape(expert_count, capacity), EXPERT)
+    returned_score = pick(all_scores, lax.axis_index(EXPERT), 1)
     slot_index = lax.broadcasted_iota(jnp.int32, (expert_count, capacity), 1)
     live_rows = (slot_index < counts[:, None]).astype(jnp.float32)
     route_grad = live_rows * returned_score / route_weight.reshape(expert_count, capacity)
 
-    spread = (kept + came.astype(jnp.float32)).astype(jnp.bfloat16)
-    gathered = lax.all_to_all(
-        spread.reshape(cube_count * 2, rows_left // (2 * cube_count), half),
-        ("zc", "core"), split_axis=0, concat_axis=0, tiled=True,
-    ).reshape(cube_count, 2, rows_left // (2 * cube_count), half)
     total = jnp.sum(gathered.astype(jnp.float32), axis=0) / replica_count
     weight_grad = jnp.concatenate([total[0], total[1]], axis=1)[None]
     return (grad_rows, weight_grad, route_grad.reshape(row_total))

time: 136 us -> 144 us (1.059)
  the two profiles are of different devices: /device:TPU:1 before, /device:TPU:16 now
where the time goes in v4:
time: 144 us; the launch traced here: 143 us
  starting transfers between devices  48.5 us (34%)
  blocking collectives  44.2 us (31%)
  waiting for transfers between devices  33.2 us (23%)
  matrix products  5.06 us (4%)
  other arithmetic  4.54 us (3%)
  Pallas kernels  4.34 us (3%)
  local copies, waits for them, and re-layouts  2.75 us (2%)
    all_gather x1, blocking collectives, body(): lax.all_gather(row_score.reshape(expert_count, capacity), EXPERT)  44.2 us
    ppermute x1, starting transfers between devices, body(): came = lax.ppermute(sent, CUBE, stage_pairs(0))  17.4 us
    all_to_all x1, waiting for transfers between devices, body(): lax.all_to_all(outgoing.reshape(expert_count * 2, capacity, half), EXPERT...  17 us
    all_to_all x1, starting transfers between devices, body(): lax.all_to_all(spread.reshape(-1, unit, half), REST, split_axis=0, concat...  16.8 us
    ppermute x1, waiting for transfers between devices, body(): came = lax.ppermute(sent, CUBE, stage_pairs(1))  8.02 us
    all_to_all x1, starting transfers between devices, body(): lax.all_to_all(outgoing.reshape(expert_count * 2, capacity, half), EXPERT...  8 us
    ppermute x1, waiting for transfers between devices, body(): came = lax.ppermute(sent, CUBE, stage_pairs(0))  6.83 us
    ppermute x2, starting transfers between devices, swap(): return lax.ppermute(value, axis, [(0, 1), (1, 0)])  4.23 us
  transfers between devices with their start and end apart: 6, of which 4 were waited for; matrix products, arithmetic and copies ran while one was open for 6% of the time, Pallas kernels for 0%

profile of v4, /device:TPU:16, one launch (start us, length us, event | category | flops | bytes accessed | tf_op | source)
XLA Modules:
  0.0 143.4 jit_solution(7312890779575100186)
XLA Ops:
  0.6 3.7 %shard_map.76 = bf16[8,2,32,1280]{3,2,1,0:T(8,128)(2,1)} custom-call(s32[8]{0:T(128)} %counts_ref.1, f32[1,256]{1,0:T(1,128)} %bitcast.52, bf16[256,2560]{1,0:T(8,128)(2,1)} %grad_ref.1), custom_call_target="tpu_custom_call" | custom-call | flops 655360 | bytes 2621440 | tf_op jit(solution)/shard_map/pallas_call | solution.py:89
  4.4 8.0 %all-to-all-start = ((bf16[16,32,1280]{2,1,0:T(8,128)(2,1)}), bf16[16,32,1280]{2,1,0:T(8,128)(2,1)S(1)}, u32[]{:S(2)}, u32[]{:S(2)}) async-start(bf16[16,32,1280]{2,1,0:T(8,128)(2,1)} %bitcast.47), calls=%async_computation | async-start | bytes 2621440 | tf_op jit(solution)/shard_map/all_to_all | solution.py:117
  12.4 0.3 fusion.4
  12.6 2.3 %collective-permute-start = (bf16[8,32,768]{2,1,0:T(8,128)(2,1)S(1)}, bf16[8,32,768]{2,1,0:T(8,128)(2,1)S(1)}, u32[]{:S(2)}, u32[]{:S(2)}) collective-permute-start(bf16[8,32,768]{2,1,0:T(8,128)(2,1)S(1)} %bitcast.50), channel_id=1, source_target_pairs={{0,1},{1,0},{2,3},{3,2},{4,5},{5,4},{6,7},{7,6},{8,9},{9,8},{10,11... | collective-permute-start | bytes 1179656 | tf_op jit(solution)/shard_map/ppermute | solution.py:17
  15.0 1.3 collective-permute-done
  16.3 0.1 pad_maximum_fusion
  16.4 0.9 copy.14
  17.4 1.4 copy.15
  18.8 0.6 shard_map.77
  19.4 17.0 %all-to-all-done = bf16[16,32,1280]{2,1,0:T(8,128)(2,1)S(1)} async-done(((bf16[16,32,1280]{2,1,0:T(8,128)(2,1)}), bf16[16,32,1280]{2,1,0:T(8,128)(2,1)S(1)}, u32[]{:S(2)}, u32[]{:S(2)}) %all-to-all-start) | async-done | bytes 1310752 | tf_op jit(solution)/shard_map/all_to_all | solution.py:117
  36.4 1.6 %convolution_convert_fusion = bf16[384,1280]{1,0:T(8,128)(2,1)} fusion(bf16[512,1280]{1,0:T(8,128)(2,1)S(1)} %bitcast.44, bf16[768,512]{1,0:T(8,128)(2,1)S(1)} %shard_map.77), kind=kOutput, calls=%fused_computation | convolution fusion | flops 503808000 | bytes 2686976 | tf_op jit(solution)/shard_map/dot_general | solution.py:140
  38.1 17.4 %collective-permute-start.2 = (bf16[384,1280]{1,0:T(8,128)(2,1)}, bf16[384,1280]{1,0:T(8,128)(2,1)S(1)}, u32[]{:S(2)}, u32[]{:S(2)}) collective-permute-start(bf16[384,1280]{1,0:T(8,128)(2,1)} %convolution_convert_fusion), channel_id=1, source_target_pairs={{0,2},{1,25},{2,0},{3,27},{4,6},{5,29},{6,4},{7,31},{24,26},{25,1}... | collective-permute-start | bytes 2949128 | tf_op jit(solution)/shard_map/ppermute | solution.py:147
  55.5 2.8 %fusion = f32[8,2,32,768]{3,2,1,0:T(8,128)S(1)} fusion(bf16[8,2,32,1280]{3,2,1,0:T(8,128)(2,1)S(1)} %bitcast.45, bf16[1,768,2560]{2,1,0:T(8,128)(2,1)} %param.9, s32[]{:T(128)S(6)} %select_n.117), kind=kOutput, calls=%fused_computation.1 | convolution fusion | flops 1006632960 | bytes 4849668 | tf_op jit(solution)/shard_map/dot_general | solution.py:154
  58.3 1.9 %collective-permute-start.1 = (f32[8,32,768]{2,1,0:T(8,128)S(1)}, f32[8,32,768]{2,1,0:T(8,128)S(1)}, u32[]{:S(2)}, u32[]{:S(2)}) collective-permute-start(f32[8,32,768]{2,1,0:T(8,128)S(1)} %dynamic-slice_bitcast_fusion), channel_id=1, source_target_pairs={{0,1},{1,0},{2,3},{3,2},{4,5},{5,4},{6,7},{7,6},{8,9},{9,8},{10,11... | collective-permute-start | bytes 2359304 | tf_op jit(solution)/shard_map/ppermute | solution.py:17
  60.3 0.7 fusion.14
  61.0 6.8 %collective-permute-done.2 = bf16[384,1280]{1,0:T(8,128)(2,1)S(1)} collective-permute-done((bf16[384,1280]{1,0:T(8,128)(2,1)}, bf16[384,1280]{1,0:T(8,128)(2,1)S(1)}, u32[]{:S(2)}, u32[]{:S(2)}) %collective-permute-start.2) | collective-permute-done | bytes 983072 | tf_op jit(solution)/shard_map/ppermute | solution.py:147
  67.8 0.2 convert_add_fusion
  68.1 2.1 %collective-permute-start.3 = (bf16[192,1280]{1,0:T(8,128)(2,1)S(1)}, bf16[192,1280]{1,0:T(8,128)(2,1)S(1)}, u32[]{:S(2)}, u32[]{:S(2)}) collective-permute-start(bf16[192,1280]{1,0:T(8,128)(2,1)S(1)} %slice.57), channel_id=1, source_target_pairs={{0,24},{1,3},{2,26},{3,1},{4,28},{5,7},{6,30},{7,5},{24,0},{25,27}... | collective-permute-start | bytes 1474568 | tf_op jit(solution)/shard_map/ppermute | solution.py:170
  70.1 0.1 bitcast_add_fusion
  70.2 0.6 fusion.7
  70.9 8.0 %collective-permute-done.3 = bf16[192,1280]{1,0:T(8,128)(2,1)S(1)} collective-permute-done((bf16[192,1280]{1,0:T(8,128)(2,1)S(1)}, bf16[192,1280]{1,0:T(8,128)(2,1)S(1)}, u32[]{:S(2)}, u32[]{:S(2)}) %collective-permute-start.3) | collective-permute-done | bytes 491552 | tf_op jit(solution)/shard_map/ppermute | solution.py:170
  78.9 0.9 fusion.3
  79.8 16.8 %all-to-all-start.1 = ((bf16[24,8,1280]{2,1,0:T(8,128)(2,1)}), bf16[24,8,1280]{2,1,0:T(8,128)(2,1)S(1)}, u32[]{:S(2)}, u32[]{:S(2)}) async-start(bf16[24,8,1280]{2,1,0:T(8,128)(2,1)} %bitcast.16), calls=%async_computation.1 | async-start | bytes 983040 | tf_op jit(solution)/shard_map/all_to_all | solution.py:175
  96.6 0.1 iota_compare_fusion
  96.7 0.1 lt.72
  96.8 0.9 pad_maximum_fusion.1
  97.7 0.1 all_gather_reshape.3
  97.8 44.2 %all_gather.3 = f32[8,8,32]{2,1,0:T(8,128)S(1)} all-gather(f32[1,8,32]{2,1,0:T(8,128)S(1)} %all_gather_reshape.3), channel_id=1, replica_groups=mesh['yh'=2,'x'=4,'y1'=2,'y0'=2,'zc'=3,'z1'=2,'z0'=2,'core'=2] {'yh','x'}, dimensions={0}, use_global_device_ids=true | all-gather | bytes 9216 | tf_op jit(solution)/shard_map/all_gather | solution.py:178
  142.0 0.1 squeeze.22
  142.1 0.6 select_divide_fusion
  142.6 0.1 convert_reduce_fusion
  142.7 0.6 maximum_bitcast_fusion
  (17 shorter events, 0.3 us)
Async XLA Ops:
  4.4 8.0 %copy-start = (bf16[256,1536]{1,0:T(8,128)(2,1)S(1)}, bf16[256,1536]{1,0:T(8,128)(2,1)}, u32[]{:S(2)}) copy-start(bf16[256,1536]{1,0:T(8,128)(2,1)} %param.8) | copy-start | bytes 2359300
  4.4 32.1 %all-to-all-start = ((bf16[16,32,1280]{2,1,0:T(8,128)(2,1)}), bf16[16,32,1280]{2,1,0:T(8,128)(2,1)S(1)}, u32[]{:S(2)}, u32[]{:S(2)}) async-start(bf16[16,32,1280]{2,1,0:T(8,128)(2,1)} %bitcast.47), calls=%async_computation | async-start | bytes 2621440 | tf_op jit(solution)/shard_map/all_to_all | solution.py:117
  12.6 3.6 %collective-permute-start = (bf16[8,32,768]{2,1,0:T(8,128)(2,1)S(1)}, bf16[8,32,768]{2,1,0:T(8,128)(2,1)S(1)}, u32[]{:S(2)}, u32[]{:S(2)}) collective-permute-start(bf16[8,32,768]{2,1,0:T(8,128)(2,1)S(1)} %bitcast.50), channel_id=1, source_target_pairs={{0,1},{1,0},{2,3},{3,2},{4,5},{5,4},{6,7},{7,6},{8,9},{9,8},{10,11... | collective-permute-start | bytes 1179656 | tf_op jit(solution)/shard_map/ppermute | solution.py:17
  38.1 29.7 %collective-permute-start.2 = (bf16[384,1280]{1,0:T(8,128)(2,1)}, bf16[384,1280]{1,0:T(8,128)(2,1)S(1)}, u32[]{:S(2)}, u32[]{:S(2)}) collective-permute-start(bf16[384,1280]{1,0:T(8,128)(2,1)} %convolution_convert_fusion), channel_id=1, source_target_pairs={{0,2},{1,25},{2,0},{3,27},{4,6},{5,29},{6,4},{7,31},{24,26},{25,1}... | collective-permute-start | bytes 2949128 | tf_op jit(solution)/shard_map/ppermute | solution.py:147
  58.3 11.8 %collective-permute-start.1 = (f32[8,32,768]{2,1,0:T(8,128)S(1)}, f32[8,32,768]{2,1,0:T(8,128)S(1)}, u32[]{:S(2)}, u32[]{:S(2)}) collective-permute-start(f32[8,32,768]{2,1,0:T(8,128)S(1)} %dynamic-slice_bitcast_fusion), channel_id=1, source_target_pairs={{0,1},{1,0},{2,3},{3,2},{4,5},{5,4},{6,7},{7,6},{8,9},{9,8},{10,11... | collective-permute-start | bytes 2359304 | tf_op jit(solution)/shard_map/ppermute | solution.py:17
  68.0 2.2 %copy-start.1 = (bf16[256,1536]{1,0:T(8,128)(2,1)S(1)}, bf16[256,1536]{1,0:T(8,128)(2,1)}, u32[]{:S(2)}) copy-start(bf16[256,1536]{1,0:T(8,128)(2,1)} %param.8) | copy-start | bytes 2359300
  68.1 10.9 %collective-permute-start.3 = (bf16[192,1280]{1,0:T(8,128)(2,1)S(1)}, bf16[192,1280]{1,0:T(8,128)(2,1)S(1)}, u32[]{:S(2)}, u32[]{:S(2)}) collective-permute-start(bf16[192,1280]{1,0:T(8,128)(2,1)S(1)} %slice.57), channel_id=1, source_target_pairs={{0,24},{1,3},{2,26},{3,1},{4,28},{5,7},{6,30},{7,5},{24,0},{25,27}... | collective-permute-start | bytes 1474568 | tf_op jit(solution)/shard_map/ppermute | solution.py:170
  70.9 25.7 %copy-start.3 = (s32[8]{0:T(128)S(1)}, s32[8]{0:T(128)}, u32[]{:S(2)}) copy-start(s32[8]{0:T(128)} %counts_ref.1) | copy-start | bytes 100
  79.8 62.3 %copy-start.2 = (f32[256]{0:T(256)S(1)}, f32[256]{0:T(256)}, u32[]{:S(2)}) copy-start(f32[256]{0:T(256)} %param.6) | copy-start | bytes 3076
  79.8 62.8 %all-to-all-start.1 = ((bf16[24,8,1280]{2,1,0:T(8,128)(2,1)}), bf16[24,8,1280]{2,1,0:T(8,128)(2,1)S(1)}, u32[]{:S(2)}, u32[]{:S(2)}) async-start(bf16[24,8,1280]{2,1,0:T(8,128)(2,1)} %bitcast.16), calls=%async_computation.1 | async-start | bytes 983040 | tf_op jit(solution)/shard_map/all_to_all | solution.py:175

commit v5 on v4

--- a/solution.py
+++ b/solution.py
@@ -19,6 +19,19 @@
 
 def pick(value, index, axis):
     return lax.dynamic_index_in_dim(value, index, axis, keepdims=False)
+
+
+def send_back(score):
+    capacity = score.shape[1]
+    score = score.reshape(2, 2, 2, 1, capacity)
+    for axis, bit in (("yh", 1), ("x", 2), ("x", 1)):
+        mine = lax.axis_index(axis) // bit % 2
+        size = lax.axis_size(axis)
+        kept = pick(score, mine, 0)
+        came = lax.ppermute(pick(score, 1 - mine, 0), axis, [(i, i ^ bit) for i in range(size)])
+        both = jnp.where(mine == 0, jnp.stack([kept, came], -2), jnp.stack([came, kept], -2))
+        score = both.reshape(kept.shape[:-2] + (-1, capacity))
+    return score
 
 
 def stage_pairs(stage):
@@ -168,15 +181,13 @@
     sent = total[rows_left:].astype(jnp.bfloat16)
     kept = total[:rows_left]
     came = lax.ppermute(sent, CUBE, stage_pairs(1))
-    came, row_score = lax.optimization_barrier((came, row_score))
+    came, _ = lax.optimization_barrier((came, row_score))
     spread = (kept + came.astype(jnp.float32)).astype(jnp.bfloat16)
     unit = rows_left // lax.axis_size(REST)
-    spread, row_score = lax.optimization_barrier((spread, row_score))
     gathered = lax.all_to_all(
         spread.reshape(-1, unit, half), REST, split_axis=0, concat_axis=0, tiled=True
     ).reshape(-1, 2, unit, half)
-    all_scores = lax.all_gather(row_score.reshape(expert_count, capacity), EXPERT)
-    returned_score = pick(all_scores, lax.axis_index(EXPERT), 1)
+    returned_score = send_back(row_score.reshape(expert_count, capacity))
     slot_index = lax.broadcasted_iota(jnp.int32, (expert_count, capacity), 1)
     live_rows = (slot_index < counts[:, None]).astype(jnp.float32)
     route_grad = live_rows * returned_score / route_weight.reshape(expert_count, capacity)

time: 144 us -> 121 us (0.84)
  the two profiles are of different devices: /device:TPU:16 before, /device:TPU:1 now
where the time goes in v5:
time: 121 us; the launch traced here: 120 us
  starting transfers between devices  51.3 us (42%)
  waiting for transfers between devices  50.9 us (42%)
  matrix products  5.06 us (4%)
  other arithmetic  4.54 us (4%)
  Pallas kernels  4.33 us (4%)
  local copies, waits for them, and re-layouts  2.78 us (2%)
    all_to_all x1, waiting for transfers between devices, body(): lax.all_to_all(outgoing.reshape(expert_count * 2, capacity, half), EXPERT...  25.3 us
    all_to_all x1, starting transfers between devices, body(): lax.all_to_all(spread.reshape(-1, unit, half), REST, split_axis=0, concat...  17.8 us
    all_to_all x1, starting transfers between devices, body(): lax.all_to_all(outgoing.reshape(expert_count * 2, capacity, half), EXPERT...  14.1 us
    ppermute x3, waiting for transfers between devices, send_back(): lax.ppermute(pick(score, 1 - mine, 0), axis, [(i, i ^ bit) for i in range...  11.8 us
    ppermute x3, starting transfers between devices, send_back(): lax.ppermute(pick(score, 1 - mine, 0), axis, [(i, i ^ bit) for i in range...  6.16 us
    ppermute x1, waiting for transfers between devices, body(): came = lax.ppermute(sent, CUBE, stage_pairs(1))  5.72 us
    ppermute x2, starting transfers between devices, swap(): return lax.ppermute(value, axis, [(0, 1), (1, 0)])  5.32 us
    ppermute x1, waiting for transfers between devices, body(): came = lax.ppermute(sent, CUBE, stage_pairs(0))  5.26 us
  transfers between devices with their start and end apart: 9, of which 8 were waited for; matrix products, arithmetic and copies ran while one was open for 8% of the time, Pallas kernels for 1%

profile of v5, /device:TPU:1, one launch (start us, length us, event | category | flops | bytes accessed | tf_op | source)
XLA Modules:
  0.0 119.9 jit_solution(9983043152152785616)
XLA Ops:
  0.6 3.7 %shard_map.76 = bf16[8,2,32,1280]{3,2,1,0:T(8,128)(2,1)} custom-call(s32[8]{0:T(128)} %counts_ref.1, f32[1,256]{1,0:T(1,128)} %bitcast.73, bf16[256,2560]{1,0:T(8,128)(2,1)} %grad_ref.1), custom_call_target="tpu_custom_call" | custom-call | flops 655360 | bytes 2621440 | tf_op jit(solution)/shard_map/pallas_call | solution.py:102
  4.4 14.1 %all-to-all-start = ((bf16[16,32,1280]{2,1,0:T(8,128)(2,1)}), bf16[16,32,1280]{2,1,0:T(8,128)(2,1)S(1)}, u32[]{:S(2)}, u32[]{:S(2)}) async-start(bf16[16,32,1280]{2,1,0:T(8,128)(2,1)} %bitcast.66), calls=%async_computation | async-start | bytes 2621440 | tf_op jit(solution)/shard_map/all_to_all | solution.py:130
  18.5 0.3 fusion.4
  18.8 2.1 %collective-permute-start = (bf16[8,32,768]{2,1,0:T(8,128)(2,1)S(1)}, bf16[8,32,768]{2,1,0:T(8,128)(2,1)S(1)}, u32[]{:S(2)}, u32[]{:S(2)}) collective-permute-start(bf16[8,32,768]{2,1,0:T(8,128)(2,1)S(1)} %bitcast.69), channel_id=1, source_target_pairs={{0,1},{1,0},{2,3},{3,2},{4,5},{5,4},{6,7},{7,6},{8,9},{9,8},{10,11... | collective-permute-start | bytes 1179656 | tf_op jit(solution)/shard_map/ppermute | solution.py:17
  21.0 1.4 %collective-permute-done = bf16[8,32,768]{2,1,0:T(8,128)(2,1)S(1)} collective-permute-done((bf16[8,32,768]{2,1,0:T(8,128)(2,1)S(1)}, bf16[8,32,768]{2,1,0:T(8,128)(2,1)S(1)}, u32[]{:S(2)}, u32[]{:S(2)}) %collective-permute-start) | collective-permute-done | bytes 393248 | tf_op jit(solution)/shard_map/ppermute | solution.py:17
  22.5 0.9 copy.14
  23.5 1.4 %copy.15 = bf16[512,768]{0,1:T(8,128)(2,1)S(1)} copy(bf16[512,768]{1,0:T(8,128)(2,1)} %bitcast.67) | data formatting | bytes 1572864 | tf_op jit(solution)/shard_map/reshape | solution.py:149
  24.9 0.6 shard_map.77
  25.5 25.3 %all-to-all-done = bf16[16,32,1280]{2,1,0:T(8,128)(2,1)S(1)} async-done(((bf16[16,32,1280]{2,1,0:T(8,128)(2,1)}), bf16[16,32,1280]{2,1,0:T(8,128)(2,1)S(1)}, u32[]{:S(2)}, u32[]{:S(2)}) %all-to-all-start) | async-done | bytes 1310752 | tf_op jit(solution)/shard_map/all_to_all | solution.py:130
  50.8 1.6 %convolution_convert_fusion = bf16[384,1280]{1,0:T(8,128)(2,1)} fusion(bf16[512,1280]{1,0:T(8,128)(2,1)S(1)} %bitcast.63, bf16[768,512]{1,0:T(8,128)(2,1)S(1)} %shard_map.77), kind=kOutput, calls=%fused_computation | convolution fusion | flops 503808000 | bytes 2686976 | tf_op jit(solution)/shard_map/dot_general | solution.py:153
  52.4 3.7 %collective-permute-start.2 = (bf16[384,1280]{1,0:T(8,128)(2,1)}, bf16[384,1280]{1,0:T(8,128)(2,1)S(1)}, u32[]{:S(2)}, u32[]{:S(2)}) collective-permute-start(bf16[384,1280]{1,0:T(8,128)(2,1)} %convolution_convert_fusion), channel_id=1, source_target_pairs={{0,2},{1,25},{2,0},{3,27},{4,6},{5,29},{6,4},{7,31},{24,26},{25,1}... | collective-permute-start | bytes 2949128 | tf_op jit(solution)/shard_map/ppermute | solution.py:160
  56.1 2.8 %fusion = f32[8,2,32,768]{3,2,1,0:T(8,128)S(1)} fusion(bf16[8,2,32,1280]{3,2,1,0:T(8,128)(2,1)S(1)} %bitcast.64, bf16[1,768,2560]{2,1,0:T(8,128)(2,1)} %param.9, s32[]{:T(128)S(6)} %select_n.195), kind=kOutput, calls=%fused_computation.1 | convolution fusion | flops 1006632960 | bytes 4849668 | tf_op jit(solution)/shard_map/dot_general | solution.py:167
  59.0 3.2 %collective-permute-start.1 = (f32[8,32,768]{2,1,0:T(8,128)S(1)}, f32[8,32,768]{2,1,0:T(8,128)S(1)}, u32[]{:S(2)}, u32[]{:S(2)}) collective-permute-start(f32[8,32,768]{2,1,0:T(8,128)S(1)} %dynamic-slice_bitcast_fusion), channel_id=1, source_target_pairs={{0,1},{1,0},{2,3},{3,2},{4,5},{5,4},{6,7},{7,6},{8,9},{9,8},{10,11... | collective-permute-start | bytes 2359304 | tf_op jit(solution)/shard_map/ppermute | solution.py:17
  62.1 0.7 fusion.15
  62.8 5.3 %collective-permute-done.2 = bf16[384,1280]{1,0:T(8,128)(2,1)S(1)} collective-permute-done((bf16[384,1280]{1,0:T(8,128)(2,1)}, bf16[384,1280]{1,0:T(8,128)(2,1)S(1)}, u32[]{:S(2)}, u32[]{:S(2)}) %collective-permute-start.2) | collective-permute-done | bytes 983072 | tf_op jit(solution)/shard_map/ppermute | solution.py:160
  68.1 0.2 convert_add_fusion
  68.4 4.1 %collective-permute-start.3 = (bf16[192,1280]{1,0:T(8,128)(2,1)S(1)}, bf16[192,1280]{1,0:T(8,128)(2,1)S(1)}, u32[]{:S(2)}, u32[]{:S(2)}) collective-permute-start(bf16[192,1280]{1,0:T(8,128)(2,1)S(1)} %slice.59), channel_id=1, source_target_pairs={{0,24},{1,3},{2,26},{3,1},{4,28},{5,7},{6,30},{7,5},{24,0},{25,27}... | collective-permute-start | bytes 1474568 | tf_op jit(solution)/shard_map/ppermute | solution.py:183
  72.5 0.1 bitcast_add_fusion
  72.6 0.6 fusion.7
  73.3 5.7 %collective-permute-done.3 = bf16[192,1280]{1,0:T(8,128)(2,1)S(1)} collective-permute-done((bf16[192,1280]{1,0:T(8,128)(2,1)S(1)}, bf16[192,1280]{1,0:T(8,128)(2,1)S(1)}, u32[]{:S(2)}, u32[]{:S(2)}) %collective-permute-start.3) | collective-permute-done | bytes 491552 | tf_op jit(solution)/shard_map/ppermute | solution.py:183
  79.0 0.9 fusion.14
  79.9 17.8 %all-to-all-start.1 = ((bf16[24,8,1280]{2,1,0:T(8,128)(2,1)}), bf16[24,8,1280]{2,1,0:T(8,128)(2,1)S(1)}, u32[]{:S(2)}, u32[]{:S(2)}) async-start(bf16[24,8,1280]{2,1,0:T(8,128)(2,1)} %fusion.14), calls=%async_computation.1 | async-start | bytes 983040 | tf_op jit(solution)/shard_map/all_to_all | solution.py:187
  97.9 2.3 %collective-permute-start.4 = (f32[2,2,1,32]{3,1,0,2:T(2,128)S(1)}, f32[2,2,1,32]{3,1,0,2:T(2,128)S(1)}, u32[]{:S(2)}, u32[]{:S(2)}) collective-permute-start(f32[2,2,1,32]{3,1,0,2:T(2,128)S(1)} %get-tuple-element.23), channel_id=1, source_target_pairs={{0,384},{384,0},{1,385},{385,1},{2,386},{386,2},{3,387},{387,3},{4... | collective-permute-start | bytes 1544 | tf_op jit(solution)/shard_map/ppermute | solution.py:31
  100.3 6.2 %collective-permute-done.4 = f32[2,2,1,32]{3,1,0,2:T(2,128)S(1)} collective-permute-done((f32[2,2,1,32]{3,1,0,2:T(2,128)S(1)}, f32[2,2,1,32]{3,1,0,2:T(2,128)S(1)}, u32[]{:S(2)}, u32[]{:S(2)}) %collective-permute-start.4) | collective-permute-done | bytes 544 | tf_op jit(solution)/shard_map/ppermute | solution.py:31
  106.5 1.9 %collective-permute-start.5 = (f32[2,2,32]{2,1,0:T(2,128)S(1)}, f32[2,2,32]{2,1,0:T(2,128)S(1)}, u32[]{:S(2)}, u32[]{:S(2)}) collective-permute-start(f32[2,2,32]{2,1,0:T(2,128)S(1)} %bitcast.77), channel_id=1, source_target_pairs={{0,192},{96,288},{192,0},{288,96},{1,193},{97,289},{193,1},{289,97... | collective-permute-start | bytes 1544 | tf_op jit(solution)/shard_map/ppermute | solution.py:31
  108.6 4.1 %collective-permute-done.5 = f32[2,2,32]{2,1,0:T(2,128)S(1)} collective-permute-done((f32[2,2,32]{2,1,0:T(2,128)S(1)}, f32[2,2,32]{2,1,0:T(2,128)S(1)}, u32[]{:S(2)}, u32[]{:S(2)}) %collective-permute-start.5) | collective-permute-done | bytes 544 | tf_op jit(solution)/shard_map/ppermute | solution.py:31
  112.7 1.9 %collective-permute-start.6 = (f32[4,32]{1,0:T(4,128)S(1)}, f32[4,32]{1,0:T(4,128)S(1)}, u32[]{:S(2)}, u32[]{:S(2)}) collective-permute-start(f32[4,32]{1,0:T(4,128)S(1)} %get-tuple-element.19), channel_id=1, source_target_pairs={{0,96},{96,0},{192,288},{288,192},{1,97},{97,1},{193,289},{289,193... | collective-permute-start | bytes 1544 | tf_op jit(solution)/shard_map/ppermute | solution.py:31
  114.6 0.9 pad_maximum_fusion.1
  115.6 1.5 %collective-permute-done.6 = f32[4,32]{1,0:T(4,128)S(1)} collective-permute-done((f32[4,32]{1,0:T(4,128)S(1)}, f32[4,32]{1,0:T(4,128)S(1)}, u32[]{:S(2)}, u32[]{:S(2)}) %collective-permute-start.6) | collective-permute-done | bytes 544 | tf_op jit(solution)/shard_map/ppermute | solution.py:31
  117.1 0.6 select_divide_fusion
  117.7 1.5 %all-to-all-done.1 = bf16[24,8,1280]{2,1,0:T(8,128)(2,1)S(1)} async-done(((bf16[24,8,1280]{2,1,0:T(8,128)(2,1)}), bf16[24,8,1280]{2,1,0:T(8,128)(2,1)S(1)}, u32[]{:S(2)}, u32[]{:S(2)}) %all-to-all-start.1) | async-done | bytes 491552 | tf_op jit(solution)/shard_map/all_to_all | solution.py:187
  119.3 0.6 maximum_bitcast_fusion
  (31 shorter events, 0.8 us)
Async XLA Ops:
  4.4 14.1 %copy-start = (bf16[256,1536]{1,0:T(8,128)(2,1)S(1)}, bf16[256,1536]{1,0:T(8,128)(2,1)}, u32[]{:S(2)}) copy-start(bf16[256,1536]{1,0:T(8,128)(2,1)} %param.8) | copy-start | bytes 2359300
  4.4 46.4 %all-to-all-start = ((bf16[16,32,1280]{2,1,0:T(8,128)(2,1)}), bf16[16,32,1280]{2,1,0:T(8,128)(2,1)S(1)}, u32[]{:S(2)}, u32[]{:S(2)}) async-start(bf16[16,32,1280]{2,1,0:T(8,128)(2,1)} %bitcast.66), calls=%async_computation | async-start | bytes 2621440 | tf_op jit(solution)/shard_map/all_to_all | solution.py:130
  18.8 3.6 %collective-permute-start = (bf16[8,32,768]{2,1,0:T(8,128)(2,1)S(1)}, bf16[8,32,768]{2,1,0:T(8,128)(2,1)S(1)}, u32[]{:S(2)}, u32[]{:S(2)}) collective-permute-start(bf16[8,32,768]{2,1,0:T(8,128)(2,1)S(1)} %bitcast.69), channel_id=1, source_target_pairs={{0,1},{1,0},{2,3},{3,2},{4,5},{5,4},{6,7},{7,6},{8,9},{9,8},{10,11... | collective-permute-start | bytes 1179656 | tf_op jit(solution)/shard_map/ppermute | solution.py:17
  52.4 15.7 %collective-permute-start.2 = (bf16[384,1280]{1,0:T(8,128)(2,1)}, bf16[384,1280]{1,0:T(8,128)(2,1)S(1)}, u32[]{:S(2)}, u32[]{:S(2)}) collective-permute-start(bf16[384,1280]{1,0:T(8,128)(2,1)} %convolution_convert_fusion), channel_id=1, source_target_pairs={{0,2},{1,25},{2,0},{3,27},{4,6},{5,29},{6,4},{7,31},{24,26},{25,1}... | collective-permute-start | bytes 2949128 | tf_op jit(solution)/shard_map/ppermute | solution.py:160
  59.0 13.6 %collective-permute-start.1 = (f32[8,32,768]{2,1,0:T(8,128)S(1)}, f32[8,32,768]{2,1,0:T(8,128)S(1)}, u32[]{:S(2)}, u32[]{:S(2)}) collective-permute-start(f32[8,32,768]{2,1,0:T(8,128)S(1)} %dynamic-slice_bitcast_fusion), channel_id=1, source_target_pairs={{0,1},{1,0},{2,3},{3,2},{4,5},{5,4},{6,7},{7,6},{8,9},{9,8},{10,11... | collective-permute-start | bytes 2359304 | tf_op jit(solution)/shard_map/ppermute | solution.py:17
  68.3 4.3 %copy-start.1 = (bf16[256,1536]{1,0:T(8,128)(2,1)S(1)}, bf16[256,1536]{1,0:T(8,128)(2,1)}, u32[]{:S(2)}) copy-start(bf16[256,1536]{1,0:T(8,128)(2,1)} %param.8) | copy-start | bytes 2359300
  68.4 10.6 %collective-permute-start.3 = (bf16[192,1280]{1,0:T(8,128)(2,1)S(1)}, bf16[192,1280]{1,0:T(8,128)(2,1)S(1)}, u32[]{:S(2)}, u32[]{:S(2)}) collective-permute-start(bf16[192,1280]{1,0:T(8,128)(2,1)S(1)} %slice.59), channel_id=1, source_target_pairs={{0,24},{1,3},{2,26},{3,1},{4,28},{5,7},{6,30},{7,5},{24,0},{25,27}... | collective-permute-start | bytes 1474568 | tf_op jit(solution)/shard_map/ppermute | solution.py:183
  73.3 24.5 %copy-start.3 = (s32[8]{0:T(128)S(1)}, s32[8]{0:T(128)}, u32[]{:S(2)}) copy-start(s32[8]{0:T(128)} %counts_ref.1) | copy-start | bytes 100
  79.9 37.3 %copy-start.2 = (f32[256]{0:T(256)S(1)}, f32[256]{0:T(256)}, u32[]{:S(2)}) copy-start(f32[256]{0:T(256)} %param.6) | copy-start | bytes 3076
  79.9 39.3 %all-to-all-start.1 = ((bf16[24,8,1280]{2,1,0:T(8,128)(2,1)}), bf16[24,8,1280]{2,1,0:T(8,128)(2,1)S(1)}, u32[]{:S(2)}, u32[]{:S(2)}) async-start(bf16[24,8,1280]{2,1,0:T(8,128)(2,1)} %fusion.14), calls=%async_computation.1 | async-start | bytes 983040 | tf_op jit(solution)/shard_map/all_to_all | solution.py:187
  97.9 8.6 %collective-permute-start.4 = (f32[2,2,1,32]{3,1,0,2:T(2,128)S(1)}, f32[2,2,1,32]{3,1,0,2:T(2,128)S(1)}, u32[]{:S(2)}, u32[]{:S(2)}) collective-permute-start(f32[2,2,1,32]{3,1,0,2:T(2,128)S(1)} %get-tuple-element.23), channel_id=1, source_target_pairs={{0,384},{384,0},{1,385},{385,1},{2,386},{386,2},{3,387},{387,3},{4... | collective-permute-start | bytes 1544 | tf_op jit(solution)/shard_map/ppermute | solution.py:31
  106.5 6.1 %collective-permute-start.5 = (f32[2,2,32]{2,1,0:T(2,128)S(1)}, f32[2,2,32]{2,1,0:T(2,128)S(1)}, u32[]{:S(2)}, u32[]{:S(2)}) collective-permute-start(f32[2,2,32]{2,1,0:T(2,128)S(1)} %bitcast.77), channel_id=1, source_target_pairs={{0,192},{96,288},{192,0},{288,96},{1,193},{97,289},{193,1},{289,97... | collective-permute-start | bytes 1544 | tf_op jit(solution)/shard_map/ppermute | solution.py:31
  112.7 4.3 %collective-permute-start.6 = (f32[4,32]{1,0:T(4,128)S(1)}, f32[4,32]{1,0:T(4,128)S(1)}, u32[]{:S(2)}, u32[]{:S(2)}) collective-permute-start(f32[4,32]{1,0:T(4,128)S(1)} %get-tuple-element.19), channel_id=1, source_target_pairs={{0,96},{96,0},{192,288},{288,192},{1,97},{97,1},{193,289},{289,193... | collective-permute-start | bytes 1544 | tf_op jit(solution)/shard_map/ppermute | solution.py:31

commit v6 on v5

--- a/solution.py
+++ b/solution.py
@@ -155,11 +155,18 @@
             preferred_element_type=jnp.float32,
         )
 
-    rows_left = hidden_count // 2
-    sent = product(hidden_units[rows_left:], arrived).astype(jnp.bfloat16)
-    came = lax.ppermute(sent, CUBE, stage_pairs(0))
-    arrived, _ = lax.optimization_barrier((arrived, sent))
-    kept = product(hidden_units[:rows_left], arrived)
+    quarter = hidden_count // 4
+    sent_first = product(hidden_units[3 * quarter :], arrived).astype(jnp.bfloat16)
+    came_first = lax.ppermute(sent_first, CUBE, stage_pairs(0))
+    arrived, _ = lax.optimization_barrier((arrived, sent_first))
+    sent_second = product(hidden_units[2 * quarter : 3 * quarter], arrived).astype(jnp.bfloat16)
+    came_second = lax.ppermute(sent_second, CUBE, stage_pairs(0))
+    arrived, _ = lax.optimization_barrier((arrived, sent_second))
+    kept = product(hidden_units[: 2 * quarter], arrived)
+    came_first, kept = lax.optimization_barrier((came_first, kept))
+    passed = (kept[quarter:] + came_first.astype(jnp.float32)).astype(jnp.bfloat16)
+    came = lax.ppermute(passed, CUBE, stage_pairs(1))
+    arrived, _ = lax.optimization_barrier((arrived, passed))
 
     weight_half = lax.dynamic_slice(
         down_weight[0], (0, core * half), (hidden_count, half)
@@ -175,15 +182,10 @@
     grad_rows = jnp.concatenate([grad_gate, grad_up], axis=1).astype(jnp.bfloat16)
     row_score = jnp.sum(grad_hidden * hidden_act.astype(jnp.float32), axis=1)
 
-    came, kept = lax.optimization_barrier((came, kept))
-    total = kept + came.astype(jnp.float32)
-    rows_left //= 2
-    sent = total[rows_left:].astype(jnp.bfloat16)
-    kept = total[:rows_left]
-    came = lax.ppermute(sent, CUBE, stage_pairs(1))
-    came, _ = lax.optimization_barrier((came, row_score))
-    spread = (kept + came.astype(jnp.float32)).astype(jnp.bfloat16)
-    unit = rows_left // lax.axis_size(REST)
+    spread = (
+        kept[:quarter] + came_second.astype(jnp.float32) + came.astype(jnp.float32)
+    ).astype(jnp.bfloat16)
+    unit = quarter // lax.axis_size(REST)
     gathered = lax.all_to_all(
         spread.reshape(-1, unit, half), REST, split_axis=0, concat_axis=0, tiled=True
     ).reshape(-1, 2, unit, half)

time: 121 us -> 118 us (0.975)
  the two profiles are of different devices: /device:TPU:1 before, /device:TPU:16 now
where the time goes in v6:
time: 118 us; the launch traced here: 117 us
  starting transfers between devices  57.2 us (48%)
  waiting for transfers between devices  40.9 us (35%)
  other arithmetic  7.6 us (6%)
  Pallas kernels  4.34 us (4%)
  matrix products  3.53 us (3%)
  local copies, waits for them, and re-layouts  2.77 us (2%)
    all_to_all x1, waiting for transfers between devices, body(): lax.all_to_all(outgoing.reshape(expert_count * 2, capacity, half), EXPERT...  19 us
    ppermute x1, starting transfers between devices, body(): came_first = lax.ppermute(sent_first, CUBE, stage_pairs(0))  17.4 us
    all_to_all x1, starting transfers between devices, body(): lax.all_to_all(spread.reshape(-1, unit, half), REST, split_axis=0, concat...  16.8 us
    ppermute x3, waiting for transfers between devices, send_back(): lax.ppermute(pick(score, 1 - mine, 0), axis, [(i, i ^ bit) for i in range...  14.4 us
    all_to_all x1, starting transfers between devices, body(): lax.all_to_all(outgoing.reshape(expert_count * 2, capacity, half), EXPERT...  8 us
    ppermute x3, starting transfers between devices, send_back(): lax.ppermute(pick(score, 1 - mine, 0), axis, [(i, i ^ bit) for i in range...  6.44 us
    ppermute x2, starting transfers between devices, swap(): return lax.ppermute(value, axis, [(0, 1), (1, 0)])  4.72 us
    pallas_call x1, Pallas kernels, scale(): pl.pallas_call(scale_kernel, grid=(expert_count // blocks,), out_shape=ja...  3.73 us
  transfers between devices with their start and end apart: 10, of which 7 were waited for; matrix products, arithmetic and copies ran while one was open for 10% of the time, Pallas kernels for 1%

profile of v6, /device:TPU:16, one launch (start us, length us, event | category | flops | bytes accessed | tf_op | source)
XLA Modules:
  0.0 117.3 jit_solution(2816862784710433280)
XLA Ops:
  0.6 3.7 %shard_map.76 = bf16[8,2,32,1280]{3,2,1,0:T(8,128)(2,1)} custom-call(s32[8]{0:T(128)} %counts_ref.1, f32[1,256]{1,0:T(1,128)} %bitcast.76, bf16[256,2560]{1,0:T(8,128)(2,1)} %grad_ref.1), custom_call_target="tpu_custom_call" | custom-call | flops 655360 | bytes 2621440 | tf_op jit(solution)/shard_map/pallas_call | solution.py:102
  4.4 8.0 %all-to-all-start = ((bf16[16,32,1280]{2,1,0:T(8,128)(2,1)}), bf16[16,32,1280]{2,1,0:T(8,128)(2,1)S(1)}, u32[]{:S(2)}, u32[]{:S(2)}) async-start(bf16[16,32,1280]{2,1,0:T(8,128)(2,1)} %bitcast.69), calls=%async_computation | async-start | bytes 2621440 | tf_op jit(solution)/shard_map/all_to_all | solution.py:130
  12.6 2.3 %collective-permute-start = (bf16[8,32,768]{2,1,0:T(8,128)(2,1)S(1)}, bf16[8,32,768]{2,1,0:T(8,128)(2,1)S(1)}, u32[]{:S(2)}, u32[]{:S(2)}) collective-permute-start(bf16[8,32,768]{2,1,0:T(8,128)(2,1)S(1)} %bitcast.72), channel_id=1, source_target_pairs={{0,1},{1,0},{2,3},{3,2},{4,5},{5,4},{6,7},{7,6},{8,9},{9,8},{10,11... | collective-permute-start | bytes 1179656 | tf_op jit(solution)/shard_map/ppermute | solution.py:17
  15.0 1.3 %collective-permute-done = bf16[8,32,768]{2,1,0:T(8,128)(2,1)S(1)} collective-permute-done((bf16[8,32,768]{2,1,0:T(8,128)(2,1)S(1)}, bf16[8,32,768]{2,1,0:T(8,128)(2,1)S(1)}, u32[]{:S(2)}, u32[]{:S(2)}) %collective-permute-start) | collective-permute-done | bytes 393248 | tf_op jit(solution)/shard_map/ppermute | solution.py:17
  16.8 0.6 shard_map.77
  17.4 19.0 %all-to-all-done = bf16[16,32,1280]{2,1,0:T(8,128)(2,1)S(1)} async-done(((bf16[16,32,1280]{2,1,0:T(8,128)(2,1)}), bf16[16,32,1280]{2,1,0:T(8,128)(2,1)S(1)}, u32[]{:S(2)}, u32[]{:S(2)}) %all-to-all-start) | async-done | bytes 1310752 | tf_op jit(solution)/shard_map/all_to_all | solution.py:130
  36.4 0.4 convolution_convert_fusion.1
  36.9 17.4 %collective-permute-start.1 = (bf16[192,1280]{1,0:T(8,128)(2,1)S(1)}, bf16[192,1280]{1,0:T(8,128)(2,1)S(1)}, u32[]{:S(2)}, u32[]{:S(2)}) collective-permute-start(bf16[192,1280]{1,0:T(8,128)(2,1)S(1)} %convolution_convert_fusion.1), channel_id=1, source_target_pairs={{0,2},{1,25},{2,0},{3,27},{4,6},{5,29},{6,4},{7,31},{24,26},{25,1}... | collective-permute-start | bytes 1474568 | tf_op jit(solution)/shard_map/ppermute | solution.py:160
  54.3 1.2 %convolution_convert_fusion = bf16[192,1280]{1,0:T(8,128)(2,1)} fusion(bf16[512,1280]{1,0:T(8,128)(2,1)S(1)} %bitcast.66, bf16[768,512]{1,0:T(8,128)(2,1)S(1)} %shard_map.77), kind=kOutput, calls=%fused_computation | convolution fusion | flops 251904000 | bytes 1998848 | tf_op jit(solution)/shard_map/dot_general | solution.py:153
  55.5 1.9 %collective-permute-start.3 = (bf16[192,1280]{1,0:T(8,128)(2,1)}, bf16[192,1280]{1,0:T(8,128)(2,1)}, u32[]{:S(2)}, u32[]{:S(2)}) collective-permute-start(bf16[192,1280]{1,0:T(8,128)(2,1)} %convolution_convert_fusion), channel_id=1, source_target_pairs={{0,2},{1,25},{2,0},{3,27},{4,6},{5,29},{6,4},{7,31},{24,26},{25,1}... | collective-permute-start | bytes 1474568 | tf_op jit(solution)/shard_map/ppermute | solution.py:163
  57.5 0.7 fusion.14
  58.2 3.0 %collective-permute-done.1 = bf16[192,1280]{1,0:T(8,128)(2,1)S(1)} collective-permute-done((bf16[192,1280]{1,0:T(8,128)(2,1)S(1)}, bf16[192,1280]{1,0:T(8,128)(2,1)S(1)}, u32[]{:S(2)}, u32[]{:S(2)}) %collective-permute-start.1) | collective-permute-done | bytes 491552 | tf_op jit(solution)/shard_map/ppermute | solution.py:160
  61.1 0.9 add_convert_fusion.1
  62.0 1.9 %collective-permute-start.4 = (bf16[192,1280]{1,0:T(8,128)(2,1)}, bf16[192,1280]{1,0:T(8,128)(2,1)}, u32[]{:S(2)}, u32[]{:S(2)}) collective-permute-start(bf16[192,1280]{1,0:T(8,128)(2,1)} %add_convert_fusion.1), channel_id=1, source_target_pairs={{0,24},{1,3},{2,26},{3,1},{4,28},{5,7},{6,30},{7,5},{24,0},{25,27}... | collective-permute-start | bytes 1474568 | tf_op jit(solution)/shard_map/ppermute | solution.py:168
  63.9 1.2 %fusion = f32[8,2,32,768]{3,2,1,0:T(8,128)S(1)} fusion(bf16[8,2,32,1280]{3,2,1,0:T(8,128)(2,1)S(1)} %bitcast.68, bf16[1,768,2560]{2,1,0:T(8,128)(2,1)S(1)} %copy-done.8, s32[]{:T(128)S(6)} %select_n.195), kind=kOutput, calls=%fused_computation.2 | convolution fusion | flops 1006632960 | bytes 4849668 | tf_op jit(solution)/shard_map/dot_general | solution.py:174
  65.2 1.2 copy-done.4
  66.3 0.9 dynamic-slice_bitcast_fusion
  67.3 2.4 %collective-permute-start.2 = (f32[8,32,768]{2,1,0:T(8,128)}, f32[8,32,768]{2,1,0:T(8,128)}, u32[]{:S(2)}, u32[]{:S(2)}) collective-permute-start(f32[8,32,768]{2,1,0:T(8,128)} %dynamic-slice_bitcast_fusion), channel_id=1, source_target_pairs={{0,1},{1,0},{2,3},{3,2},{4,5},{5,4},{6,7},{7,6},{8,9},{9,8},{10,11... | collective-permute-start | bytes 2359304 | tf_op jit(solution)/shard_map/ppermute | solution.py:17
  69.8 3.2 %collective-permute-done.4 = bf16[192,1280]{1,0:T(8,128)(2,1)} collective-permute-done((bf16[192,1280]{1,0:T(8,128)(2,1)}, bf16[192,1280]{1,0:T(8,128)(2,1)}, u32[]{:S(2)}, u32[]{:S(2)}) %collective-permute-start.4) | collective-permute-done | bytes 491552 | tf_op jit(solution)/shard_map/ppermute | solution.py:168
  73.0 2.1 %fusion.13 = bf16[24,8,1280]{2,1,0:T(8,128)(2,1)} fusion(bf16[192,1280]{1,0:T(8,128)(2,1)} %collective-permute-done.4, bf16[192,1280]{1,0:T(8,128)(2,1)} %collective-permute-done.3, f32[384,1280]{1,0:T(8,128)S(1)} %copy-done.1), kind=kLoop, calls=%fused_computation.29 | loop fusion | flops 1228800 | bytes 2457600 | tf_op jit(solution)/shard_map/reshape | solution.py:190
  75.2 16.8 %all-to-all-start.1 = ((bf16[24,8,1280]{2,1,0:T(8,128)(2,1)}), bf16[24,8,1280]{2,1,0:T(8,128)(2,1)S(1)}, u32[]{:S(2)}, u32[]{:S(2)}) async-start(bf16[24,8,1280]{2,1,0:T(8,128)(2,1)} %fusion.13), calls=%async_computation.1 | async-start | bytes 983040 | tf_op jit(solution)/shard_map/all_to_all | solution.py:189
  92.0 1.2 %bitcast_add_fusion = f32[8,32,768]{2,1,0:T(8,128)S(1)} fusion(f32[8,32,768]{2,1,0:T(8,128)} %collective-permute-done.2, f32[8,2,32,768]{3,2,1,0:T(8,128)S(1)} %copy-done.5, s32[]{:T(128)S(6)} %select_n.196), kind=kLoop, calls=%fused_computation.27 | loop fusion | flops 196608 | bytes 2359300 | tf_op jit(solution)/shard_map/add | solution.py:179
  93.2 0.6 fusion.6
  93.9 2.6 %collective-permute-start.5 = (f32[2,2,1,32]{3,1,0,2:T(2,128)S(1)}, f32[2,2,1,32]{3,1,0,2:T(2,128)S(1)}, u32[]{:S(2)}, u32[]{:S(2)}) collective-permute-start(f32[2,2,1,32]{3,1,0,2:T(2,128)S(1)} %get-tuple-element.25), channel_id=1, source_target_pairs={{0,384},{384,0},{1,385},{385,1},{2,386},{386,2},{3,387},{387,3},{4... | collective-permute-start | bytes 1544 | tf_op jit(solution)/shard_map/ppermute | solution.py:31
  96.6 6.8 %collective-permute-done.5 = f32[2,2,1,32]{3,1,0,2:T(2,128)S(1)} collective-permute-done((f32[2,2,1,32]{3,1,0,2:T(2,128)S(1)}, f32[2,2,1,32]{3,1,0,2:T(2,128)S(1)}, u32[]{:S(2)}, u32[]{:S(2)}) %collective-permute-start.5) | collective-permute-done | bytes 544 | tf_op jit(solution)/shard_map/ppermute | solution.py:31
  103.4 1.9 %collective-permute-start.6 = (f32[2,2,32]{2,1,0:T(2,128)S(1)}, f32[2,2,32]{2,1,0:T(2,128)S(1)}, u32[]{:S(2)}, u32[]{:S(2)}) collective-permute-start(f32[2,2,32]{2,1,0:T(2,128)S(1)} %bitcast.80), channel_id=1, source_target_pairs={{0,192},{96,288},{192,0},{288,96},{1,193},{97,289},{193,1},{289,97... | collective-permute-start | bytes 1544 | tf_op jit(solution)/shard_map/ppermute | solution.py:31
  105.5 5.0 %collective-permute-done.6 = f32[2,2,32]{2,1,0:T(2,128)S(1)} collective-permute-done((f32[2,2,32]{2,1,0:T(2,128)S(1)}, f32[2,2,32]{2,1,0:T(2,128)S(1)}, u32[]{:S(2)}, u32[]{:S(2)}) %collective-permute-start.6) | collective-permute-done | bytes 544 | tf_op jit(solution)/shard_map/ppermute | solution.py:31
  110.4 1.9 %collective-permute-start.7 = (f32[4,32]{1,0:T(4,128)S(1)}, f32[4,32]{1,0:T(4,128)S(1)}, u32[]{:S(2)}, u32[]{:S(2)}) collective-permute-start(f32[4,32]{1,0:T(4,128)S(1)} %get-tuple-element.21), channel_id=1, source_target_pairs={{0,96},{96,0},{192,288},{288,192},{1,97},{97,1},{193,289},{289,193... | collective-permute-start | bytes 1544 | tf_op jit(solution)/shard_map/ppermute | solution.py:31
  112.4 0.9 pad_maximum_fusion.1
  113.3 2.6 %collective-permute-done.7 = f32[4,32]{1,0:T(4,128)S(1)} collective-permute-done((f32[4,32]{1,0:T(4,128)S(1)}, f32[4,32]{1,0:T(4,128)S(1)}, u32[]{:S(2)}, u32[]{:S(2)}) %collective-permute-start.7) | collective-permute-done | bytes 544 | tf_op jit(solution)/shard_map/ppermute | solution.py:31
  116.0 0.6 select_divide_fusion
  116.7 0.6 maximum_bitcast_fusion
  (43 shorter events, 1.3 us)
Async XLA Ops:
  4.4 8.0 %copy-start.2 = (bf16[256,1536]{1,0:T(8,128)(2,1)S(1)}, bf16[256,1536]{1,0:T(8,128)(2,1)}, u32[]{:S(2)}) copy-start(bf16[256,1536]{1,0:T(8,128)(2,1)} %param.8) | copy-start | bytes 2359300
  4.4 32.1 %all-to-all-start = ((bf16[16,32,1280]{2,1,0:T(8,128)(2,1)}), bf16[16,32,1280]{2,1,0:T(8,128)(2,1)S(1)}, u32[]{:S(2)}, u32[]{:S(2)}) async-start(bf16[16,32,1280]{2,1,0:T(8,128)(2,1)} %bitcast.69), calls=%async_computation | async-start | bytes 2621440 | tf_op jit(solution)/shard_map/all_to_all | solution.py:130
  12.6 3.6 %collective-permute-start = (bf16[8,32,768]{2,1,0:T(8,128)(2,1)S(1)}, bf16[8,32,768]{2,1,0:T(8,128)(2,1)S(1)}, u32[]{:S(2)}, u32[]{:S(2)}) collective-permute-start(bf16[8,32,768]{2,1,0:T(8,128)(2,1)S(1)} %bitcast.72), channel_id=1, source_target_pairs={{0,1},{1,0},{2,3},{3,2},{4,5},{5,4},{6,7},{7,6},{8,9},{9,8},{10,11... | collective-permute-start | bytes 1179656 | tf_op jit(solution)/shard_map/ppermute | solution.py:17
  36.9 24.2 %collective-permute-start.1 = (bf16[192,1280]{1,0:T(8,128)(2,1)S(1)}, bf16[192,1280]{1,0:T(8,128)(2,1)S(1)}, u32[]{:S(2)}, u32[]{:S(2)}) collective-permute-start(bf16[192,1280]{1,0:T(8,128)(2,1)S(1)} %convolution_convert_fusion.1), channel_id=1, source_target_pairs={{0,2},{1,25},{2,0},{3,27},{4,6},{5,29},{6,4},{7,31},{24,26},{25,1}... | collective-permute-start | bytes 1474568 | tf_op jit(solution)/shard_map/ppermute | solution.py:160
  55.5 14.3 %collective-permute-start.3 = (bf16[192,1280]{1,0:T(8,128)(2,1)}, bf16[192,1280]{1,0:T(8,128)(2,1)}, u32[]{:S(2)}, u32[]{:S(2)}) collective-permute-start(bf16[192,1280]{1,0:T(8,128)(2,1)} %convolution_convert_fusion), channel_id=1, source_target_pairs={{0,2},{1,25},{2,0},{3,27},{4,6},{5,29},{6,4},{7,31},{24,26},{25,1}... | collective-permute-start | bytes 1474568 | tf_op jit(solution)/shard_map/ppermute | solution.py:163
  57.5 6.5 %copy-start.8 = (bf16[1,768,2560]{2,1,0:T(8,128)(2,1)S(1)}, bf16[1,768,2560]{2,1,0:T(8,128)(2,1)}, u32[]{:S(2)}) copy-start(bf16[1,768,2560]{2,1,0:T(8,128)(2,1)} %param.9) | copy-start | bytes 11796484
  58.1 3.0 %copy-start = (f32[384,1280]{1,0:T(8,128)}, f32[384,1280]{1,0:T(8,128)S(1)}, u32[]{:S(2)}) copy-start(f32[384,1280]{1,0:T(8,128)S(1)} %fusion.14) | copy-start | bytes 5898244
  62.0 11.0 %collective-permute-start.4 = (bf16[192,1280]{1,0:T(8,128)(2,1)}, bf16[192,1280]{1,0:T(8,128)(2,1)}, u32[]{:S(2)}, u32[]{:S(2)}) collective-permute-start(bf16[192,1280]{1,0:T(8,128)(2,1)} %add_convert_fusion.1), channel_id=1, source_target_pairs={{0,24},{1,3},{2,26},{3,1},{4,28},{5,7},{6,30},{7,5},{24,0},{25,27}... | collective-permute-start | bytes 1474568 | tf_op jit(solution)/shard_map/ppermute | solution.py:168
  63.9 9.1 %copy-start.1 = (f32[384,1280]{1,0:T(8,128)S(1)}, f32[384,1280]{1,0:T(8,128)}, u32[]{:S(2)}) copy-start(f32[384,1280]{1,0:T(8,128)} %copy-done) | copy-start | bytes 5898244
  65.2 1.2 copy-start.4
  66.3 3.4 %copy-start.7 = (s32[8]{0:T(128)S(1)}, s32[8]{0:T(128)}, u32[]{:S(2)}) copy-start(s32[8]{0:T(128)} %counts_ref.1) | copy-start | bytes 100
  67.3 24.7 %collective-permute-start.2 = (f32[8,32,768]{2,1,0:T(8,128)}, f32[8,32,768]{2,1,0:T(8,128)}, u32[]{:S(2)}, u32[]{:S(2)}) collective-permute-start(f32[8,32,768]{2,1,0:T(8,128)} %dynamic-slice_bitcast_fusion), channel_id=1, source_target_pairs={{0,1},{1,0},{2,3},{3,2},{4,5},{5,4},{6,7},{7,6},{8,9},{9,8},{10,11... | collective-permute-start | bytes 2359304 | tf_op jit(solution)/shard_map/ppermute | solution.py:17
  69.8 22.1 %copy-start.5 = (f32[8,2,32,768]{3,2,1,0:T(8,128)S(1)}, f32[8,2,32,768]{3,2,1,0:T(8,128)}, u32[]{:S(2)}) copy-start(f32[8,2,32,768]{3,2,1,0:T(8,128)} %copy-done.4) | copy-start | bytes 4718596
  75.2 18.0 %copy-start.3 = (bf16[256,1536]{1,0:T(8,128)(2,1)S(1)}, bf16[256,1536]{1,0:T(8,128)(2,1)}, u32[]{:S(2)}) copy-start(bf16[256,1536]{1,0:T(8,128)(2,1)} %param.8) | copy-start | bytes 2359300
  75.2 41.4 %all-to-all-start.1 = ((bf16[24,8,1280]{2,1,0:T(8,128)(2,1)}), bf16[24,8,1280]{2,1,0:T(8,128)(2,1)S(1)}, u32[]{:S(2)}, u32[]{:S(2)}) async-start(bf16[24,8,1280]{2,1,0:T(8,128)(2,1)} %fusion.13), calls=%async_computation.1 | async-start | bytes 983040 | tf_op jit(solution)/shard_map/all_to_all | solution.py:189
  93.2 22.8 %copy-start.6 = (f32[256]{0:T(256)S(1)}, f32[256]{0:T(256)}, u32[]{:S(2)}) copy-start(f32[256]{0:T(256)} %param.6) | copy-start | bytes 3076
  93.9 9.5 %collective-permute-start.5 = (f32[2,2,1,32]{3,1,0,2:T(2,128)S(1)}, f32[2,2,1,32]{3,1,0,2:T(2,128)S(1)}, u32[]{:S(2)}, u32[]{:S(2)}) collective-permute-start(f32[2,2,1,32]{3,1,0,2:T(2,128)S(1)} %get-tuple-element.25), channel_id=1, source_target_pairs={{0,384},{384,0},{1,385},{385,1},{2,386},{386,2},{3,387},{387,3},{4... | collective-permute-start | bytes 1544 | tf_op jit(solution)/shard_map/ppermute | solution.py:31
  103.4 7.0 %collective-permute-start.6 = (f32[2,2,32]{2,1,0:T(2,128)S(1)}, f32[2,2,32]{2,1,0:T(2,128)S(1)}, u32[]{:S(2)}, u32[]{:S(2)}) collective-permute-start(f32[2,2,32]{2,1,0:T(2,128)S(1)} %bitcast.80), channel_id=1, source_target_pairs={{0,192},{96,288},{192,0},{288,96},{1,193},{97,289},{193,1},{289,97... | collective-permute-start | bytes 1544 | tf_op jit(solution)/shard_map/ppermute | solution.py:31
  110.4 5.5 %collective-permute-start.7 = (f32[4,32]{1,0:T(4,128)S(1)}, f32[4,32]{1,0:T(4,128)S(1)}, u32[]{:S(2)}, u32[]{:S(2)}) collective-permute-start(f32[4,32]{1,0:T(4,128)S(1)} %get-tuple-element.21), channel_id=1, source_target_pairs={{0,96},{96,0},{192,288},{288,192},{1,97},{97,1},{193,289},{289,193... | collective-permute-start | bytes 1544 | tf_op jit(solution)/shard_map/ppermute | solution.py:31

commit v7 on v6

--- a/solution.py
+++ b/solution.py
@@ -23,15 +23,20 @@
 
 def send_back(score):
     capacity = score.shape[1]
-    score = score.reshape(2, 2, 2, 1, capacity)
-    for axis, bit in (("yh", 1), ("x", 2), ("x", 1)):
-        mine = lax.axis_index(axis) // bit % 2
-        size = lax.axis_size(axis)
-        kept = pick(score, mine, 0)
-        came = lax.ppermute(pick(score, 1 - mine, 0), axis, [(i, i ^ bit) for i in range(size)])
-        both = jnp.where(mine == 0, jnp.stack([kept, came], -2), jnp.stack([came, kept], -2))
-        score = both.reshape(kept.shape[:-2] + (-1, capacity))
-    return score
+    width = lax.axis_size("x")
+    score = score.reshape(2, width, capacity)
+    half, place = lax.axis_index("yh"), lax.axis_index("x")
+    kept = pick(score, half, 0)
+    came = swap(pick(score, 1 - half, 0), "yh")
+    score = jnp.where(half == 0, jnp.stack([kept, came], 1), jnp.stack([came, kept], 1))
+    source = lax.broadcasted_iota(jnp.int32, (2, width, capacity), 1)
+    returned = jnp.zeros((2, width, capacity), jnp.float32)
+    for shift in range(width):
+        part = pick(score, (place + shift) % width, 0)
+        if shift > 0:
+            part = lax.ppermute(part, "x", [(i, (i + shift) % width) for i in range(width)])
+        returned = jnp.where(source == (place + width - shift) % width, part[:, None], returned)
+    return returned.reshape(2 * width, capacity)
 
 
 def stage_pairs(stage):
@@ -159,6 +164,14 @@
     sent_first = product(hidden_units[3 * quarter :], arrived).astype(jnp.bfloat16)
     came_first = lax.ppermute(sent_first, CUBE, stage_pairs(0))
     arrived, _ = lax.optimization_barrier((arrived, sent_first))
+    weight_half = lax.dynamic_slice(
+        down_weight[0], (0, core * half), (hidden_count, half)
+    )
+    grad_partial = lax.dot_general(
+        arrived.reshape(2 * row_total, half), weight_half, (((1,), (1,)), ((), ())),
+        preferred_element_type=jnp.float32,
+    ).reshape(expert_count, 2, capacity, hidden_count)
+    arrived, _ = lax.optimization_barrier((arrived, grad_partial))
     sent_second = product(hidden_units[2 * quarter : 3 * quarter], arrived).astype(jnp.bfloat16)
     came_second = lax.ppermute(sent_second, CUBE, stage_pairs(0))
     arrived, _ = lax.optimization_barrier((arrived, sent_second))
@@ -166,15 +179,7 @@
     came_first, kept = lax.optimization_barrier((came_first, kept))
     passed = (kept[quarter:] + came_first.astype(jnp.float32)).astype(jnp.bfloat16)
     came = lax.ppermute(passed, CUBE, stage_pairs(1))
-    arrived, _ = lax.optimization_barrier((arrived, passed))
-
-    weight_half = lax.dynamic_slice(
-        down_weight[0], (0, core * half), (hidden_count, half)
-    )
-    grad_partial = lax.dot_general(
-        arrived.reshape(2 * row_total, half), weight_half, (((1,), (1,)), ((), ())),
-        preferred_element_type=jnp.float32,
-    ).reshape(expert_count, 2, capacity, hidden_count)
+
     grad_other = swap(pick(grad_partial, 1 - core, 1), "core")
     grad_hidden = (pick(grad_partial, core, 1) + grad_other).reshape(row_total, hidden_count)
     grad_gate = grad_hidden * up_value * sigmoid_gate * (1.0 + gate_value * (1.0 - sigmoid_gate))
@@ -182,6 +187,7 @@
     grad_rows = jnp.concatenate([grad_gate, grad_up], axis=1).astype(jnp.bfloat16)
     row_score = jnp.sum(grad_hidden * hidden_act.astype(jnp.float32), axis=1)
 
+    came_second, _ = lax.optimization_barrier((came_second, row_score))
     spread = (
         kept[:quarter] + came_second.astype(jnp.float32) + came.astype(jnp.float32)
     ).astype(jnp.bfloat16)

time: 118 us -> 116 us (0.983)
  the two profiles are of different devices: /device:TPU:16 before, /device:TPU:1 now
where the time goes in v7:
time: 116 us; the launch traced here: 115 us
  starting transfers between devices  55.5 us (48%)
  waiting for transfers between devices  41.5 us (36%)
  other arithmetic  4.49 us (4%)
  Pallas kernels  4.34 us (4%)
  matrix products  4.29 us (4%)
  local copies, waits for them, and re-layouts  4.01 us (3%)
    all_to_all x1, waiting for transfers between devices, body(): lax.all_to_all(outgoing.reshape(expert_count * 2, capacity, half), EXPERT...  25.3 us
    all_to_all x1, starting transfers between devices, body(): lax.all_to_all(spread.reshape(-1, unit, half), REST, split_axis=0, concat...  16.3 us
    all_to_all x1, starting transfers between devices, body(): lax.all_to_all(outgoing.reshape(expert_count * 2, capacity, half), EXPERT...  14.1 us
    ppermute x3, starting transfers between devices, send_back(): lax.ppermute(part, 'x', [(i, (i + shift) % width) for i in range(width)])  7.97 us
    ppermute x3, starting transfers between devices, swap(): return lax.ppermute(value, axis, [(0, 1), (1, 0)])  7.63 us
    ppermute x3, waiting for transfers between devices, swap(): return lax.ppermute(value, axis, [(0, 1), (1, 0)])  7.13 us
    ppermute x1, waiting for transfers between devices, body(): came = lax.ppermute(passed, CUBE, stage_pairs(1))  6.03 us
    ppermute x1, starting transfers between devices, body(): came = lax.ppermute(passed, CUBE, stage_pairs(1))  3.77 us
  transfers between devices with their start and end apart: 11, of which 6 were waited for; matrix products, arithmetic and copies ran while one was open for 9% of the time, Pallas kernels for 1%

profile of v7, /device:TPU:1, one launch (start us, length us, event | category | flops | bytes accessed | tf_op | source)
XLA Modules:
  0.0 115.1 jit_solution(7636139744660151557)
XLA Ops:
  0.6 3.7 %shard_map.76 = bf16[8,2,32,1280]{3,2,1,0:T(8,128)(2,1)} custom-call(s32[8]{0:T(128)} %counts_ref.1, f32[1,256]{1,0:T(1,128)} %bitcast.65, bf16[256,2560]{1,0:T(8,128)(2,1)} %grad_ref.1), custom_call_target="tpu_custom_call" | custom-call | flops 655360 | bytes 2621440 | tf_op jit(solution)/shard_map/pallas_call | solution.py:107
  4.4 14.1 %all-to-all-start = ((bf16[16,32,1280]{2,1,0:T(8,128)(2,1)}), bf16[16,32,1280]{2,1,0:T(8,128)(2,1)S(1)}, u32[]{:S(2)}, u32[]{:S(2)}) async-start(bf16[16,32,1280]{2,1,0:T(8,128)(2,1)} %bitcast.60), calls=%async_computation | async-start | bytes 2621440 | tf_op jit(solution)/shard_map/all_to_all | solution.py:135
  18.5 0.3 fusion.3
  18.8 2.1 %collective-permute-start = (bf16[8,32,768]{2,1,0:T(8,128)(2,1)S(1)}, bf16[8,32,768]{2,1,0:T(8,128)(2,1)S(1)}, u32[]{:S(2)}, u32[]{:S(2)}) collective-permute-start(bf16[8,32,768]{2,1,0:T(8,128)(2,1)S(1)} %bitcast.63), channel_id=1, source_target_pairs={{0,1},{1,0},{2,3},{3,2},{4,5},{5,4},{6,7},{7,6},{8,9},{9,8},{10,11... | collective-permute-start | bytes 1179656 | tf_op jit(solution)/shard_map/ppermute | solution.py:17
  21.0 1.4 %collective-permute-done = bf16[8,32,768]{2,1,0:T(8,128)(2,1)S(1)} collective-permute-done((bf16[8,32,768]{2,1,0:T(8,128)(2,1)S(1)}, bf16[8,32,768]{2,1,0:T(8,128)(2,1)S(1)}, u32[]{:S(2)}, u32[]{:S(2)}) %collective-permute-start) | collective-permute-done | bytes 393248 | tf_op jit(solution)/shard_map/ppermute | solution.py:17
  22.5 0.9 copy.12
  23.5 1.4 %copy.13 = bf16[512,768]{0,1:T(8,128)(2,1)S(1)} copy(bf16[512,768]{1,0:T(8,128)(2,1)} %bitcast.61) | data formatting | bytes 1572864 | tf_op jit(solution)/shard_map/reshape | solution.py:154
  24.9 0.6 shard_map.77
  25.5 25.3 %all-to-all-done = bf16[16,32,1280]{2,1,0:T(8,128)(2,1)S(1)} async-done(((bf16[16,32,1280]{2,1,0:T(8,128)(2,1)}), bf16[16,32,1280]{2,1,0:T(8,128)(2,1)S(1)}, u32[]{:S(2)}, u32[]{:S(2)}) %all-to-all-start) | async-done | bytes 1310752 | tf_op jit(solution)/shard_map/all_to_all | solution.py:135
  50.8 0.4 convolution_convert_fusion.1
  51.2 3.7 %collective-permute-start.2 = (bf16[192,1280]{1,0:T(8,128)(2,1)S(1)}, bf16[192,1280]{1,0:T(8,128)(2,1)S(1)}, u32[]{:S(2)}, u32[]{:S(2)}) collective-permute-start(bf16[192,1280]{1,0:T(8,128)(2,1)S(1)} %convolution_convert_fusion.1), channel_id=1, source_target_pairs={{0,2},{1,25},{2,0},{3,27},{4,6},{5,29},{6,4},{7,31},{24,26},{25,1}... | collective-permute-start | bytes 1474568 | tf_op jit(solution)/shard_map/ppermute | solution.py:165
  54.9 2.8 %fusion = f32[8,2,32,768]{3,2,1,0:T(8,128)S(1)} fusion(bf16[8,2,32,1280]{3,2,1,0:T(8,128)(2,1)S(1)} %bitcast.57, bf16[1,768,2560]{2,1,0:T(8,128)(2,1)} %param.9, s32[]{:T(128)S(6)} %select_n.190), kind=kOutput, calls=%fused_computation.2 | convolution fusion | flops 1006632960 | bytes 4849668 | tf_op jit(solution)/shard_map/dot_general | solution.py:170
  57.7 0.4 convolution_convert_fusion
  58.1 1.9 %collective-permute-start.3 = (bf16[192,1280]{1,0:T(8,128)(2,1)S(1)}, bf16[192,1280]{1,0:T(8,128)(2,1)S(1)}, u32[]{:S(2)}, u32[]{:S(2)}) collective-permute-start(bf16[192,1280]{1,0:T(8,128)(2,1)S(1)} %convolution_convert_fusion), channel_id=1, source_target_pairs={{0,2},{1,25},{2,0},{3,27},{4,6},{5,29},{6,4},{7,31},{24,26},{25,1}... | collective-permute-start | bytes 1474568 | tf_op jit(solution)/shard_map/ppermute | solution.py:176
  60.1 3.2 %collective-permute-start.1 = (f32[8,32,768]{2,1,0:T(8,128)S(1)}, f32[8,32,768]{2,1,0:T(8,128)S(1)}, u32[]{:S(2)}, u32[]{:S(2)}) collective-permute-start(f32[8,32,768]{2,1,0:T(8,128)S(1)} %dynamic-slice_bitcast_fusion), channel_id=1, source_target_pairs={{0,1},{1,0},{2,3},{3,2},{4,5},{5,4},{6,7},{7,6},{8,9},{9,8},{10,11... | collective-permute-start | bytes 2359304 | tf_op jit(solution)/shard_map/ppermute | solution.py:17
  63.3 0.7 fusion.14
  64.1 3.8 %collective-permute-start.4 = (bf16[192,1280]{1,0:T(8,128)(2,1)S(1)}, bf16[192,1280]{1,0:T(8,128)(2,1)S(1)}, u32[]{:S(2)}, u32[]{:S(2)}) collective-permute-start(bf16[192,1280]{1,0:T(8,128)(2,1)S(1)} %add_convert_fusion.1), channel_id=1, source_target_pairs={{0,24},{1,3},{2,26},{3,1},{4,28},{5,7},{6,30},{7,5},{24,0},{25,27}... | collective-permute-start | bytes 1474568 | tf_op jit(solution)/shard_map/ppermute | solution.py:181
  67.9 0.1 bitcast_add_fusion
  68.0 0.6 fusion.6
  68.7 6.0 %collective-permute-done.4 = bf16[192,1280]{1,0:T(8,128)(2,1)S(1)} collective-permute-done((bf16[192,1280]{1,0:T(8,128)(2,1)S(1)}, bf16[192,1280]{1,0:T(8,128)(2,1)S(1)}, u32[]{:S(2)}, u32[]{:S(2)}) %collective-permute-start.4) | collective-permute-done | bytes 491552 | tf_op jit(solution)/shard_map/ppermute | solution.py:181
  74.7 0.9 fusion.13
  75.6 16.3 %all-to-all-start.1 = ((bf16[24,8,1280]{2,1,0:T(8,128)(2,1)}), bf16[24,8,1280]{2,1,0:T(8,128)(2,1)S(1)}, u32[]{:S(2)}, u32[]{:S(2)}) async-start(bf16[24,8,1280]{2,1,0:T(8,128)(2,1)} %fusion.13), calls=%async_computation.1 | async-start | bytes 983040 | tf_op jit(solution)/shard_map/all_to_all | solution.py:195
  93.4 2.3 %collective-permute-start.5 = (f32[4,32]{1,0:T(4,128)S(1)}, f32[4,32]{1,0:T(4,128)S(1)}, u32[]{:S(2)}, u32[]{:S(2)}) collective-permute-start(f32[4,32]{1,0:T(4,128)S(1)} %get-tuple-element.27), channel_id=1, source_target_pairs={{0,384},{384,0},{1,385},{385,1},{2,386},{386,2},{3,387},{387,3},{4... | collective-permute-start | bytes 1544 | tf_op jit(solution)/shard_map/ppermute | solution.py:17
  95.7 0.9 pad_maximum_fusion.1
  96.6 5.7 %collective-permute-done.5 = f32[4,32]{1,0:T(4,128)S(1)} collective-permute-done((f32[4,32]{1,0:T(4,128)S(1)}, f32[4,32]{1,0:T(4,128)S(1)}, u32[]{:S(2)}, u32[]{:S(2)}) %collective-permute-start.5) | collective-permute-done | bytes 544 | tf_op jit(solution)/shard_map/ppermute | solution.py:17
  102.4 3.6 %collective-permute-start.6 = (f32[2,32]{1,0:T(2,128)S(1)}, f32[2,32]{1,0:T(2,128)S(1)}, u32[]{:S(2)}, u32[]{:S(2)}) collective-permute-start(f32[2,32]{1,0:T(2,128)S(1)} %bitcast.70), channel_id=1, source_target_pairs={{0,288},{96,0},{192,96},{288,192},{1,289},{97,1},{193,97},{289,193... | collective-permute-start | bytes 776 | tf_op jit(solution)/shard_map/ppermute | solution.py:37
  105.9 1.9 %collective-permute-start.7 = (f32[2,32]{1,0:T(2,128)S(1)}, f32[2,32]{1,0:T(2,128)S(1)}, u32[]{:S(2)}, u32[]{:S(2)}) collective-permute-start(f32[2,32]{1,0:T(2,128)S(1)} %bitcast.69), channel_id=1, source_target_pairs={{0,192},{96,288},{192,0},{288,96},{1,193},{97,289},{193,1},{289,97... | collective-permute-start | bytes 776 | tf_op jit(solution)/shard_map/ppermute | solution.py:37
  107.9 2.5 %collective-permute-start.8 = (f32[2,32]{1,0:T(2,128)S(1)}, f32[2,32]{1,0:T(2,128)S(1)}, u32[]{:S(2)}, u32[]{:S(2)}) collective-permute-start(f32[2,32]{1,0:T(2,128)S(1)} %bitcast.68), channel_id=1, source_target_pairs={{0,96},{96,192},{192,288},{288,0},{1,97},{97,193},{193,289},{289,1... | collective-permute-start | bytes 776 | tf_op jit(solution)/shard_map/ppermute | solution.py:37
  110.6 1.2 %collective-permute-done.7 = f32[2,32]{1,0:T(2,128)S(1)} collective-permute-done((f32[2,32]{1,0:T(2,128)S(1)}, f32[2,32]{1,0:T(2,128)S(1)}, u32[]{:S(2)}, u32[]{:S(2)}) %collective-permute-start.7) | collective-permute-done | bytes 288 | tf_op jit(solution)/shard_map/ppermute | solution.py:37
  111.9 1.8 %collective-permute-done.8 = f32[2,32]{1,0:T(2,128)S(1)} collective-permute-done((f32[2,32]{1,0:T(2,128)S(1)}, f32[2,32]{1,0:T(2,128)S(1)}, u32[]{:S(2)}, u32[]{:S(2)}) %collective-permute-start.8) | collective-permute-done | bytes 288 | tf_op jit(solution)/shard_map/ppermute | solution.py:37
  113.8 0.6 select_divide_fusion
  114.5 0.6 maximum_bitcast_fusion
  (55 shorter events, 2.1 us)
Async XLA Ops:
  4.4 14.1 %copy-start = (bf16[256,1536]{1,0:T(8,128)(2,1)S(1)}, bf16[256,1536]{1,0:T(8,128)(2,1)}, u32[]{:S(2)}) copy-start(bf16[256,1536]{1,0:T(8,128)(2,1)} %param.8) | copy-start | bytes 2359300
  4.4 46.4 %all-to-all-start = ((bf16[16,32,1280]{2,1,0:T(8,128)(2,1)}), bf16[16,32,1280]{2,1,0:T(8,128)(2,1)S(1)}, u32[]{:S(2)}, u32[]{:S(2)}) async-start(bf16[16,32,1280]{2,1,0:T(8,128)(2,1)} %bitcast.60), calls=%async_computation | async-start | bytes 2621440 | tf_op jit(solution)/shard_map/all_to_all | solution.py:135
  18.8 3.6 %collective-permute-start = (bf16[8,32,768]{2,1,0:T(8,128)(2,1)S(1)}, bf16[8,32,768]{2,1,0:T(8,128)(2,1)S(1)}, u32[]{:S(2)}, u32[]{:S(2)}) collective-permute-start(bf16[8,32,768]{2,1,0:T(8,128)(2,1)S(1)} %bitcast.63), channel_id=1, source_target_pairs={{0,1},{1,0},{2,3},{3,2},{4,5},{5,4},{6,7},{7,6},{8,9},{9,8},{10,11... | collective-permute-start | bytes 1179656 | tf_op jit(solution)/shard_map/ppermute | solution.py:17
  51.2 12.8 %collective-permute-start.2 = (bf16[192,1280]{1,0:T(8,128)(2,1)S(1)}, bf16[192,1280]{1,0:T(8,128)(2,1)S(1)}, u32[]{:S(2)}, u32[]{:S(2)}) collective-permute-start(bf16[192,1280]{1,0:T(8,128)(2,1)S(1)} %convolution_convert_fusion.1), channel_id=1, source_target_pairs={{0,2},{1,25},{2,0},{3,27},{4,6},{5,29},{6,4},{7,31},{24,26},{25,1}... | collective-permute-start | bytes 1474568 | tf_op jit(solution)/shard_map/ppermute | solution.py:165
  58.1 10.5 %collective-permute-start.3 = (bf16[192,1280]{1,0:T(8,128)(2,1)S(1)}, bf16[192,1280]{1,0:T(8,128)(2,1)S(1)}, u32[]{:S(2)}, u32[]{:S(2)}) collective-permute-start(bf16[192,1280]{1,0:T(8,128)(2,1)S(1)} %convolution_convert_fusion), channel_id=1, source_target_pairs={{0,2},{1,25},{2,0},{3,27},{4,6},{5,29},{6,4},{7,31},{24,26},{25,1}... | collective-permute-start | bytes 1474568 | tf_op jit(solution)/shard_map/ppermute | solution.py:176
  60.1 7.8 %collective-permute-start.1 = (f32[8,32,768]{2,1,0:T(8,128)S(1)}, f32[8,32,768]{2,1,0:T(8,128)S(1)}, u32[]{:S(2)}, u32[]{:S(2)}) collective-permute-start(f32[8,32,768]{2,1,0:T(8,128)S(1)} %dynamic-slice_bitcast_fusion), channel_id=1, source_target_pairs={{0,1},{1,0},{2,3},{3,2},{4,5},{5,4},{6,7},{7,6},{8,9},{9,8},{10,11... | collective-permute-start | bytes 2359304 | tf_op jit(solution)/shard_map/ppermute | solution.py:17
  64.1 3.9 %copy-start.1 = (bf16[256,1536]{1,0:T(8,128)(2,1)S(1)}, bf16[256,1536]{1,0:T(8,128)(2,1)}, u32[]{:S(2)}) copy-start(bf16[256,1536]{1,0:T(8,128)(2,1)} %param.8) | copy-start | bytes 2359300
  64.1 10.6 %collective-permute-start.4 = (bf16[192,1280]{1,0:T(8,128)(2,1)S(1)}, bf16[192,1280]{1,0:T(8,128)(2,1)S(1)}, u32[]{:S(2)}, u32[]{:S(2)}) collective-permute-start(bf16[192,1280]{1,0:T(8,128)(2,1)S(1)} %add_convert_fusion.1), channel_id=1, source_target_pairs={{0,24},{1,3},{2,26},{3,1},{4,28},{5,7},{6,30},{7,5},{24,0},{25,27}... | collective-permute-start | bytes 1474568 | tf_op jit(solution)/shard_map/ppermute | solution.py:181
  68.7 24.5 %copy-start.3 = (s32[8]{0:T(128)S(1)}, s32[8]{0:T(128)}, u32[]{:S(2)}) copy-start(s32[8]{0:T(128)} %counts_ref.1) | copy-start | bytes 100
  75.6 38.1 %copy-start.2 = (f32[256]{0:T(256)S(1)}, f32[256]{0:T(256)}, u32[]{:S(2)}) copy-start(f32[256]{0:T(256)} %param.6) | copy-start | bytes 3076
  75.6 38.7 %all-to-all-start.1 = ((bf16[24,8,1280]{2,1,0:T(8,128)(2,1)}), bf16[24,8,1280]{2,1,0:T(8,128)(2,1)S(1)}, u32[]{:S(2)}, u32[]{:S(2)}) async-start(bf16[24,8,1280]{2,1,0:T(8,128)(2,1)} %fusion.13), calls=%async_computation.1 | async-start | bytes 983040 | tf_op jit(solution)/shard_map/all_to_all | solution.py:195
  93.4 9.0 %collective-permute-start.5 = (f32[4,32]{1,0:T(4,128)S(1)}, f32[4,32]{1,0:T(4,128)S(1)}, u32[]{:S(2)}, u32[]{:S(2)}) collective-permute-start(f32[4,32]{1,0:T(4,128)S(1)} %get-tuple-element.27), channel_id=1, source_target_pairs={{0,384},{384,0},{1,385},{385,1},{2,386},{386,2},{3,387},{387,3},{4... | collective-permute-start | bytes 1544 | tf_op jit(solution)/shard_map/ppermute | solution.py:17
  102.4 8.1 %collective-permute-start.6 = (f32[2,32]{1,0:T(2,128)S(1)}, f32[2,32]{1,0:T(2,128)S(1)}, u32[]{:S(2)}, u32[]{:S(2)}) collective-permute-start(f32[2,32]{1,0:T(2,128)S(1)} %bitcast.70), channel_id=1, source_target_pairs={{0,288},{96,0},{192,96},{288,192},{1,289},{97,1},{193,97},{289,193... | collective-permute-start | bytes 776 | tf_op jit(solution)/shard_map/ppermute | solution.py:37
  105.9 5.8 %collective-permute-start.7 = (f32[2,32]{1,0:T(2,128)S(1)}, f32[2,32]{1,0:T(2,128)S(1)}, u32[]{:S(2)}, u32[]{:S(2)}) collective-permute-start(f32[2,32]{1,0:T(2,128)S(1)} %bitcast.69), channel_id=1, source_target_pairs={{0,192},{96,288},{192,0},{288,96},{1,193},{97,289},{193,1},{289,97... | collective-permute-start | bytes 776 | tf_op jit(solution)/shard_map/ppermute | solution.py:37
  107.9 5.8 %collective-permute-start.8 = (f32[2,32]{1,0:T(2,128)S(1)}, f32[2,32]{1,0:T(2,128)S(1)}, u32[]{:S(2)}, u32[]{:S(2)}) collective-permute-start(f32[2,32]{1,0:T(2,128)S(1)} %bitcast.68), channel_id=1, source_target_pairs={{0,96},{96,192},{192,288},{288,0},{1,97},{97,193},{193,289},{289,1... | collective-permute-start | bytes 776 | tf_op jit(solution)/shard_map/ppermute | solution.py:37

commit v8 on v7

--- a/solution.py
+++ b/solution.py
@@ -29,13 +29,14 @@
     kept = pick(score, half, 0)
     came = swap(pick(score, 1 - half, 0), "yh")
     score = jnp.where(half == 0, jnp.stack([kept, came], 1), jnp.stack([came, kept], 1))
-    source = lax.broadcasted_iota(jnp.int32, (2, width, capacity), 1)
-    returned = jnp.zeros((2, width, capacity), jnp.float32)
+    parts = []
     for shift in range(width):
         part = pick(score, (place + shift) % width, 0)
         if shift > 0:
             part = lax.ppermute(part, "x", [(i, (i + shift) % width) for i in range(width)])
-        returned = jnp.where(source == (place + width - shift) % width, part[:, None], returned)
+        parts.append(part)
+    turned = jnp.stack([parts[-k % width] for k in range(width)] * 2, axis=1)
+    returned = lax.dynamic_slice_in_dim(turned, (width - place) % width, width, axis=1)
     return returned.reshape(2 * width, capacity)
 
 
@@ -103,7 +104,7 @@
     expert_count = counts.shape[0]
     capacity = row_total // expert_count
     half = feature_count // 2
-    blocks = 2
+    blocks = expert_count // 2
     return pl.pallas_call(
         scale_kernel,
         grid=(expert_count // blocks,),
@@ -179,6 +180,7 @@
     came_first, kept = lax.optimization_barrier((came_first, kept))
     passed = (kept[quarter:] + came_first.astype(jnp.float32)).astype(jnp.bfloat16)
     came = lax.ppermute(passed, CUBE, stage_pairs(1))
+    grad_partial, _ = lax.optimization_barrier((grad_partial, passed))
 
     grad_other = swap(pick(grad_partial, 1 - core, 1), "core")
     grad_hidden = (pick(grad_partial, core, 1) + grad_other).reshape(row_total, hidden_count)
@@ -187,7 +189,6 @@
     grad_rows = jnp.concatenate([grad_gate, grad_up], axis=1).astype(jnp.bfloat16)
     row_score = jnp.sum(grad_hidden * hidden_act.astype(jnp.float32), axis=1)
 
-    came_second, _ = lax.optimization_barrier((came_second, row_score))
     spread = (
         kept[:quarter] + came_second.astype(jnp.float32) + came.astype(jnp.float32)
     ).astype(jnp.bfloat16)

time: 116 us -> 119 us (1.026)
  other arithmetic: 4.49 us -> 6.84 us
  matrix products: 4.29 us -> 6.24 us
  Pallas kernels: 4.34 us -> 3 us
    ppermute x1, waiting for transfers between devices: 6.03 us -> 4.35 us  [body(): came = lax.ppermute(passed, CUBE, stage_pairs(1))]
    pallas_call x1, Pallas kernels: 3.74 us -> 2.39 us  [scale(): pl.pallas_call(scale_kernel, grid=(expert_count // blocks,), out_shape=ja...]
    unnamed x8 -> x19, local copies, waits for them, and re-layouts: 0.02 us -> 1.33 us
    reshape x1, other arithmetic: 0.93 us -> 2.14 us  [body(): spread.reshape(-1, unit, half)]
    all_to_all x1, waiting for transfers between devices: 0.01 us -> 1.21 us  [body(): lax.all_to_all(spread.reshape(-1, unit, half), REST, split_axis=0, concat...]
  transfers between devices with their start and end apart: 11 -> 11, of which waited for: 6 -> 7; matrix products, arithmetic and copies ran while one was open for 9% -> 13% of each run, Pallas kernels for 1% -> 1%
where the time goes in v8:
time: 119 us; the launch traced here: 118 us
  starting transfers between devices  55.2 us (46%)
  waiting for transfers between devices  40.8 us (34%)
  other arithmetic  6.84 us (6%)
  matrix products  6.24 us (5%)
  local copies, waits for them, and re-layouts  4.94 us (4%)
  Pallas kernels  3 us (3%)
    all_to_all x1, waiting for transfers between devices, body(): lax.all_to_all(outgoing.reshape(expert_count * 2, capacity, half), EXPERT...  25.3 us
    all_to_all x1, starting transfers between devices, body(): lax.all_to_all(spread.reshape(-1, unit, half), REST, split_axis=0, concat...  16.2 us
    all_to_all x1, starting transfers between devices, body(): lax.all_to_all(outgoing.reshape(expert_count * 2, capacity, half), EXPERT...  14.1 us
    ppermute x3, starting transfers between devices, swap(): return lax.ppermute(value, axis, [(0, 1), (1, 0)])  7.65 us
    ppermute x3, starting transfers between devices, send_back(): lax.ppermute(part, 'x', [(i, (i + shift) % width) for i in range(width)])  7.62 us
    ppermute x3, waiting for transfers between devices, swap(): return lax.ppermute(value, axis, [(0, 1), (1, 0)])  6.68 us
    ppermute x1, waiting for transfers between devices, body(): came = lax.ppermute(passed, CUBE, stage_pairs(1))  4.35 us
    ppermute x1, starting transfers between devices, body(): came = lax.ppermute(passed, CUBE, stage_pairs(1))  4 us
  transfers between devices with their start and end apart: 11, of which 7 were waited for; matrix products, arithmetic and copies ran while one was open for 13% of the time, Pallas kernels for 1%

profile of v8, /device:TPU:1, one launch (start us, length us, event | category | flops | bytes accessed | tf_op | source)
XLA Modules:
  0.0 118.0 jit_solution(4238311128368006872)
XLA Ops:
  0.6 2.4 %shard_map.76 = bf16[8,2,32,1280]{3,2,1,0:T(8,128)(2,1)} custom-call(s32[8]{0:T(128)} %counts_ref.1, f32[1,256]{1,0:T(1,128)} %bitcast.76, bf16[256,2560]{1,0:T(8,128)(2,1)} %grad_ref.1), custom_call_target="tpu_custom_call" | custom-call | flops 655360 | bytes 2621440 | tf_op jit(solution)/shard_map/pallas_call | solution.py:108
  3.0 14.1 %all-to-all-start = ((bf16[16,32,1280]{2,1,0:T(8,128)(2,1)}), bf16[16,32,1280]{2,1,0:T(8,128)(2,1)S(1)}, u32[]{:S(2)}, u32[]{:S(2)}) async-start(bf16[16,32,1280]{2,1,0:T(8,128)(2,1)} %bitcast.69), calls=%async_computation | async-start | bytes 2621440 | tf_op jit(solution)/shard_map/all_to_all | solution.py:136
  17.4 2.1 %collective-permute-start = (bf16[8,32,768]{2,1,0:T(8,128)(2,1)S(1)}, bf16[8,32,768]{2,1,0:T(8,128)(2,1)S(1)}, u32[]{:S(2)}, u32[]{:S(2)}) collective-permute-start(bf16[8,32,768]{2,1,0:T(8,128)(2,1)S(1)} %bitcast.72), channel_id=1, source_target_pairs={{0,1},{1,0},{2,3},{3,2},{4,5},{5,4},{6,7},{7,6},{8,9},{9,8},{10,11... | collective-permute-start | bytes 1179656 | tf_op jit(solution)/shard_map/ppermute | solution.py:17
  19.6 1.4 %collective-permute-done = bf16[8,32,768]{2,1,0:T(8,128)(2,1)S(1)} collective-permute-done((bf16[8,32,768]{2,1,0:T(8,128)(2,1)S(1)}, bf16[8,32,768]{2,1,0:T(8,128)(2,1)S(1)}, u32[]{:S(2)}, u32[]{:S(2)}) %collective-permute-start) | collective-permute-done | bytes 393248 | tf_op jit(solution)/shard_map/ppermute | solution.py:17
  21.2 0.9 copy.12
  22.1 1.4 %copy.13 = bf16[512,768]{0,1:T(8,128)(2,1)S(1)} copy(bf16[512,768]{1,0:T(8,128)(2,1)} %bitcast.70) | data formatting | bytes 1572864 | tf_op jit(solution)/shard_map/reshape | solution.py:155
  23.5 0.6 shard_map.77
  24.2 25.3 %all-to-all-done = bf16[16,32,1280]{2,1,0:T(8,128)(2,1)S(1)} async-done(((bf16[16,32,1280]{2,1,0:T(8,128)(2,1)}), bf16[16,32,1280]{2,1,0:T(8,128)(2,1)S(1)}, u32[]{:S(2)}, u32[]{:S(2)}) %all-to-all-start) | async-done | bytes 1310752 | tf_op jit(solution)/shard_map/all_to_all | solution.py:136
  49.9 3.7 %collective-permute-start.1 = (bf16[192,1280]{1,0:T(8,128)(2,1)S(1)}, bf16[192,1280]{1,0:T(8,128)(2,1)S(1)}, u32[]{:S(2)}, u32[]{:S(2)}) collective-permute-start(bf16[192,1280]{1,0:T(8,128)(2,1)S(1)} %convolution_convert_fusion.1), channel_id=1, source_target_pairs={{0,2},{1,25},{2,0},{3,27},{4,6},{5,29},{6,4},{7,31},{24,26},{25,1}... | collective-permute-start | bytes 1474568 | tf_op jit(solution)/shard_map/ppermute | solution.py:166
  53.6 3.9 %fusion = f32[8,2,32,768]{3,2,1,0:T(8,128)} fusion(bf16[8,2,32,1280]{3,2,1,0:T(8,128)(2,1)S(1)} %bitcast.66, bf16[1,768,2560]{2,1,0:T(8,128)(2,1)} %param.9, s32[]{:T(128)S(6)} %select_n.166), kind=kOutput, calls=%fused_computation.2 | convolution fusion | flops 1006632960 | bytes 4849668 | tf_op jit(solution)/shard_map/dot_general | solution.py:171
  57.5 1.2 %convolution_convert_fusion = bf16[192,1280]{1,0:T(8,128)(2,1)} fusion(bf16[512,1280]{1,0:T(8,128)(2,1)S(1)} %bitcast.67, bf16[768,512]{1,0:T(8,128)(2,1)S(1)} %shard_map.77), kind=kOutput, calls=%fused_computation | convolution fusion | flops 251904000 | bytes 1998848 | tf_op jit(solution)/shard_map/dot_general | solution.py:159
  58.7 1.9 %collective-permute-start.3 = (bf16[192,1280]{1,0:T(8,128)(2,1)}, bf16[192,1280]{1,0:T(8,128)(2,1)S(1)}, u32[]{:S(2)}, u32[]{:S(2)}) collective-permute-start(bf16[192,1280]{1,0:T(8,128)(2,1)} %convolution_convert_fusion), channel_id=1, source_target_pairs={{0,2},{1,25},{2,0},{3,27},{4,6},{5,29},{6,4},{7,31},{24,26},{25,1}... | collective-permute-start | bytes 1474568 | tf_op jit(solution)/shard_map/ppermute | solution.py:177
  60.7 0.7 fusion.14
  61.4 1.3 %copy-done = f32[384,1280]{1,0:T(8,128)} copy-done((f32[384,1280]{1,0:T(8,128)}, f32[384,1280]{1,0:T(8,128)S(1)}, u32[]{:S(2)}) %copy-start) | copy-done | bytes 1966104
  62.7 4.0 %collective-permute-start.4 = (bf16[192,1280]{1,0:T(8,128)(2,1)S(1)}, bf16[192,1280]{1,0:T(8,128)(2,1)S(1)}, u32[]{:S(2)}, u32[]{:S(2)}) collective-permute-start(bf16[192,1280]{1,0:T(8,128)(2,1)S(1)} %add_convert_fusion.1), channel_id=1, source_target_pairs={{0,24},{1,3},{2,26},{3,1},{4,28},{5,7},{6,30},{7,5},{24,0},{25,27}... | collective-permute-start | bytes 1474568 | tf_op jit(solution)/shard_map/ppermute | solution.py:182
  66.8 1.0 dynamic-slice_bitcast_fusion
  67.7 3.2 %collective-permute-start.2 = (f32[8,32,768]{2,1,0:T(8,128)}, f32[8,32,768]{2,1,0:T(8,128)}, u32[]{:S(2)}, u32[]{:S(2)}) collective-permute-start(f32[8,32,768]{2,1,0:T(8,128)} %dynamic-slice_bitcast_fusion), channel_id=1, source_target_pairs={{0,1},{1,0},{2,3},{3,2},{4,5},{5,4},{6,7},{7,6},{8,9},{9,8},{10,11... | collective-permute-start | bytes 2359304 | tf_op jit(solution)/shard_map/ppermute | solution.py:17
  71.2 4.3 %collective-permute-done.4 = bf16[192,1280]{1,0:T(8,128)(2,1)S(1)} collective-permute-done((bf16[192,1280]{1,0:T(8,128)(2,1)S(1)}, bf16[192,1280]{1,0:T(8,128)(2,1)S(1)}, u32[]{:S(2)}, u32[]{:S(2)}) %collective-permute-start.4) | collective-permute-done | bytes 491552 | tf_op jit(solution)/shard_map/ppermute | solution.py:182
  75.5 2.1 %fusion.13 = bf16[24,8,1280]{2,1,0:T(8,128)(2,1)} fusion(bf16[192,1280]{1,0:T(8,128)(2,1)S(1)} %collective-permute-done.4, bf16[192,1280]{1,0:T(8,128)(2,1)S(1)} %collective-permute-done.3, f32[384,1280]{1,0:T(8,128)} %copy-done), kind=kLoop, calls=%fused_computation.29 | loop fusion | flops 1228800 | bytes 2457600 | tf_op jit(solution)/shard_map/reshape | solution.py:197
  77.7 16.2 %all-to-all-start.1 = ((bf16[24,8,1280]{2,1,0:T(8,128)(2,1)}), bf16[24,8,1280]{2,1,0:T(8,128)(2,1)S(1)}, u32[]{:S(2)}, u32[]{:S(2)}) async-start(bf16[24,8,1280]{2,1,0:T(8,128)(2,1)} %fusion.13), calls=%async_computation.1 | async-start | bytes 983040 | tf_op jit(solution)/shard_map/all_to_all | solution.py:196
  93.8 1.2 %bitcast_add_fusion = f32[8,32,768]{2,1,0:T(8,128)S(1)} fusion(f32[8,32,768]{2,1,0:T(8,128)} %collective-permute-done.2, f32[8,2,32,768]{3,2,1,0:T(8,128)S(1)} %copy-done.3, s32[]{:T(128)S(6)} %select_n.167), kind=kLoop, calls=%fused_computation.27 | loop fusion | flops 196608 | bytes 2359300 | tf_op jit(solution)/shard_map/add | solution.py:186
  95.1 0.6 fusion.6
  95.8 2.3 %collective-permute-start.5 = (f32[4,32]{1,0:T(4,128)S(1)}, f32[4,32]{1,0:T(4,128)S(1)}, u32[]{:S(2)}, u32[]{:S(2)}) collective-permute-start(f32[4,32]{1,0:T(4,128)S(1)} %get-tuple-element.27), channel_id=1, source_target_pairs={{0,384},{384,0},{1,385},{385,1},{2,386},{386,2},{3,387},{387,3},{4... | collective-permute-start | bytes 1544 | tf_op jit(solution)/shard_map/ppermute | solution.py:17
  98.2 0.9 pad_maximum_fusion.1
  99.1 5.2 %collective-permute-done.5 = f32[4,32]{1,0:T(4,128)S(1)} collective-permute-done((f32[4,32]{1,0:T(4,128)S(1)}, f32[4,32]{1,0:T(4,128)S(1)}, u32[]{:S(2)}, u32[]{:S(2)}) %collective-permute-start.5) | collective-permute-done | bytes 544 | tf_op jit(solution)/shard_map/ppermute | solution.py:17
  104.4 3.2 %collective-permute-start.6 = (f32[2,32]{1,0:T(2,128)S(1)}, f32[2,32]{1,0:T(2,128)S(1)}, u32[]{:S(2)}, u32[]{:S(2)}) collective-permute-start(f32[2,32]{1,0:T(2,128)S(1)} %bitcast.80), channel_id=1, source_target_pairs={{0,288},{96,0},{192,96},{288,192},{1,289},{97,1},{193,97},{289,193... | collective-permute-start | bytes 776 | tf_op jit(solution)/shard_map/ppermute | solution.py:36
  107.6 1.9 %collective-permute-start.7 = (f32[2,32]{1,0:T(2,128)S(1)}, f32[2,32]{1,0:T(2,128)S(1)}, u32[]{:S(2)}, u32[]{:S(2)}) collective-permute-start(f32[2,32]{1,0:T(2,128)S(1)} %bitcast.79), channel_id=1, source_target_pairs={{0,192},{96,288},{192,0},{288,96},{1,193},{97,289},{193,1},{289,97... | collective-permute-start | bytes 776 | tf_op jit(solution)/shard_map/ppermute | solution.py:36
  109.5 2.5 %collective-permute-start.8 = (f32[2,32]{1,0:T(2,128)S(1)}, f32[2,32]{1,0:T(2,128)S(1)}, u32[]{:S(2)}, u32[]{:S(2)}) collective-permute-start(f32[2,32]{1,0:T(2,128)S(1)} %bitcast.78), channel_id=1, source_target_pairs={{0,96},{96,192},{192,288},{288,0},{1,97},{97,193},{193,289},{289,1... | collective-permute-start | bytes 776 | tf_op jit(solution)/shard_map/ppermute | solution.py:36
  112.1 1.7 %collective-permute-done.7 = f32[2,32]{1,0:T(2,128)S(1)} collective-permute-done((f32[2,32]{1,0:T(2,128)S(1)}, f32[2,32]{1,0:T(2,128)S(1)}, u32[]{:S(2)}, u32[]{:S(2)}) %collective-permute-start.7) | collective-permute-done | bytes 288 | tf_op jit(solution)/shard_map/ppermute | solution.py:36
  113.7 1.6 %collective-permute-done.8 = f32[2,32]{1,0:T(2,128)S(1)} collective-permute-done((f32[2,32]{1,0:T(2,128)S(1)}, f32[2,32]{1,0:T(2,128)S(1)}, u32[]{:S(2)}, u32[]{:S(2)}) %collective-permute-start.8) | collective-permute-done | bytes 288 | tf_op jit(solution)/shard_map/ppermute | solution.py:36
  116.1 1.2 %all-to-all-done.1 = bf16[24,8,1280]{2,1,0:T(8,128)(2,1)S(1)} async-done(((bf16[24,8,1280]{2,1,0:T(8,128)(2,1)}), bf16[24,8,1280]{2,1,0:T(8,128)(2,1)S(1)}, u32[]{:S(2)}, u32[]{:S(2)}) %all-to-all-start.1) | async-done | bytes 491552 | tf_op jit(solution)/shard_map/all_to_all | solution.py:196
  117.4 0.6 maximum_bitcast_fusion
  (42 shorter events, 2.1 us)
Async XLA Ops:
  3.0 14.1 %copy-start.1 = (bf16[256,1536]{1,0:T(8,128)(2,1)S(1)}, bf16[256,1536]{1,0:T(8,128)(2,1)}, u32[]{:S(2)}) copy-start(bf16[256,1536]{1,0:T(8,128)(2,1)} %param.8) | copy-start | bytes 2359300
  3.0 46.4 %all-to-all-start = ((bf16[16,32,1280]{2,1,0:T(8,128)(2,1)}), bf16[16,32,1280]{2,1,0:T(8,128)(2,1)S(1)}, u32[]{:S(2)}, u32[]{:S(2)}) async-start(bf16[16,32,1280]{2,1,0:T(8,128)(2,1)} %bitcast.69), calls=%async_computation | async-start | bytes 2621440 | tf_op jit(solution)/shard_map/all_to_all | solution.py:136
  17.4 3.6 %collective-permute-start = (bf16[8,32,768]{2,1,0:T(8,128)(2,1)S(1)}, bf16[8,32,768]{2,1,0:T(8,128)(2,1)S(1)}, u32[]{:S(2)}, u32[]{:S(2)}) collective-permute-start(bf16[8,32,768]{2,1,0:T(8,128)(2,1)S(1)} %bitcast.72), channel_id=1, source_target_pairs={{0,1},{1,0},{2,3},{3,2},{4,5},{5,4},{6,7},{7,6},{8,9},{9,8},{10,11... | collective-permute-start | bytes 1179656 | tf_op jit(solution)/shard_map/ppermute | solution.py:17
  49.9 11.5 %collective-permute-start.1 = (bf16[192,1280]{1,0:T(8,128)(2,1)S(1)}, bf16[192,1280]{1,0:T(8,128)(2,1)S(1)}, u32[]{:S(2)}, u32[]{:S(2)}) collective-permute-start(bf16[192,1280]{1,0:T(8,128)(2,1)S(1)} %convolution_convert_fusion.1), channel_id=1, source_target_pairs={{0,2},{1,25},{2,0},{3,27},{4,6},{5,29},{6,4},{7,31},{24,26},{25,1}... | collective-permute-start | bytes 1474568 | tf_op jit(solution)/shard_map/ppermute | solution.py:166
  58.7 12.4 %collective-permute-start.3 = (bf16[192,1280]{1,0:T(8,128)(2,1)}, bf16[192,1280]{1,0:T(8,128)(2,1)S(1)}, u32[]{:S(2)}, u32[]{:S(2)}) collective-permute-start(bf16[192,1280]{1,0:T(8,128)(2,1)} %convolution_convert_fusion), channel_id=1, source_target_pairs={{0,2},{1,25},{2,0},{3,27},{4,6},{5,29},{6,4},{7,31},{24,26},{25,1}... | collective-permute-start | bytes 1474568 | tf_op jit(solution)/shard_map/ppermute | solution.py:177
  61.3 1.3 %copy-start = (f32[384,1280]{1,0:T(8,128)}, f32[384,1280]{1,0:T(8,128)S(1)}, u32[]{:S(2)}) copy-start(f32[384,1280]{1,0:T(8,128)S(1)} %fusion.14) | copy-start | bytes 5898244
  61.3 5.4 %copy-start.3 = (f32[8,2,32,768]{3,2,1,0:T(8,128)S(1)}, f32[8,2,32,768]{3,2,1,0:T(8,128)}, u32[]{:S(2)}) copy-start(f32[8,2,32,768]{3,2,1,0:T(8,128)} %fusion) | copy-start | bytes 4718596
  61.4 9.6 %copy-start.5 = (s32[8]{0:T(128)S(1)}, s32[8]{0:T(128)}, u32[]{:S(2)}) copy-start(s32[8]{0:T(128)} %counts_ref.1) | copy-start | bytes 100
  62.7 12.8 %collective-permute-start.4 = (bf16[192,1280]{1,0:T(8,128)(2,1)S(1)}, bf16[192,1280]{1,0:T(8,128)(2,1)S(1)}, u32[]{:S(2)}, u32[]{:S(2)}) collective-permute-start(bf16[192,1280]{1,0:T(8,128)(2,1)S(1)} %add_convert_fusion.1), channel_id=1, source_target_pairs={{0,24},{1,3},{2,26},{3,1},{4,28},{5,7},{6,30},{7,5},{24,0},{25,27}... | collective-permute-start | bytes 1474568 | tf_op jit(solution)/shard_map/ppermute | solution.py:182
  67.7 26.1 %collective-permute-start.2 = (f32[8,32,768]{2,1,0:T(8,128)}, f32[8,32,768]{2,1,0:T(8,128)}, u32[]{:S(2)}, u32[]{:S(2)}) collective-permute-start(f32[8,32,768]{2,1,0:T(8,128)} %dynamic-slice_bitcast_fusion), channel_id=1, source_target_pairs={{0,1},{1,0},{2,3},{3,2},{4,5},{5,4},{6,7},{7,6},{8,9},{9,8},{10,11... | collective-permute-start | bytes 2359304 | tf_op jit(solution)/shard_map/ppermute | solution.py:17
  77.7 17.4 %copy-start.2 = (bf16[256,1536]{1,0:T(8,128)(2,1)S(1)}, bf16[256,1536]{1,0:T(8,128)(2,1)}, u32[]{:S(2)}) copy-start(bf16[256,1536]{1,0:T(8,128)(2,1)} %param.8) | copy-start | bytes 2359300
  77.7 39.6 %all-to-all-start.1 = ((bf16[24,8,1280]{2,1,0:T(8,128)(2,1)}), bf16[24,8,1280]{2,1,0:T(8,128)(2,1)S(1)}, u32[]{:S(2)}, u32[]{:S(2)}) async-start(bf16[24,8,1280]{2,1,0:T(8,128)(2,1)} %fusion.13), calls=%async_computation.1 | async-start | bytes 983040 | tf_op jit(solution)/shard_map/all_to_all | solution.py:196
  95.1 20.4 %copy-start.4 = (f32[256]{0:T(256)S(1)}, f32[256]{0:T(256)}, u32[]{:S(2)}) copy-start(f32[256]{0:T(256)} %param.6) | copy-start | bytes 3076
  95.8 8.5 %collective-permute-start.5 = (f32[4,32]{1,0:T(4,128)S(1)}, f32[4,32]{1,0:T(4,128)S(1)}, u32[]{:S(2)}, u32[]{:S(2)}) collective-permute-start(f32[4,32]{1,0:T(4,128)S(1)} %get-tuple-element.27), channel_id=1, source_target_pairs={{0,384},{384,0},{1,385},{385,1},{2,386},{386,2},{3,387},{387,3},{4... | collective-permute-start | bytes 1544 | tf_op jit(solution)/shard_map/ppermute | solution.py:17
  104.4 7.7 %collective-permute-start.6 = (f32[2,32]{1,0:T(2,128)S(1)}, f32[2,32]{1,0:T(2,128)S(1)}, u32[]{:S(2)}, u32[]{:S(2)}) collective-permute-start(f32[2,32]{1,0:T(2,128)S(1)} %bitcast.80), channel_id=1, source_target_pairs={{0,288},{96,0},{192,96},{288,192},{1,289},{97,1},{193,97},{289,193... | collective-permute-start | bytes 776 | tf_op jit(solution)/shard_map/ppermute | solution.py:36
  107.6 6.1 %collective-permute-start.7 = (f32[2,32]{1,0:T(2,128)S(1)}, f32[2,32]{1,0:T(2,128)S(1)}, u32[]{:S(2)}, u32[]{:S(2)}) collective-permute-start(f32[2,32]{1,0:T(2,128)S(1)} %bitcast.79), channel_id=1, source_target_pairs={{0,192},{96,288},{192,0},{288,96},{1,193},{97,289},{193,1},{289,97... | collective-permute-start | bytes 776 | tf_op jit(solution)/shard_map/ppermute | solution.py:36
  109.5 5.8 %collective-permute-start.8 = (f32[2,32]{1,0:T(2,128)S(1)}, f32[2,32]{1,0:T(2,128)S(1)}, u32[]{:S(2)}, u32[]{:S(2)}) collective-permute-start(f32[2,32]{1,0:T(2,128)S(1)} %bitcast.78), channel_id=1, source_target_pairs={{0,96},{96,192},{192,288},{288,0},{1,97},{97,193},{193,289},{289,1... | collective-permute-start | bytes 776 | tf_op jit(solution)/shard_map/ppermute | solution.py:36

commit v9 on v8

--- a/solution.py
+++ b/solution.py
@@ -180,7 +180,6 @@
     came_first, kept = lax.optimization_barrier((came_first, kept))
     passed = (kept[quarter:] + came_first.astype(jnp.float32)).astype(jnp.bfloat16)
     came = lax.ppermute(passed, CUBE, stage_pairs(1))
-    grad_partial, _ = lax.optimization_barrier((grad_partial, passed))
 
     grad_other = swap(pick(grad_partial, 1 - core, 1), "core")
     grad_hidden = (pick(grad_partial, core, 1) + grad_other).reshape(row_total, hidden_count)
@@ -189,6 +188,7 @@
     grad_rows = jnp.concatenate([grad_gate, grad_up], axis=1).astype(jnp.bfloat16)
     row_score = jnp.sum(grad_hidden * hidden_act.astype(jnp.float32), axis=1)
 
+    came_second, _ = lax.optimization_barrier((came_second, row_score))
     spread = (
         kept[:quarter] + came_second.astype(jnp.float32) + came.astype(jnp.float32)
     ).astype(jnp.bfloat16)

time: 119 us -> 129 us (1.084); the launches traced: 118 us -> 126 us
  waiting for transfers between devices: 40.8 us -> 52 us
  local copies, waits for them, and re-layouts: 4.94 us -> 0.78 us
  starting transfers between devices: 55.2 us -> 57.8 us
    all_to_all x1, waiting for transfers between devices: 1.21 us -> 20.7 us  [body(): lax.all_to_all(spread.reshape(-1, unit, half), REST, split_axis=0, concat...]
    ppermute x1, waiting for transfers between devices: 4.35 us -> 0.01 us  [body(): came = lax.ppermute(passed, CUBE, stage_pairs(1))]
    ppermute x3, waiting for transfers between devices: 3.3 us -> 0.01 us  [send_back(): lax.ppermute(part, 'x', [(i, (i + shift) % width) for i in range(width)])]
    ppermute x3, waiting for transfers between devices: 6.68 us -> 4 us  [swap(): return lax.ppermute(value, axis, [(0, 1), (1, 0)])]
    ppermute x3, starting transfers between devices: 7.65 us -> 9.9 us  [swap(): return lax.ppermute(value, axis, [(0, 1), (1, 0)])]
    all_to_all x1, waiting for transfers between devices: 25.3 us -> 27.3 us  [body(): lax.all_to_all(outgoing.reshape(expert_count * 2, capacity, half), EXPERT...]
  transfers between devices with their start and end apart: 11 -> 11, of which waited for: 7 -> 4; matrix products, arithmetic and copies ran while one was open for 13% -> 9% of each run, Pallas kernels for 1% -> 0%
where the time goes in v9:
time: 129 us; the launch traced here: 126 us
  starting transfers between devices  57.8 us (45%)
  waiting for transfers between devices  52 us (40%)
  other arithmetic  6.62 us (5%)
  matrix products  5.08 us (4%)
  Pallas kernels  2.99 us (2%)
    all_to_all x1, waiting for transfers between devices, body(): lax.all_to_all(outgoing.reshape(expert_count * 2, capacity, half), EXPERT...  27.3 us
    all_to_all x1, waiting for transfers between devices, body(): lax.all_to_all(spread.reshape(-1, unit, half), REST, split_axis=0, concat...  20.7 us
    all_to_all x1, starting transfers between devices, body(): lax.all_to_all(spread.reshape(-1, unit, half), REST, split_axis=0, concat...  16.8 us
    all_to_all x1, starting transfers between devices, body(): lax.all_to_all(outgoing.reshape(expert_count * 2, capacity, half), EXPERT...  14.1 us
    ppermute x3, starting transfers between devices, swap(): return lax.ppermute(value, axis, [(0, 1), (1, 0)])  9.9 us
    ppermute x3, starting transfers between devices, send_back(): lax.ppermute(part, 'x', [(i, (i + shift) % width) for i in range(width)])  7.5 us
    ppermute x3, waiting for transfers between devices, swap(): return lax.ppermute(value, axis, [(0, 1), (1, 0)])  4 us
    ppermute x1, starting transfers between devices, body(): came = lax.ppermute(passed, CUBE, stage_pairs(1))  3.76 us
  transfers between devices with their start and end apart: 11, of which 4 were waited for; matrix products, arithmetic and copies ran while one was open for 9% of the time, Pallas kernels for 0%

profile of v9, /device:TPU:1, one launch (start us, length us, event | category | flops | bytes accessed | tf_op | source)
XLA Modules:
  0.0 126.2 jit_solution(2118023905031026672)
XLA Ops:
  0.6 2.4 %shard_map.76 = bf16[8,2,32,1280]{3,2,1,0:T(8,128)(2,1)} custom-call(s32[8]{0:T(128)} %counts_ref.1, f32[1,256]{1,0:T(1,128)} %bitcast.76, bf16[256,2560]{1,0:T(8,128)(2,1)} %grad_ref.1), custom_call_target="tpu_custom_call" | custom-call | flops 655360 | bytes 2621440 | tf_op jit(solution)/shard_map/pallas_call | solution.py:108
  3.0 14.1 %all-to-all-start = ((bf16[16,32,1280]{2,1,0:T(8,128)(2,1)}), bf16[16,32,1280]{2,1,0:T(8,128)(2,1)S(1)}, u32[]{:S(2)}, u32[]{:S(2)}) async-start(bf16[16,32,1280]{2,1,0:T(8,128)(2,1)} %bitcast.69), calls=%async_computation | async-start | bytes 2621440 | tf_op jit(solution)/shard_map/all_to_all | solution.py:136
  17.2 0.3 fusion.3
  17.4 2.1 %collective-permute-start = (bf16[8,32,768]{2,1,0:T(8,128)(2,1)S(1)}, bf16[8,32,768]{2,1,0:T(8,128)(2,1)S(1)}, u32[]{:S(2)}, u32[]{:S(2)}) collective-permute-start(bf16[8,32,768]{2,1,0:T(8,128)(2,1)S(1)} %bitcast.72), channel_id=1, source_target_pairs={{0,1},{1,0},{2,3},{3,2},{4,5},{5,4},{6,7},{7,6},{8,9},{9,8},{10,11... | collective-permute-start | bytes 1179656 | tf_op jit(solution)/shard_map/ppermute | solution.py:17
  19.7 0.1 lt.113
  19.8 1.2 collective-permute-done
  21.2 0.3 copy.13
  21.5 0.6 shard_map.77
  22.1 27.3 %all-to-all-done = bf16[16,32,1280]{2,1,0:T(8,128)(2,1)S(1)} async-done(((bf16[16,32,1280]{2,1,0:T(8,128)(2,1)}), bf16[16,32,1280]{2,1,0:T(8,128)(2,1)S(1)}, u32[]{:S(2)}, u32[]{:S(2)}) %all-to-all-start) | async-done | bytes 1310752 | tf_op jit(solution)/shard_map/all_to_all | solution.py:136
  49.4 0.4 convolution_convert_fusion.1
  49.9 3.7 %collective-permute-start.2 = (bf16[192,1280]{1,0:T(8,128)(2,1)S(1)}, bf16[192,1280]{1,0:T(8,128)(2,1)S(1)}, u32[]{:S(2)}, u32[]{:S(2)}) collective-permute-start(bf16[192,1280]{1,0:T(8,128)(2,1)S(1)} %convolution_convert_fusion.1), channel_id=1, source_target_pairs={{0,2},{1,25},{2,0},{3,27},{4,6},{5,29},{6,4},{7,31},{24,26},{25,1}... | collective-permute-start | bytes 1474568 | tf_op jit(solution)/shard_map/ppermute | solution.py:166
  53.6 2.8 %fusion = f32[8,2,32,768]{3,2,1,0:T(8,128)S(1)} fusion(bf16[8,2,32,1280]{3,2,1,0:T(8,128)(2,1)S(1)} %bitcast.66, bf16[1,768,2560]{2,1,0:T(8,128)(2,1)} %param.9, s32[]{:T(128)S(6)} %select_n.166), kind=kOutput, calls=%fused_computation.2 | convolution fusion | flops 1006632960 | bytes 4849668 | tf_op jit(solution)/shard_map/dot_general | solution.py:171
  56.4 1.2 convolution_convert_fusion
  57.6 1.9 %collective-permute-start.3 = (bf16[192,1280]{1,0:T(8,128)(2,1)}, bf16[192,1280]{1,0:T(8,128)(2,1)S(1)}, u32[]{:S(2)}, u32[]{:S(2)}) collective-permute-start(bf16[192,1280]{1,0:T(8,128)(2,1)} %convolution_convert_fusion), channel_id=1, source_target_pairs={{0,2},{1,25},{2,0},{3,27},{4,6},{5,29},{6,4},{7,31},{24,26},{25,1}... | collective-permute-start | bytes 1474568 | tf_op jit(solution)/shard_map/ppermute | solution.py:177
  59.6 3.2 %collective-permute-start.1 = (f32[8,32,768]{2,1,0:T(8,128)S(1)}, f32[8,32,768]{2,1,0:T(8,128)S(1)}, u32[]{:S(2)}, u32[]{:S(2)}) collective-permute-start(f32[8,32,768]{2,1,0:T(8,128)S(1)} %dynamic-slice_bitcast_fusion), channel_id=1, source_target_pairs={{0,1},{1,0},{2,3},{3,2},{4,5},{5,4},{6,7},{7,6},{8,9},{9,8},{10,11... | collective-permute-start | bytes 2359304 | tf_op jit(solution)/shard_map/ppermute | solution.py:17
  62.8 0.7 fusion.14
  63.5 1.0 add_convert_fusion.1
  64.5 3.8 %collective-permute-start.4 = (bf16[192,1280]{1,0:T(8,128)(2,1)}, bf16[192,1280]{1,0:T(8,128)(2,1)S(1)}, u32[]{:S(2)}, u32[]{:S(2)}) collective-permute-start(bf16[192,1280]{1,0:T(8,128)(2,1)} %add_convert_fusion.1), channel_id=1, source_target_pairs={{0,24},{1,3},{2,26},{3,1},{4,28},{5,7},{6,30},{7,5},{24,0},{25,27}... | collective-permute-start | bytes 1474568 | tf_op jit(solution)/shard_map/ppermute | solution.py:182
  68.3 0.1 bitcast_add_fusion
  68.4 0.6 fusion.6
  69.0 0.1 reshape_reshape.7
  69.1 4.6 %collective-permute-start.5 = (f32[4,32]{1,0:T(4,128)S(1)}, f32[4,32]{1,0:T(4,128)S(1)}, u32[]{:S(2)}, u32[]{:S(2)}) collective-permute-start(f32[4,32]{1,0:T(4,128)S(1)} %get-tuple-element.27), channel_id=1, source_target_pairs={{0,384},{384,0},{1,385},{385,1},{2,386},{386,2},{3,387},{387,3},{4... | collective-permute-start | bytes 1544 | tf_op jit(solution)/shard_map/ppermute | solution.py:17
  73.7 0.9 pad_maximum_fusion.1
  74.6 2.8 %collective-permute-done.5 = f32[4,32]{1,0:T(4,128)S(1)} collective-permute-done((f32[4,32]{1,0:T(4,128)S(1)}, f32[4,32]{1,0:T(4,128)S(1)}, u32[]{:S(2)}, u32[]{:S(2)}) %collective-permute-start.5) | collective-permute-done | bytes 544 | tf_op jit(solution)/shard_map/ppermute | solution.py:17
  77.5 3.1 %collective-permute-start.6 = (f32[2,32]{1,0:T(2,128)S(1)}, f32[2,32]{1,0:T(2,128)S(1)}, u32[]{:S(2)}, u32[]{:S(2)}) collective-permute-start(f32[2,32]{1,0:T(2,128)S(1)} %bitcast.80), channel_id=1, source_target_pairs={{0,288},{96,0},{192,96},{288,192},{1,289},{97,1},{193,97},{289,193... | collective-permute-start | bytes 776 | tf_op jit(solution)/shard_map/ppermute | solution.py:36
  80.6 1.9 %collective-permute-start.7 = (f32[2,32]{1,0:T(2,128)S(1)}, f32[2,32]{1,0:T(2,128)S(1)}, u32[]{:S(2)}, u32[]{:S(2)}) collective-permute-start(f32[2,32]{1,0:T(2,128)S(1)} %bitcast.79), channel_id=1, source_target_pairs={{0,192},{96,288},{192,0},{288,96},{1,193},{97,289},{193,1},{289,97... | collective-permute-start | bytes 776 | tf_op jit(solution)/shard_map/ppermute | solution.py:36
  82.5 2.5 %collective-permute-start.8 = (f32[2,32]{1,0:T(2,128)S(1)}, f32[2,32]{1,0:T(2,128)S(1)}, u32[]{:S(2)}, u32[]{:S(2)}) collective-permute-start(f32[2,32]{1,0:T(2,128)S(1)} %bitcast.78), channel_id=1, source_target_pairs={{0,96},{96,192},{192,288},{288,0},{1,97},{97,193},{193,289},{289,1... | collective-permute-start | bytes 776 | tf_op jit(solution)/shard_map/ppermute | solution.py:36
  85.1 2.1 %fusion.13 = bf16[24,8,1280]{2,1,0:T(8,128)(2,1)} fusion(bf16[192,1280]{1,0:T(8,128)(2,1)S(1)} %collective-permute-done.4, bf16[192,1280]{1,0:T(8,128)(2,1)S(1)} %collective-permute-done.3, f32[384,1280]{1,0:T(8,128)} %copy-done), kind=kLoop, calls=%fused_computation.29 | loop fusion | flops 1228800 | bytes 2457600 | tf_op jit(solution)/shard_map/reshape | solution.py:197
  87.2 16.8 %all-to-all-start.1 = ((bf16[24,8,1280]{2,1,0:T(8,128)(2,1)}), bf16[24,8,1280]{2,1,0:T(8,128)(2,1)S(1)}, u32[]{:S(2)}, u32[]{:S(2)}) async-start(bf16[24,8,1280]{2,1,0:T(8,128)(2,1)} %fusion.13), calls=%async_computation.1 | async-start | bytes 983040 | tf_op jit(solution)/shard_map/all_to_all | solution.py:196
  104.2 0.6 select_divide_fusion
  104.8 20.7 %all-to-all-done.1 = bf16[24,8,1280]{2,1,0:T(8,128)(2,1)S(1)} async-done(((bf16[24,8,1280]{2,1,0:T(8,128)(2,1)}), bf16[24,8,1280]{2,1,0:T(8,128)(2,1)S(1)}, u32[]{:S(2)}, u32[]{:S(2)}) %all-to-all-start.1) | async-done | bytes 491552 | tf_op jit(solution)/shard_map/all_to_all | solution.py:196
  125.6 0.6 maximum_bitcast_fusion
  (40 shorter events, 0.7 us)
Async XLA Ops:
  3.0 14.1 %copy-start.1 = (bf16[256,1536]{1,0:T(8,128)(2,1)S(1)}, bf16[256,1536]{1,0:T(8,128)(2,1)}, u32[]{:S(2)}) copy-start(bf16[256,1536]{1,0:T(8,128)(2,1)} %param.8) | copy-start | bytes 2359300
  3.0 16.6 %copy-start.4 = (s32[8]{0:T(128)S(1)}, s32[8]{0:T(128)}, u32[]{:S(2)}) copy-start(s32[8]{0:T(128)} %counts_ref.1) | copy-start | bytes 100
  3.0 46.4 %all-to-all-start = ((bf16[16,32,1280]{2,1,0:T(8,128)(2,1)}), bf16[16,32,1280]{2,1,0:T(8,128)(2,1)S(1)}, u32[]{:S(2)}, u32[]{:S(2)}) async-start(bf16[16,32,1280]{2,1,0:T(8,128)(2,1)} %bitcast.69), calls=%async_computation | async-start | bytes 2621440 | tf_op jit(solution)/shard_map/all_to_all | solution.py:136
  17.4 3.6 %collective-permute-start = (bf16[8,32,768]{2,1,0:T(8,128)(2,1)S(1)}, bf16[8,32,768]{2,1,0:T(8,128)(2,1)S(1)}, u32[]{:S(2)}, u32[]{:S(2)}) collective-permute-start(bf16[8,32,768]{2,1,0:T(8,128)(2,1)S(1)} %bitcast.72), channel_id=1, source_target_pairs={{0,1},{1,0},{2,3},{3,2},{4,5},{5,4},{6,7},{7,6},{8,9},{9,8},{10,11... | collective-permute-start | bytes 1179656 | tf_op jit(solution)/shard_map/ppermute | solution.py:17
  49.9 13.6 %collective-permute-start.2 = (bf16[192,1280]{1,0:T(8,128)(2,1)S(1)}, bf16[192,1280]{1,0:T(8,128)(2,1)S(1)}, u32[]{:S(2)}, u32[]{:S(2)}) collective-permute-start(bf16[192,1280]{1,0:T(8,128)(2,1)S(1)} %convolution_convert_fusion.1), channel_id=1, source_target_pairs={{0,2},{1,25},{2,0},{3,27},{4,6},{5,29},{6,4},{7,31},{24,26},{25,1}... | collective-permute-start | bytes 1474568 | tf_op jit(solution)/shard_map/ppermute | solution.py:166
  57.6 17.1 %collective-permute-start.3 = (bf16[192,1280]{1,0:T(8,128)(2,1)}, bf16[192,1280]{1,0:T(8,128)(2,1)S(1)}, u32[]{:S(2)}, u32[]{:S(2)}) collective-permute-start(bf16[192,1280]{1,0:T(8,128)(2,1)} %convolution_convert_fusion), channel_id=1, source_target_pairs={{0,2},{1,25},{2,0},{3,27},{4,6},{5,29},{6,4},{7,31},{24,26},{25,1}... | collective-permute-start | bytes 1474568 | tf_op jit(solution)/shard_map/ppermute | solution.py:177
  59.6 8.7 %collective-permute-start.1 = (f32[8,32,768]{2,1,0:T(8,128)S(1)}, f32[8,32,768]{2,1,0:T(8,128)S(1)}, u32[]{:S(2)}, u32[]{:S(2)}) collective-permute-start(f32[8,32,768]{2,1,0:T(8,128)S(1)} %dynamic-slice_bitcast_fusion), channel_id=1, source_target_pairs={{0,1},{1,0},{2,3},{3,2},{4,5},{5,4},{6,7},{7,6},{8,9},{9,8},{10,11... | collective-permute-start | bytes 2359304 | tf_op jit(solution)/shard_map/ppermute | solution.py:17
  63.4 4.9 %copy-start = (f32[384,1280]{1,0:T(8,128)}, f32[384,1280]{1,0:T(8,128)S(1)}, u32[]{:S(2)}) copy-start(f32[384,1280]{1,0:T(8,128)S(1)} %fusion.14) | copy-start | bytes 5898244
  64.5 3.9 %copy-start.2 = (bf16[256,1536]{1,0:T(8,128)(2,1)S(1)}, bf16[256,1536]{1,0:T(8,128)(2,1)}, u32[]{:S(2)}) copy-start(bf16[256,1536]{1,0:T(8,128)(2,1)} %param.8) | copy-start | bytes 2359300
  64.5 20.6 %collective-permute-start.4 = (bf16[192,1280]{1,0:T(8,128)(2,1)}, bf16[192,1280]{1,0:T(8,128)(2,1)S(1)}, u32[]{:S(2)}, u32[]{:S(2)}) collective-permute-start(bf16[192,1280]{1,0:T(8,128)(2,1)} %add_convert_fusion.1), channel_id=1, source_target_pairs={{0,24},{1,3},{2,26},{3,1},{4,28},{5,7},{6,30},{7,5},{24,0},{25,27}... | collective-permute-start | bytes 1474568 | tf_op jit(solution)/shard_map/ppermute | solution.py:182
  69.1 8.3 %collective-permute-start.5 = (f32[4,32]{1,0:T(4,128)S(1)}, f32[4,32]{1,0:T(4,128)S(1)}, u32[]{:S(2)}, u32[]{:S(2)}) collective-permute-start(f32[4,32]{1,0:T(4,128)S(1)} %get-tuple-element.27), channel_id=1, source_target_pairs={{0,384},{384,0},{1,385},{385,1},{2,386},{386,2},{3,387},{387,3},{4... | collective-permute-start | bytes 1544 | tf_op jit(solution)/shard_map/ppermute | solution.py:17
  77.5 7.5 %collective-permute-start.6 = (f32[2,32]{1,0:T(2,128)S(1)}, f32[2,32]{1,0:T(2,128)S(1)}, u32[]{:S(2)}, u32[]{:S(2)}) collective-permute-start(f32[2,32]{1,0:T(2,128)S(1)} %bitcast.80), channel_id=1, source_target_pairs={{0,288},{96,0},{192,96},{288,192},{1,289},{97,1},{193,97},{289,193... | collective-permute-start | bytes 776 | tf_op jit(solution)/shard_map/ppermute | solution.py:36
  80.6 23.4 %collective-permute-start.7 = (f32[2,32]{1,0:T(2,128)S(1)}, f32[2,32]{1,0:T(2,128)S(1)}, u32[]{:S(2)}, u32[]{:S(2)}) collective-permute-start(f32[2,32]{1,0:T(2,128)S(1)} %bitcast.79), channel_id=1, source_target_pairs={{0,192},{96,288},{192,0},{288,96},{1,193},{97,289},{193,1},{289,97... | collective-permute-start | bytes 776 | tf_op jit(solution)/shard_map/ppermute | solution.py:36
  82.5 21.5 %collective-permute-start.8 = (f32[2,32]{1,0:T(2,128)S(1)}, f32[2,32]{1,0:T(2,128)S(1)}, u32[]{:S(2)}, u32[]{:S(2)}) collective-permute-start(f32[2,32]{1,0:T(2,128)S(1)} %bitcast.78), channel_id=1, source_target_pairs={{0,96},{96,192},{192,288},{288,0},{1,97},{97,193},{193,289},{289,1... | collective-permute-start | bytes 776 | tf_op jit(solution)/shard_map/ppermute | solution.py:36
  85.0 19.2 %copy-start.3 = (f32[256]{0:T(256)S(1)}, f32[256]{0:T(256)}, u32[]{:S(2)}) copy-start(f32[256]{0:T(256)} %param.6) | copy-start | bytes 3076
  87.2 38.3 %all-to-all-start.1 = ((bf16[24,8,1280]{2,1,0:T(8,128)(2,1)}), bf16[24,8,1280]{2,1,0:T(8,128)(2,1)S(1)}, u32[]{:S(2)}, u32[]{:S(2)}) async-start(bf16[24,8,1280]{2,1,0:T(8,128)(2,1)} %fusion.13), calls=%async_computation.1 | async-start | bytes 983040 | tf_op jit(solution)/shard_map/all_to_all | solution.py:196

commit v10 on v7

--- a/solution.py
+++ b/solution.py
@@ -103,7 +103,7 @@
     expert_count = counts.shape[0]
     capacity = row_total // expert_count
     half = feature_count // 2
-    blocks = 2
+    blocks = expert_count // 2
     return pl.pallas_call(
         scale_kernel,
         grid=(expert_count // blocks,),

time: 116 us -> 115 us (level)
  Pallas kernels: 4.34 us -> 2.99 us
    pallas_call x1, Pallas kernels: 3.74 us -> 2.38 us  [scale(): pl.pallas_call(scale_kernel, grid=(expert_count // blocks,), out_shape=ja...]
where the time goes in v10:
time: 115 us; the launch traced here: 114 us
  starting transfers between devices  55.5 us (48%)
  waiting for transfers between devices  41.5 us (36%)
  other arithmetic  4.49 us (4%)
  matrix products  4.29 us (4%)
  local copies, waits for them, and re-layouts  4.01 us (3%)
  Pallas kernels  2.99 us (3%)
    all_to_all x1, waiting for transfers between devices, body(): lax.all_to_all(outgoing.reshape(expert_count * 2, capacity, half), EXPERT...  25.3 us
    all_to_all x1, starting transfers between devices, body(): lax.all_to_all(spread.reshape(-1, unit, half), REST, split_axis=0, concat...  16.3 us
    all_to_all x1, starting transfers between devices, body(): lax.all_to_all(outgoing.reshape(expert_count * 2, capacity, half), EXPERT...  14.1 us
    ppermute x3, starting transfers between devices, send_back(): lax.ppermute(part, 'x', [(i, (i + shift) % width) for i in range(width)])  7.97 us
    ppermute x3, starting transfers between devices, swap(): return lax.ppermute(value, axis, [(0, 1), (1, 0)])  7.66 us
    ppermute x3, waiting for transfers between devices, swap(): return lax.ppermute(value, axis, [(0, 1), (1, 0)])  7.1 us
    ppermute x1, waiting for transfers between devices, body(): came = lax.ppermute(passed, CUBE, stage_pairs(1))  6.03 us
    ppermute x1, starting transfers between devices, body(): came = lax.ppermute(passed, CUBE, stage_pairs(1))  3.77 us
  transfers between devices with their start and end apart: 11, of which 6 were waited for; matrix products, arithmetic and copies ran while one was open for 9% of the time, Pallas kernels for 1%

profile of v10, /device:TPU:1, one launch (start us, length us, event | category | flops | bytes accessed | tf_op | source)
XLA Modules:
  0.0 113.7 jit_solution(3560365292732419644)
XLA Ops:
  0.6 2.4 %shard_map.76 = bf16[8,2,32,1280]{3,2,1,0:T(8,128)(2,1)} custom-call(s32[8]{0:T(128)} %counts_ref.1, f32[1,256]{1,0:T(1,128)} %bitcast.65, bf16[256,2560]{1,0:T(8,128)(2,1)} %grad_ref.1), custom_call_target="tpu_custom_call" | custom-call | flops 655360 | bytes 2621440 | tf_op jit(solution)/shard_map/pallas_call | solution.py:107
  3.0 14.1 %all-to-all-start = ((bf16[16,32,1280]{2,1,0:T(8,128)(2,1)}), bf16[16,32,1280]{2,1,0:T(8,128)(2,1)S(1)}, u32[]{:S(2)}, u32[]{:S(2)}) async-start(bf16[16,32,1280]{2,1,0:T(8,128)(2,1)} %bitcast.60), calls=%async_computation | async-start | bytes 2621440 | tf_op jit(solution)/shard_map/all_to_all | solution.py:135
  17.2 0.3 fusion.3
  17.4 2.1 %collective-permute-start = (bf16[8,32,768]{2,1,0:T(8,128)(2,1)S(1)}, bf16[8,32,768]{2,1,0:T(8,128)(2,1)S(1)}, u32[]{:S(2)}, u32[]{:S(2)}) collective-permute-start(bf16[8,32,768]{2,1,0:T(8,128)(2,1)S(1)} %bitcast.63), channel_id=1, source_target_pairs={{0,1},{1,0},{2,3},{3,2},{4,5},{5,4},{6,7},{7,6},{8,9},{9,8},{10,11... | collective-permute-start | bytes 1179656 | tf_op jit(solution)/shard_map/ppermute | solution.py:17
  19.6 1.4 %collective-permute-done = bf16[8,32,768]{2,1,0:T(8,128)(2,1)S(1)} collective-permute-done((bf16[8,32,768]{2,1,0:T(8,128)(2,1)S(1)}, bf16[8,32,768]{2,1,0:T(8,128)(2,1)S(1)}, u32[]{:S(2)}, u32[]{:S(2)}) %collective-permute-start) | collective-permute-done | bytes 393248 | tf_op jit(solution)/shard_map/ppermute | solution.py:17
  21.2 0.9 copy.12
  22.1 1.4 %copy.13 = bf16[512,768]{0,1:T(8,128)(2,1)S(1)} copy(bf16[512,768]{1,0:T(8,128)(2,1)} %bitcast.61) | data formatting | bytes 1572864 | tf_op jit(solution)/shard_map/reshape | solution.py:154
  23.5 0.6 shard_map.77
  24.1 25.3 %all-to-all-done = bf16[16,32,1280]{2,1,0:T(8,128)(2,1)S(1)} async-done(((bf16[16,32,1280]{2,1,0:T(8,128)(2,1)}), bf16[16,32,1280]{2,1,0:T(8,128)(2,1)S(1)}, u32[]{:S(2)}, u32[]{:S(2)}) %all-to-all-start) | async-done | bytes 1310752 | tf_op jit(solution)/shard_map/all_to_all | solution.py:135
  49.4 0.4 convolution_convert_fusion.1
  49.9 3.7 %collective-permute-start.2 = (bf16[192,1280]{1,0:T(8,128)(2,1)S(1)}, bf16[192,1280]{1,0:T(8,128)(2,1)S(1)}, u32[]{:S(2)}, u32[]{:S(2)}) collective-permute-start(bf16[192,1280]{1,0:T(8,128)(2,1)S(1)} %convolution_convert_fusion.1), channel_id=1, source_target_pairs={{0,2},{1,25},{2,0},{3,27},{4,6},{5,29},{6,4},{7,31},{24,26},{25,1}... | collective-permute-start | bytes 1474568 | tf_op jit(solution)/shard_map/ppermute | solution.py:165
  53.6 2.8 %fusion = f32[8,2,32,768]{3,2,1,0:T(8,128)S(1)} fusion(bf16[8,2,32,1280]{3,2,1,0:T(8,128)(2,1)S(1)} %bitcast.57, bf16[1,768,2560]{2,1,0:T(8,128)(2,1)} %param.9, s32[]{:T(128)S(6)} %select_n.190), kind=kOutput, calls=%fused_computation.2 | convolution fusion | flops 1006632960 | bytes 4849668 | tf_op jit(solution)/shard_map/dot_general | solution.py:170
  56.4 0.4 convolution_convert_fusion
  56.8 1.9 %collective-permute-start.3 = (bf16[192,1280]{1,0:T(8,128)(2,1)S(1)}, bf16[192,1280]{1,0:T(8,128)(2,1)S(1)}, u32[]{:S(2)}, u32[]{:S(2)}) collective-permute-start(bf16[192,1280]{1,0:T(8,128)(2,1)S(1)} %convolution_convert_fusion), channel_id=1, source_target_pairs={{0,2},{1,25},{2,0},{3,27},{4,6},{5,29},{6,4},{7,31},{24,26},{25,1}... | collective-permute-start | bytes 1474568 | tf_op jit(solution)/shard_map/ppermute | solution.py:176
  58.8 3.2 %collective-permute-start.1 = (f32[8,32,768]{2,1,0:T(8,128)S(1)}, f32[8,32,768]{2,1,0:T(8,128)S(1)}, u32[]{:S(2)}, u32[]{:S(2)}) collective-permute-start(f32[8,32,768]{2,1,0:T(8,128)S(1)} %dynamic-slice_bitcast_fusion), channel_id=1, source_target_pairs={{0,1},{1,0},{2,3},{3,2},{4,5},{5,4},{6,7},{7,6},{8,9},{9,8},{10,11... | collective-permute-start | bytes 2359304 | tf_op jit(solution)/shard_map/ppermute | solution.py:17
  62.0 0.7 fusion.14
  62.8 3.8 %collective-permute-start.4 = (bf16[192,1280]{1,0:T(8,128)(2,1)S(1)}, bf16[192,1280]{1,0:T(8,128)(2,1)S(1)}, u32[]{:S(2)}, u32[]{:S(2)}) collective-permute-start(bf16[192,1280]{1,0:T(8,128)(2,1)S(1)} %add_convert_fusion.1), channel_id=1, source_target_pairs={{0,24},{1,3},{2,26},{3,1},{4,28},{5,7},{6,30},{7,5},{24,0},{25,27}... | collective-permute-start | bytes 1474568 | tf_op jit(solution)/shard_map/ppermute | solution.py:181
  66.6 0.1 bitcast_add_fusion
  66.7 0.6 fusion.6
  67.3 6.0 %collective-permute-done.4 = bf16[192,1280]{1,0:T(8,128)(2,1)S(1)} collective-permute-done((bf16[192,1280]{1,0:T(8,128)(2,1)S(1)}, bf16[192,1280]{1,0:T(8,128)(2,1)S(1)}, u32[]{:S(2)}, u32[]{:S(2)}) %collective-permute-start.4) | collective-permute-done | bytes 491552 | tf_op jit(solution)/shard_map/ppermute | solution.py:181
  73.4 0.9 fusion.13
  74.3 16.3 %all-to-all-start.1 = ((bf16[24,8,1280]{2,1,0:T(8,128)(2,1)}), bf16[24,8,1280]{2,1,0:T(8,128)(2,1)S(1)}, u32[]{:S(2)}, u32[]{:S(2)}) async-start(bf16[24,8,1280]{2,1,0:T(8,128)(2,1)} %fusion.13), calls=%async_computation.1 | async-start | bytes 983040 | tf_op jit(solution)/shard_map/all_to_all | solution.py:195
  92.0 2.3 %collective-permute-start.5 = (f32[4,32]{1,0:T(4,128)S(1)}, f32[4,32]{1,0:T(4,128)S(1)}, u32[]{:S(2)}, u32[]{:S(2)}) collective-permute-start(f32[4,32]{1,0:T(4,128)S(1)} %get-tuple-element.27), channel_id=1, source_target_pairs={{0,384},{384,0},{1,385},{385,1},{2,386},{386,2},{3,387},{387,3},{4... | collective-permute-start | bytes 1544 | tf_op jit(solution)/shard_map/ppermute | solution.py:17
  94.4 0.9 pad_maximum_fusion.1
  95.3 5.7 %collective-permute-done.5 = f32[4,32]{1,0:T(4,128)S(1)} collective-permute-done((f32[4,32]{1,0:T(4,128)S(1)}, f32[4,32]{1,0:T(4,128)S(1)}, u32[]{:S(2)}, u32[]{:S(2)}) %collective-permute-start.5) | collective-permute-done | bytes 544 | tf_op jit(solution)/shard_map/ppermute | solution.py:17
  101.0 3.6 %collective-permute-start.6 = (f32[2,32]{1,0:T(2,128)S(1)}, f32[2,32]{1,0:T(2,128)S(1)}, u32[]{:S(2)}, u32[]{:S(2)}) collective-permute-start(f32[2,32]{1,0:T(2,128)S(1)} %bitcast.70), channel_id=1, source_target_pairs={{0,288},{96,0},{192,96},{288,192},{1,289},{97,1},{193,97},{289,193... | collective-permute-start | bytes 776 | tf_op jit(solution)/shard_map/ppermute | solution.py:37
  104.6 1.9 %collective-permute-start.7 = (f32[2,32]{1,0:T(2,128)S(1)}, f32[2,32]{1,0:T(2,128)S(1)}, u32[]{:S(2)}, u32[]{:S(2)}) collective-permute-start(f32[2,32]{1,0:T(2,128)S(1)} %bitcast.69), channel_id=1, source_target_pairs={{0,192},{96,288},{192,0},{288,96},{1,193},{97,289},{193,1},{289,97... | collective-permute-start | bytes 776 | tf_op jit(solution)/shard_map/ppermute | solution.py:37
  106.5 2.5 %collective-permute-start.8 = (f32[2,32]{1,0:T(2,128)S(1)}, f32[2,32]{1,0:T(2,128)S(1)}, u32[]{:S(2)}, u32[]{:S(2)}) collective-permute-start(f32[2,32]{1,0:T(2,128)S(1)} %bitcast.68), channel_id=1, source_target_pairs={{0,96},{96,192},{192,288},{288,0},{1,97},{97,193},{193,289},{289,1... | collective-permute-start | bytes 776 | tf_op jit(solution)/shard_map/ppermute | solution.py:37
  109.2 1.2 %collective-permute-done.7 = f32[2,32]{1,0:T(2,128)S(1)} collective-permute-done((f32[2,32]{1,0:T(2,128)S(1)}, f32[2,32]{1,0:T(2,128)S(1)}, u32[]{:S(2)}, u32[]{:S(2)}) %collective-permute-start.7) | collective-permute-done | bytes 288 | tf_op jit(solution)/shard_map/ppermute | solution.py:37
  110.5 1.8 %collective-permute-done.8 = f32[2,32]{1,0:T(2,128)S(1)} collective-permute-done((f32[2,32]{1,0:T(2,128)S(1)}, f32[2,32]{1,0:T(2,128)S(1)}, u32[]{:S(2)}, u32[]{:S(2)}) %collective-permute-start.8) | collective-permute-done | bytes 288 | tf_op jit(solution)/shard_map/ppermute | solution.py:37
  112.4 0.6 select_divide_fusion
  113.1 0.6 maximum_bitcast_fusion
  (55 shorter events, 2.1 us)
Async XLA Ops:
  3.0 14.1 %copy-start = (bf16[256,1536]{1,0:T(8,128)(2,1)S(1)}, bf16[256,1536]{1,0:T(8,128)(2,1)}, u32[]{:S(2)}) copy-start(bf16[256,1536]{1,0:T(8,128)(2,1)} %param.8) | copy-start | bytes 2359300
  3.0 46.4 %all-to-all-start = ((bf16[16,32,1280]{2,1,0:T(8,128)(2,1)}), bf16[16,32,1280]{2,1,0:T(8,128)(2,1)S(1)}, u32[]{:S(2)}, u32[]{:S(2)}) async-start(bf16[16,32,1280]{2,1,0:T(8,128)(2,1)} %bitcast.60), calls=%async_computation | async-start | bytes 2621440 | tf_op jit(solution)/shard_map/all_to_all | solution.py:135
  17.4 3.6 %collective-permute-start = (bf16[8,32,768]{2,1,0:T(8,128)(2,1)S(1)}, bf16[8,32,768]{2,1,0:T(8,128)(2,1)S(1)}, u32[]{:S(2)}, u32[]{:S(2)}) collective-permute-start(bf16[8,32,768]{2,1,0:T(8,128)(2,1)S(1)} %bitcast.63), channel_id=1, source_target_pairs={{0,1},{1,0},{2,3},{3,2},{4,5},{5,4},{6,7},{7,6},{8,9},{9,8},{10,11... | collective-permute-start | bytes 1179656 | tf_op jit(solution)/shard_map/ppermute | solution.py:17
  49.9 12.8 %collective-permute-start.2 = (bf16[192,1280]{1,0:T(8,128)(2,1)S(1)}, bf16[192,1280]{1,0:T(8,128)(2,1)S(1)}, u32[]{:S(2)}, u32[]{:S(2)}) collective-permute-start(bf16[192,1280]{1,0:T(8,128)(2,1)S(1)} %convolution_convert_fusion.1), channel_id=1, source_target_pairs={{0,2},{1,25},{2,0},{3,27},{4,6},{5,29},{6,4},{7,31},{24,26},{25,1}... | collective-permute-start | bytes 1474568 | tf_op jit(solution)/shard_map/ppermute | solution.py:165
  56.8 10.5 %collective-permute-start.3 = (bf16[192,1280]{1,0:T(8,128)(2,1)S(1)}, bf16[192,1280]{1,0:T(8,128)(2,1)S(1)}, u32[]{:S(2)}, u32[]{:S(2)}) collective-permute-start(bf16[192,1280]{1,0:T(8,128)(2,1)S(1)} %convolution_convert_fusion), channel_id=1, source_target_pairs={{0,2},{1,25},{2,0},{3,27},{4,6},{5,29},{6,4},{7,31},{24,26},{25,1}... | collective-permute-start | bytes 1474568 | tf_op jit(solution)/shard_map/ppermute | solution.py:176
  58.8 7.8 %collective-permute-start.1 = (f32[8,32,768]{2,1,0:T(8,128)S(1)}, f32[8,32,768]{2,1,0:T(8,128)S(1)}, u32[]{:S(2)}, u32[]{:S(2)}) collective-permute-start(f32[8,32,768]{2,1,0:T(8,128)S(1)} %dynamic-slice_bitcast_fusion), channel_id=1, source_target_pairs={{0,1},{1,0},{2,3},{3,2},{4,5},{5,4},{6,7},{7,6},{8,9},{9,8},{10,11... | collective-permute-start | bytes 2359304 | tf_op jit(solution)/shard_map/ppermute | solution.py:17
  62.8 3.9 %copy-start.1 = (bf16[256,1536]{1,0:T(8,128)(2,1)S(1)}, bf16[256,1536]{1,0:T(8,128)(2,1)}, u32[]{:S(2)}) copy-start(bf16[256,1536]{1,0:T(8,128)(2,1)} %param.8) | copy-start | bytes 2359300
  62.8 10.6 %collective-permute-start.4 = (bf16[192,1280]{1,0:T(8,128)(2,1)S(1)}, bf16[192,1280]{1,0:T(8,128)(2,1)S(1)}, u32[]{:S(2)}, u32[]{:S(2)}) collective-permute-start(bf16[192,1280]{1,0:T(8,128)(2,1)S(1)} %add_convert_fusion.1), channel_id=1, source_target_pairs={{0,24},{1,3},{2,26},{3,1},{4,28},{5,7},{6,30},{7,5},{24,0},{25,27}... | collective-permute-start | bytes 1474568 | tf_op jit(solution)/shard_map/ppermute | solution.py:181
  67.3 24.4 %copy-start.3 = (s32[8]{0:T(128)S(1)}, s32[8]{0:T(128)}, u32[]{:S(2)}) copy-start(s32[8]{0:T(128)} %counts_ref.1) | copy-start | bytes 100
  74.3 38.1 %copy-start.2 = (f32[256]{0:T(256)S(1)}, f32[256]{0:T(256)}, u32[]{:S(2)}) copy-start(f32[256]{0:T(256)} %param.6) | copy-start | bytes 3076
  74.3 38.7 %all-to-all-start.1 = ((bf16[24,8,1280]{2,1,0:T(8,128)(2,1)}), bf16[24,8,1280]{2,1,0:T(8,128)(2,1)S(1)}, u32[]{:S(2)}, u32[]{:S(2)}) async-start(bf16[24,8,1280]{2,1,0:T(8,128)(2,1)} %fusion.13), calls=%async_computation.1 | async-start | bytes 983040 | tf_op jit(solution)/shard_map/all_to_all | solution.py:195
  92.0 9.0 %collective-permute-start.5 = (f32[4,32]{1,0:T(4,128)S(1)}, f32[4,32]{1,0:T(4,128)S(1)}, u32[]{:S(2)}, u32[]{:S(2)}) collective-permute-start(f32[4,32]{1,0:T(4,128)S(1)} %get-tuple-element.27), channel_id=1, source_target_pairs={{0,384},{384,0},{1,385},{385,1},{2,386},{386,2},{3,387},{387,3},{4... | collective-permute-start | bytes 1544 | tf_op jit(solution)/shard_map/ppermute | solution.py:17
  101.0 8.1 %collective-permute-start.6 = (f32[2,32]{1,0:T(2,128)S(1)}, f32[2,32]{1,0:T(2,128)S(1)}, u32[]{:S(2)}, u32[]{:S(2)}) collective-permute-start(f32[2,32]{1,0:T(2,128)S(1)} %bitcast.70), channel_id=1, source_target_pairs={{0,288},{96,0},{192,96},{288,192},{1,289},{97,1},{193,97},{289,193... | collective-permute-start | bytes 776 | tf_op jit(solution)/shard_map/ppermute | solution.py:37
  104.6 5.8 %collective-permute-start.7 = (f32[2,32]{1,0:T(2,128)S(1)}, f32[2,32]{1,0:T(2,128)S(1)}, u32[]{:S(2)}, u32[]{:S(2)}) collective-permute-start(f32[2,32]{1,0:T(2,128)S(1)} %bitcast.69), channel_id=1, source_target_pairs={{0,192},{96,288},{192,0},{288,96},{1,193},{97,289},{193,1},{289,97... | collective-permute-start | bytes 776 | tf_op jit(solution)/shard_map/ppermute | solution.py:37
  106.5 5.8 %collective-permute-start.8 = (f32[2,32]{1,0:T(2,128)S(1)}, f32[2,32]{1,0:T(2,128)S(1)}, u32[]{:S(2)}, u32[]{:S(2)}) collective-permute-start(f32[2,32]{1,0:T(2,128)S(1)} %bitcast.68), channel_id=1, source_target_pairs={{0,96},{96,192},{192,288},{288,0},{1,97},{97,193},{193,289},{289,1... | collective-permute-start | bytes 776 | tf_op jit(solution)/shard_map/ppermute | solution.py:37

commit v11 on v10

--- a/solution.py
+++ b/solution.py
@@ -21,7 +21,7 @@
     return lax.dynamic_index_in_dim(value, index, axis, keepdims=False)
 
 
-def send_back(score):
+def send_back(score, source):
     capacity = score.shape[1]
     width = lax.axis_size("x")
     score = score.reshape(2, width, capacity)
@@ -29,13 +29,12 @@
     kept = pick(score, half, 0)
     came = swap(pick(score, 1 - half, 0), "yh")
     score = jnp.where(half == 0, jnp.stack([kept, came], 1), jnp.stack([came, kept], 1))
-    source = lax.broadcasted_iota(jnp.int32, (2, width, capacity), 1)
     returned = jnp.zeros((2, width, capacity), jnp.float32)
     for shift in range(width):
         part = pick(score, (place + shift) % width, 0)
         if shift > 0:
             part = lax.ppermute(part, "x", [(i, (i + shift) % width) for i in range(width)])
-        returned = jnp.where(source == (place + width - shift) % width, part[:, None], returned)
+        returned = jnp.where(source == shift, part[:, None], returned)
     return returned.reshape(2 * width, capacity)
 
 
@@ -153,6 +152,10 @@
         axis=1,
     ).reshape(2 * row_total, hidden_count)
     hidden_units = reorder(hidden_all.T, block_order(cube_count))
+    width = lax.axis_size("x")
+    source = lax.broadcasted_iota(jnp.int32, (2, width, capacity), 1)
+    source = (lax.axis_index("x") + width - source) % width
+    hidden_units, source = lax.optimization_barrier((hidden_units, source))
 
     def product(units, rows):
         return lax.dot_general(
@@ -195,7 +198,7 @@
     gathered = lax.all_to_all(
         spread.reshape(-1, unit, half), REST, split_axis=0, concat_axis=0, tiled=True
     ).reshape(-1, 2, unit, half)
-    returned_score = send_back(row_score.reshape(expert_count, capacity))
+    returned_score = send_back(row_score.reshape(expert_count, capacity), source)
     slot_index = lax.broadcasted_iota(jnp.int32, (expert_count, capacity), 1)
     live_rows = (slot_index < counts[:, None]).astype(jnp.float32)
     route_grad = live_rows * returned_score / route_weight.reshape(expert_count, capacity)

time: 115 us -> 114 us (level)
  local copies, waits for them, and re-layouts: 4.01 us -> 0.7 us
  waiting for transfers between devices: 41.5 us -> 44.2 us
    all_to_all x1, waiting for transfers between devices: 25.3 us -> 27.3 us  [body(): lax.all_to_all(outgoing.reshape(expert_count * 2, capacity, half), EXPERT...]
    all_to_all x1, waiting for transfers between devices: 0.01 us -> 1.36 us  [body(): lax.all_to_all(spread.reshape(-1, unit, half), REST, split_axis=0, concat...]
  transfers between devices with their start and end apart: 11 -> 11, of which waited for: 6 -> 7; matrix products, arithmetic and copies ran while one was open for 9% -> 7% of each run, Pallas kernels for 1% -> 1%
where the time goes in v11:
time: 114 us; the launch traced here: 113 us
  starting transfers between devices  55.1 us (48%)
  waiting for transfers between devices  44.2 us (39%)
  other arithmetic  4.57 us (4%)
  matrix products  4.29 us (4%)
  Pallas kernels  2.99 us (3%)
    all_to_all x1, waiting for transfers between devices, body(): lax.all_to_all(outgoing.reshape(expert_count * 2, capacity, half), EXPERT...  27.3 us
    all_to_all x1, starting transfers between devices, body(): lax.all_to_all(spread.reshape(-1, unit, half), REST, split_axis=0, concat...  16.3 us
    all_to_all x1, starting transfers between devices, body(): lax.all_to_all(outgoing.reshape(expert_count * 2, capacity, half), EXPERT...  14.1 us
    ppermute x3, starting transfers between devices, swap(): return lax.ppermute(value, axis, [(0, 1), (1, 0)])  7.62 us
    ppermute x3, starting transfers between devices, send_back(): lax.ppermute(part, 'x', [(i, (i + shift) % width) for i in range(width)])  7.56 us
    ppermute x3, waiting for transfers between devices, swap(): return lax.ppermute(value, axis, [(0, 1), (1, 0)])  7.46 us
    ppermute x1, waiting for transfers between devices, body(): came = lax.ppermute(passed, CUBE, stage_pairs(1))  6.03 us
    ppermute x1, starting transfers between devices, body(): came = lax.ppermute(passed, CUBE, stage_pairs(1))  3.77 us
  transfers between devices with their start and end apart: 11, of which 7 were waited for; matrix products, arithmetic and copies ran while one was open for 7% of the time, Pallas kernels for 1%

profile of v11, /device:TPU:1, one launch (start us, length us, event | category | flops | bytes accessed | tf_op | source)
XLA Modules:
  0.0 112.8 jit_solution(3888374907933806693)
XLA Ops:
  0.6 2.4 %shard_map.76 = bf16[8,2,32,1280]{3,2,1,0:T(8,128)(2,1)} custom-call(s32[8]{0:T(128)} %counts_ref.1, f32[1,256]{1,0:T(1,128)} %bitcast.65, bf16[256,2560]{1,0:T(8,128)(2,1)} %grad_ref.1), custom_call_target="tpu_custom_call" | custom-call | flops 655360 | bytes 2621440 | tf_op jit(solution)/shard_map/pallas_call | solution.py:106
  3.0 14.1 %all-to-all-start = ((bf16[16,32,1280]{2,1,0:T(8,128)(2,1)}), bf16[16,32,1280]{2,1,0:T(8,128)(2,1)S(1)}, u32[]{:S(2)}, u32[]{:S(2)}) async-start(bf16[16,32,1280]{2,1,0:T(8,128)(2,1)} %bitcast.60), calls=%async_computation | async-start | bytes 2621440 | tf_op jit(solution)/shard_map/all_to_all | solution.py:134
  17.2 0.3 fusion.3
  17.4 2.1 %collective-permute-start = (bf16[8,32,768]{2,1,0:T(8,128)(2,1)S(1)}, bf16[8,32,768]{2,1,0:T(8,128)(2,1)S(1)}, u32[]{:S(2)}, u32[]{:S(2)}) collective-permute-start(bf16[8,32,768]{2,1,0:T(8,128)(2,1)S(1)} %bitcast.63), channel_id=1, source_target_pairs={{0,1},{1,0},{2,3},{3,2},{4,5},{5,4},{6,7},{7,6},{8,9},{9,8},{10,11... | collective-permute-start | bytes 1179656 | tf_op jit(solution)/shard_map/ppermute | solution.py:17
  19.7 1.3 %collective-permute-done = bf16[8,32,768]{2,1,0:T(8,128)(2,1)S(1)} collective-permute-done((bf16[8,32,768]{2,1,0:T(8,128)(2,1)S(1)}, bf16[8,32,768]{2,1,0:T(8,128)(2,1)S(1)}, u32[]{:S(2)}, u32[]{:S(2)}) %collective-permute-start) | collective-permute-done | bytes 393248 | tf_op jit(solution)/shard_map/ppermute | solution.py:17
  21.2 0.3 copy.13
  21.5 0.6 shard_map.77
  22.1 27.3 %all-to-all-done = bf16[16,32,1280]{2,1,0:T(8,128)(2,1)S(1)} async-done(((bf16[16,32,1280]{2,1,0:T(8,128)(2,1)}), bf16[16,32,1280]{2,1,0:T(8,128)(2,1)S(1)}, u32[]{:S(2)}, u32[]{:S(2)}) %all-to-all-start) | async-done | bytes 1310752 | tf_op jit(solution)/shard_map/all_to_all | solution.py:134
  49.4 0.4 convolution_convert_fusion.1
  49.9 3.7 %collective-permute-start.2 = (bf16[192,1280]{1,0:T(8,128)(2,1)S(1)}, bf16[192,1280]{1,0:T(8,128)(2,1)S(1)}, u32[]{:S(2)}, u32[]{:S(2)}) collective-permute-start(bf16[192,1280]{1,0:T(8,128)(2,1)S(1)} %convolution_convert_fusion.1), channel_id=1, source_target_pairs={{0,2},{1,25},{2,0},{3,27},{4,6},{5,29},{6,4},{7,31},{24,26},{25,1}... | collective-permute-start | bytes 1474568 | tf_op jit(solution)/shard_map/ppermute | solution.py:168
  53.6 2.8 %fusion = f32[8,2,32,768]{3,2,1,0:T(8,128)S(1)} fusion(bf16[8,2,32,1280]{3,2,1,0:T(8,128)(2,1)S(1)} %bitcast.57, bf16[1,768,2560]{2,1,0:T(8,128)(2,1)} %param.9, s32[]{:T(128)S(6)} %select_n.179), kind=kOutput, calls=%fused_computation.2 | convolution fusion | flops 1006632960 | bytes 4849668 | tf_op jit(solution)/shard_map/dot_general | solution.py:173
  56.4 0.4 convolution_convert_fusion
  56.8 1.9 %collective-permute-start.3 = (bf16[192,1280]{1,0:T(8,128)(2,1)S(1)}, bf16[192,1280]{1,0:T(8,128)(2,1)S(1)}, u32[]{:S(2)}, u32[]{:S(2)}) collective-permute-start(bf16[192,1280]{1,0:T(8,128)(2,1)S(1)} %convolution_convert_fusion), channel_id=1, source_target_pairs={{0,2},{1,25},{2,0},{3,27},{4,6},{5,29},{6,4},{7,31},{24,26},{25,1}... | collective-permute-start | bytes 1474568 | tf_op jit(solution)/shard_map/ppermute | solution.py:179
  58.8 3.2 %collective-permute-start.1 = (f32[8,32,768]{2,1,0:T(8,128)S(1)}, f32[8,32,768]{2,1,0:T(8,128)S(1)}, u32[]{:S(2)}, u32[]{:S(2)}) collective-permute-start(f32[8,32,768]{2,1,0:T(8,128)S(1)} %dynamic-slice_bitcast_fusion), channel_id=1, source_target_pairs={{0,1},{1,0},{2,3},{3,2},{4,5},{5,4},{6,7},{7,6},{8,9},{9,8},{10,11... | collective-permute-start | bytes 2359304 | tf_op jit(solution)/shard_map/ppermute | solution.py:17
  62.0 0.7 fusion.14
  62.8 3.8 %collective-permute-start.4 = (bf16[192,1280]{1,0:T(8,128)(2,1)S(1)}, bf16[192,1280]{1,0:T(8,128)(2,1)S(1)}, u32[]{:S(2)}, u32[]{:S(2)}) collective-permute-start(bf16[192,1280]{1,0:T(8,128)(2,1)S(1)} %add_convert_fusion.1), channel_id=1, source_target_pairs={{0,24},{1,3},{2,26},{3,1},{4,28},{5,7},{6,30},{7,5},{24,0},{25,27}... | collective-permute-start | bytes 1474568 | tf_op jit(solution)/shard_map/ppermute | solution.py:184
  66.6 0.1 bitcast_add_fusion
  66.7 0.6 fusion.6
  67.3 6.0 %collective-permute-done.4 = bf16[192,1280]{1,0:T(8,128)(2,1)S(1)} collective-permute-done((bf16[192,1280]{1,0:T(8,128)(2,1)S(1)}, bf16[192,1280]{1,0:T(8,128)(2,1)S(1)}, u32[]{:S(2)}, u32[]{:S(2)}) %collective-permute-start.4) | collective-permute-done | bytes 491552 | tf_op jit(solution)/shard_map/ppermute | solution.py:184
  73.4 0.9 fusion.13
  74.3 16.3 %all-to-all-start.1 = ((bf16[24,8,1280]{2,1,0:T(8,128)(2,1)}), bf16[24,8,1280]{2,1,0:T(8,128)(2,1)S(1)}, u32[]{:S(2)}, u32[]{:S(2)}) async-start(bf16[24,8,1280]{2,1,0:T(8,128)(2,1)} %fusion.13), calls=%async_computation.1 | async-start | bytes 983040 | tf_op jit(solution)/shard_map/all_to_all | solution.py:198
  90.9 2.3 %collective-permute-start.5 = (f32[4,32]{1,0:T(4,128)S(1)}, f32[4,32]{1,0:T(4,128)S(1)}, u32[]{:S(2)}, u32[]{:S(2)}) collective-permute-start(f32[4,32]{1,0:T(4,128)S(1)} %get-tuple-element.31), channel_id=1, source_target_pairs={{0,384},{384,0},{1,385},{385,1},{2,386},{386,2},{3,387},{387,3},{4... | collective-permute-start | bytes 1544 | tf_op jit(solution)/shard_map/ppermute | solution.py:17
  93.3 6.1 %collective-permute-done.5 = f32[4,32]{1,0:T(4,128)S(1)} collective-permute-done((f32[4,32]{1,0:T(4,128)S(1)}, f32[4,32]{1,0:T(4,128)S(1)}, u32[]{:S(2)}, u32[]{:S(2)}) %collective-permute-start.5) | collective-permute-done | bytes 544 | tf_op jit(solution)/shard_map/ppermute | solution.py:17
  99.4 3.2 %collective-permute-start.6 = (f32[2,32]{1,0:T(2,128)S(1)}, f32[2,32]{1,0:T(2,128)S(1)}, u32[]{:S(2)}, u32[]{:S(2)}) collective-permute-start(f32[2,32]{1,0:T(2,128)S(1)} %bitcast.70), channel_id=1, source_target_pairs={{0,288},{96,0},{192,96},{288,192},{1,289},{97,1},{193,97},{289,193... | collective-permute-start | bytes 776 | tf_op jit(solution)/shard_map/ppermute | solution.py:36
  102.6 1.9 %collective-permute-start.7 = (f32[2,32]{1,0:T(2,128)S(1)}, f32[2,32]{1,0:T(2,128)S(1)}, u32[]{:S(2)}, u32[]{:S(2)}) collective-permute-start(f32[2,32]{1,0:T(2,128)S(1)} %bitcast.69), channel_id=1, source_target_pairs={{0,192},{96,288},{192,0},{288,96},{1,193},{97,289},{193,1},{289,97... | collective-permute-start | bytes 776 | tf_op jit(solution)/shard_map/ppermute | solution.py:36
  104.5 2.5 %collective-permute-start.8 = (f32[2,32]{1,0:T(2,128)S(1)}, f32[2,32]{1,0:T(2,128)S(1)}, u32[]{:S(2)}, u32[]{:S(2)}) collective-permute-start(f32[2,32]{1,0:T(2,128)S(1)} %bitcast.68), channel_id=1, source_target_pairs={{0,96},{96,192},{192,288},{288,0},{1,97},{97,193},{193,289},{289,1... | collective-permute-start | bytes 776 | tf_op jit(solution)/shard_map/ppermute | solution.py:36
  107.0 0.9 pad_maximum_fusion.1
  108.0 0.8 collective-permute-done.7
  108.7 1.3 %collective-permute-done.8 = f32[2,32]{1,0:T(2,128)S(1)} collective-permute-done((f32[2,32]{1,0:T(2,128)S(1)}, f32[2,32]{1,0:T(2,128)S(1)}, u32[]{:S(2)}, u32[]{:S(2)}) %collective-permute-start.8) | collective-permute-done | bytes 288 | tf_op jit(solution)/shard_map/ppermute | solution.py:36
  110.1 0.6 select_divide_fusion
  110.7 1.4 %all-to-all-done.1 = bf16[24,8,1280]{2,1,0:T(8,128)(2,1)S(1)} async-done(((bf16[24,8,1280]{2,1,0:T(8,128)(2,1)}), bf16[24,8,1280]{2,1,0:T(8,128)(2,1)S(1)}, u32[]{:S(2)}, u32[]{:S(2)}) %all-to-all-start.1) | async-done | bytes 491552 | tf_op jit(solution)/shard_map/all_to_all | solution.py:198
  112.2 0.6 maximum_bitcast_fusion
  (32 shorter events, 0.9 us)
Async XLA Ops:
  3.0 14.1 %copy-start = (bf16[256,1536]{1,0:T(8,128)(2,1)S(1)}, bf16[256,1536]{1,0:T(8,128)(2,1)}, u32[]{:S(2)}) copy-start(bf16[256,1536]{1,0:T(8,128)(2,1)} %param.8) | copy-start | bytes 2359300
  3.0 46.4 %all-to-all-start = ((bf16[16,32,1280]{2,1,0:T(8,128)(2,1)}), bf16[16,32,1280]{2,1,0:T(8,128)(2,1)S(1)}, u32[]{:S(2)}, u32[]{:S(2)}) async-start(bf16[16,32,1280]{2,1,0:T(8,128)(2,1)} %bitcast.60), calls=%async_computation | async-start | bytes 2621440 | tf_op jit(solution)/shard_map/all_to_all | solution.py:134
  17.4 3.6 %collective-permute-start = (bf16[8,32,768]{2,1,0:T(8,128)(2,1)S(1)}, bf16[8,32,768]{2,1,0:T(8,128)(2,1)S(1)}, u32[]{:S(2)}, u32[]{:S(2)}) collective-permute-start(bf16[8,32,768]{2,1,0:T(8,128)(2,1)S(1)} %bitcast.63), channel_id=1, source_target_pairs={{0,1},{1,0},{2,3},{3,2},{4,5},{5,4},{6,7},{7,6},{8,9},{9,8},{10,11... | collective-permute-start | bytes 1179656 | tf_op jit(solution)/shard_map/ppermute | solution.py:17
  49.9 12.8 %collective-permute-start.2 = (bf16[192,1280]{1,0:T(8,128)(2,1)S(1)}, bf16[192,1280]{1,0:T(8,128)(2,1)S(1)}, u32[]{:S(2)}, u32[]{:S(2)}) collective-permute-start(bf16[192,1280]{1,0:T(8,128)(2,1)S(1)} %convolution_convert_fusion.1), channel_id=1, source_target_pairs={{0,2},{1,25},{2,0},{3,27},{4,6},{5,29},{6,4},{7,31},{24,26},{25,1}... | collective-permute-start | bytes 1474568 | tf_op jit(solution)/shard_map/ppermute | solution.py:168
  56.8 10.5 %collective-permute-start.3 = (bf16[192,1280]{1,0:T(8,128)(2,1)S(1)}, bf16[192,1280]{1,0:T(8,128)(2,1)S(1)}, u32[]{:S(2)}, u32[]{:S(2)}) collective-permute-start(bf16[192,1280]{1,0:T(8,128)(2,1)S(1)} %convolution_convert_fusion), channel_id=1, source_target_pairs={{0,2},{1,25},{2,0},{3,27},{4,6},{5,29},{6,4},{7,31},{24,26},{25,1}... | collective-permute-start | bytes 1474568 | tf_op jit(solution)/shard_map/ppermute | solution.py:179
  58.8 7.8 %collective-permute-start.1 = (f32[8,32,768]{2,1,0:T(8,128)S(1)}, f32[8,32,768]{2,1,0:T(8,128)S(1)}, u32[]{:S(2)}, u32[]{:S(2)}) collective-permute-start(f32[8,32,768]{2,1,0:T(8,128)S(1)} %dynamic-slice_bitcast_fusion), channel_id=1, source_target_pairs={{0,1},{1,0},{2,3},{3,2},{4,5},{5,4},{6,7},{7,6},{8,9},{9,8},{10,11... | collective-permute-start | bytes 2359304 | tf_op jit(solution)/shard_map/ppermute | solution.py:17
  62.7 3.9 %copy-start.1 = (bf16[256,1536]{1,0:T(8,128)(2,1)S(1)}, bf16[256,1536]{1,0:T(8,128)(2,1)}, u32[]{:S(2)}) copy-start(bf16[256,1536]{1,0:T(8,128)(2,1)} %param.8) | copy-start | bytes 2359300
  62.8 10.6 %collective-permute-start.4 = (bf16[192,1280]{1,0:T(8,128)(2,1)S(1)}, bf16[192,1280]{1,0:T(8,128)(2,1)S(1)}, u32[]{:S(2)}, u32[]{:S(2)}) collective-permute-start(bf16[192,1280]{1,0:T(8,128)(2,1)S(1)} %add_convert_fusion.1), channel_id=1, source_target_pairs={{0,24},{1,3},{2,26},{3,1},{4,28},{5,7},{6,30},{7,5},{24,0},{25,27}... | collective-permute-start | bytes 1474568 | tf_op jit(solution)/shard_map/ppermute | solution.py:184
  67.3 23.4 %copy-start.3 = (s32[8]{0:T(128)S(1)}, s32[8]{0:T(128)}, u32[]{:S(2)}) copy-start(s32[8]{0:T(128)} %counts_ref.1) | copy-start | bytes 100
  74.3 35.9 %copy-start.2 = (f32[256]{0:T(256)S(1)}, f32[256]{0:T(256)}, u32[]{:S(2)}) copy-start(f32[256]{0:T(256)} %param.6) | copy-start | bytes 3076
  74.3 37.8 %all-to-all-start.1 = ((bf16[24,8,1280]{2,1,0:T(8,128)(2,1)}), bf16[24,8,1280]{2,1,0:T(8,128)(2,1)S(1)}, u32[]{:S(2)}, u32[]{:S(2)}) async-start(bf16[24,8,1280]{2,1,0:T(8,128)(2,1)} %fusion.13), calls=%async_computation.1 | async-start | bytes 983040 | tf_op jit(solution)/shard_map/all_to_all | solution.py:198
  90.9 8.6 %collective-permute-start.5 = (f32[4,32]{1,0:T(4,128)S(1)}, f32[4,32]{1,0:T(4,128)S(1)}, u32[]{:S(2)}, u32[]{:S(2)}) collective-permute-start(f32[4,32]{1,0:T(4,128)S(1)} %get-tuple-element.31), channel_id=1, source_target_pairs={{0,384},{384,0},{1,385},{385,1},{2,386},{386,2},{3,387},{387,3},{4... | collective-permute-start | bytes 1544 | tf_op jit(solution)/shard_map/ppermute | solution.py:17
  99.4 8.5 %collective-permute-start.6 = (f32[2,32]{1,0:T(2,128)S(1)}, f32[2,32]{1,0:T(2,128)S(1)}, u32[]{:S(2)}, u32[]{:S(2)}) collective-permute-start(f32[2,32]{1,0:T(2,128)S(1)} %bitcast.70), channel_id=1, source_target_pairs={{0,288},{96,0},{192,96},{288,192},{1,289},{97,1},{193,97},{289,193... | collective-permute-start | bytes 776 | tf_op jit(solution)/shard_map/ppermute | solution.py:36
  102.6 6.1 %collective-permute-start.7 = (f32[2,32]{1,0:T(2,128)S(1)}, f32[2,32]{1,0:T(2,128)S(1)}, u32[]{:S(2)}, u32[]{:S(2)}) collective-permute-start(f32[2,32]{1,0:T(2,128)S(1)} %bitcast.69), channel_id=1, source_target_pairs={{0,192},{96,288},{192,0},{288,96},{1,193},{97,289},{193,1},{289,97... | collective-permute-start | bytes 776 | tf_op jit(solution)/shard_map/ppermute | solution.py:36
  104.5 5.5 %collective-permute-start.8 = (f32[2,32]{1,0:T(2,128)S(1)}, f32[2,32]{1,0:T(2,128)S(1)}, u32[]{:S(2)}, u32[]{:S(2)}) collective-permute-start(f32[2,32]{1,0:T(2,128)S(1)} %bitcast.68), channel_id=1, source_target_pairs={{0,96},{96,192},{192,288},{288,0},{1,97},{97,193},{193,289},{289,1... | collective-permute-start | bytes 776 | tf_op jit(solution)/shard_map/ppermute | solution.py:36
